TPU v7x, 32 devices: a whole 2x2x4 slice. The times are simulated.
32 devices in a mesh: rows: 8 (over y, x, core), cols: 4 (over z).
Axes of the slice: x: 2, y: 2, z: 4, core: 2. Of those that a mesh axis runs over, the one named last changes fastest.
Arguments:
- owner_map: int32 [2, 128], replicated, may hold values from 0 to 127, as said below
- colidx: int32 [2, 128, 24], P(None, 'rows', 'cols'), may hold values from 0 to 191, as said below
- live: int32 [2, 128], P(None, 'rows'), may hold values from 1 to 24
- blocks: bfloat16 [2, 128, 24, 128, 128], P(None, 'rows', 'cols'), may hold values from -0.15625 to 0.15625
- diag_inverse: float32 [2, 128, 128, 128], P(None, 'rows')
- right_side: float32 [2, 128, 64, 128], P(None, 'rows'), may hold values from -6 to 6
- prior: bfloat16 [64, 64, 128], P('rows'), may hold values from -6 to 6
Outputs:
- solved: float32 [2, 128, 64, 128], P(None, 'rows')
Inputs may be any that keep to these rules, and one draw needn't show every extreme that they name: Each row of owner_map is a permutation of the block rows of a front. `colidx`: front 0 refers only to earlier block rows; in front 1, even slots refer to rows of front 0 and odd slots to earlier block rows. Take the even slots of front 1 that lie in block rows s with s // 16 equal to one value and in slots j with j // 6 equal to one value. Among them, at most 6 refer to front-0 rows r whose slot t (owner_map[0, t] = r) has t // 16 equal to any single value; some such group reaches 6.
All inputs are finite; a program needn't handle non-finite values.
Results may differ from a plain program's by a relative error of at most 0.0017.
Values may be sent and summed in bfloat16 or wider, within the bound.
No kernel may reach another device: no remote copies, remote signals or barrier semaphores. Data moves between devices by JAX's collectives and lax.ppermute only.
A program may use at most 64 MiB of HBM per device.

v0:
```python
import jax
import jax.numpy as jnp
from jax import lax
from jax.sharding import PartitionSpec as P


def solve_diag(resid, inverse):
    return jnp.einsum(
        "rpb,rcb->rpc",
        resid,
        inverse,
        precision=lax.Precision.HIGHEST,
        preferred_element_type=jnp.float32,
    )


def block_products(blk, values):
    return jnp.einsum("rjcb,rjpb->rpc", blk, values, preferred_element_type=jnp.float32)


def finish(partial_value, rhs_front, inverse):
    total = lax.psum(partial_value, "cols")
    return solve_diag(rhs_front - total, inverse)


def shards(owner_map, colidx, live, blocks, diag_inverse, right_side, prior):
    slot_count = blocks.shape[2]
    col_here = lax.axis_index("cols")
    rows_front = owner_map.shape[1]
    slot_ids = col_here * slot_count + jnp.arange(slot_count, dtype=jnp.int32)
    live_mask = slot_ids[None, None, :] < live[:, :, None]
    prior_all = lax.all_gather(prior, "rows", axis=0, tiled=True)
    prior_count = prior_all.shape[0]
    zero_value = jnp.zeros((), jnp.bfloat16)
    first_idx = jnp.clip(colidx[0], 0, prior_count - 1)
    first_values = jnp.where(live_mask[0][:, :, None, None], prior_all[first_idx], zero_value)
    first = finish(block_products(blocks[0], first_values), right_side[0], diag_inverse[0])
    first_low = first.astype(jnp.bfloat16)
    second_idx = colidx[1]
    from_prior = second_idx < prior_count
    inverse_map = (
        jnp.zeros((rows_front,), jnp.int32)
        .at[owner_map[0]]
        .set(jnp.arange(rows_front, dtype=jnp.int32))
    )
    slot_pos = inverse_map[jnp.clip(second_idx - prior_count, 0, rows_front - 1)]
    whole_front = lax.all_gather(first_low, "rows", axis=0, tiled=True)
    recent_values = whole_front[slot_pos]
    early_values = prior_all[jnp.clip(second_idx, 0, prior_count - 1)]
    chosen = jnp.where(from_prior[:, :, None, None], early_values, recent_values)
    second_values = jnp.where(live_mask[1][:, :, None, None], chosen, zero_value)
    second = finish(block_products(blocks[1], second_values), right_side[1], diag_inverse[1])
    return jnp.stack([first, second])


def solution(mesh):
    placed = (
        P(),
        P(None, "rows", "cols"),
        P(None, "rows"),
        P(None, "rows", "cols", None, None),
        P(None, "rows", None, None),
        P(None, "rows", None, None),
        P("rows", None, None),
    )
    return jax.shard_map(
        shards, mesh=mesh, in_specs=placed, out_specs=P(None, "rows", None, None), check_vma=False
    )
```

profile of v0, /device:TPU:0, one launch (start us, length us, event | category | flops | bytes accessed | tf_op | source)
XLA Modules:
  0.0 171.6 jit_solution(139626868818625352)
XLA Ops:
  6.5 0.7 all-gather.3.cloned.1.call-update
  7.3 0.8 fusion.38
  8.2 0.1 reshape.128
  8.3 0.8 broadcast_compare_fusion
  9.1 0.1 copy.32
  9.2 26.3 %all-gather.3.cloned.1.call-done = bf16[64,64,128]{2,1,0:T(8,128)(2,1)} async-done(((bf16[8,64,128]{2,1,0:T(8,128)(2,1)}), bf16[64,64,128]{2,1,0:T(8,128)(2,1)}) %all-gather.3.cloned.1.call-update) | async-done | bytes 1048592 | tf_op jit(solution)/shard_map/all_gather | solution.py:32
  35.5 3.2 %gather_fusion = bf16[96,64,128]{2,1,0:T(8,128)(2,1)} fusion(bf16[64,64,128]{2,1,0:T(8,128)(2,1)} %all-gather.3.cloned.1.call-done, s32[1024]{0:T(1024)S(1)} %pad_clamp_fusion.3), kind=kCustom, calls=%fused_computation | custom fusion | bytes 3146112 | tf_op jit(solution)/shard_map/gather | solution.py:36
  38.7 4.6 %fusion.17 = f32[16,64,128]{2,1,0:T(8,128)} fusion(bf16[2,16,6,128,128]{4,3,2,1,0:T(8,128)(2,1)} %param.10, bf16[16,6,64,128]{3,2,1,0:T(8,128)(2,1)} %bitcast.62, pred[16,6]{1,0:T(8,128)(4,1)S(1)} %copy.32), kind=kOutput, calls=%fused_computation.18 | convolution fusion | flops 202113024 | bytes 5242976 | tf_op jit(solution)/shard_map/rjcb,rjpb->rpc/dot_general | solution.py:18
  43.3 38.4 %all-reduce.3.cloned.1.call-done = f32[16,64,128]{2,1,0:T(8,128)} async-done(((f32[16,64,128]{2,1,0:T(8,128)}), f32[16,64,128]{2,1,0:T(8,128)}) %all-reduce.3.cloned.1.call-update) | async-done | bytes 524304 | tf_op jit(solution)/shard_map/psum | solution.py:22
  81.7 4.1 %fusion.39 = (bf16[16,64,128]{2,1,0:T(8,128)(2,1)}, f32[16,64,128]{2,1,0:T(8,128)}) fusion(f32[2,16,128,128]{3,2,1,0:T(8,128)S(1)} %copy-done.1, f32[16,64,128]{2,1,0:T(8,128)} %all-reduce.3.cloned.1.call-done, f32[2,16,64,128]{3,2,1,0:T(8,128)S(1)} %copy-done.3), kind=kOutput, calls=%fused_computation.57 | convolution fusion | flops 201588736 | bytes 2883584 | tf_op jit(solution)/shard_map/rpb,rcb->rpc/dot_general | solution.py:8
  85.9 0.1 reshape.144
  86.0 1.0 scatter_custom_fusion
  87.1 1.2 gather_fusion.2
  88.4 0.1 copy.40
  88.6 0.1 reshape.152
  88.9 0.1 copy.37
  89.0 0.1 copy.35
  89.1 2.0 %gather_fusion.1 = bf16[96,64,128]{2,1,0:T(8,128)(2,1)} fusion(bf16[64,64,128]{2,1,0:T(8,128)(2,1)S(1)} %copy-done, s32[1024]{0:T(1024)S(1)} %pad_clamp_fusion.2), kind=kCustom, calls=%fused_computation.1 | custom fusion | bytes 3146112 | tf_op jit(solution)/shard_map/gather | solution.py:49
  91.1 22.8 %all-gather.5.cloned.1.call-done = bf16[128,64,128]{2,1,0:T(8,128)(2,1)} async-done(((bf16[16,64,128]{2,1,0:T(8,128)(2,1)}), bf16[128,64,128]{2,1,0:T(8,128)(2,1)}) %all-gather.5.cloned.1.call-update) | async-done | bytes 2097168 | tf_op jit(solution)/shard_map/all_gather | solution.py:47
  113.8 3.5 %gather_fusion.3 = bf16[96,64,128]{2,1,0:T(8,128)(2,1)} fusion(bf16[128,64,128]{2,1,0:T(8,128)(2,1)} %all-gather.5.cloned.1.call-done, s32[1024]{0:T(1024)S(1)} %pad_clamp_fusion), kind=kCustom, calls=%fused_computation.3 | custom fusion | bytes 3146112 | tf_op jit(solution)/shard_map/gather | solution.py:48
  117.4 4.9 %fusion.12 = f32[16,64,128]{2,1,0:T(8,128)} fusion(bf16[2,16,6,128,128]{4,3,2,1,0:T(8,128)(2,1)} %param.10, bf16[16,6,64,128]{3,2,1,0:T(8,128)(2,1)} %bitcast.60, bf16[16,6,64,128]{3,2,1,0:T(8,128)(2,1)} %bitcast.61, pred[16,6]{1,0:T(8,128)(4,1)S(1)} %copy.37, pred[16,6]{1,0:T(8,128)(4,1)S(1)} %copy.35), kind=kOutput, calls=%fused_computation.17 | convolution fusion | flops 202899456 | bytes 6815936 | tf_op jit(solution)/shard_map/rjcb,rjpb->rpc/dot_general | solution.py:18
  122.3 38.5 %all-reduce.5.cloned.1.call-done = f32[16,64,128]{2,1,0:T(8,128)} async-done(((f32[16,64,128]{2,1,0:T(8,128)}), f32[16,64,128]{2,1,0:T(8,128)}) %all-reduce.5.cloned.1.call-update) | async-done | bytes 524304 | tf_op jit(solution)/shard_map/psum | solution.py:22
  160.7 3.3 %convolution_bitcast_fusion = f32[1,16,64,128]{3,2,1,0:T(8,128)S(1)} fusion(f32[2,16,128,128]{3,2,1,0:T(8,128)S(1)} %copy-done.1, f32[16,64,128]{2,1,0:T(8,128)} %all-reduce.5.cloned.1.call-done, f32[2,16,64,128]{3,2,1,0:T(8,128)} %param.12), kind=kOutput, calls=%fused_computation.19 | convolution fusion | flops 201457664 | bytes 2621440 | tf_op jit(solution)/shard_map/rpb,rcb->rpc/dot_general | solution.py:8
  164.0 1.0 pad_maximum_fusion
  (37 shorter events, 0.8 us)
Async XLA Ops:
  6.5 28.9 %all-gather.3.cloned.1.call-start = ((), (), s32[]{:S(2)}) async-start(), calls=%async_computation | async-start | bytes 1179648 | tf_op jit(solution)/shard_map/all_gather | solution.py:32
  7.3 74.4 %all-reduce.3.cloned.1.call-start = ((), (), s32[]{:S(2)}) async-start(), calls=%async_computation.1 | async-start | bytes 1048576 | tf_op jit(solution)/shard_map/psum | solution.py:22
  38.7 43.0 %copy-start.1 = (f32[2,16,128,128]{3,2,1,0:T(8,128)S(1)}, f32[2,16,128,128]{3,2,1,0:T(8,128)}, u32[]{:S(2)}) copy-start(f32[2,16,128,128]{3,2,1,0:T(8,128)} %param.11) | copy-start | bytes 6291460
  38.7 43.0 %copy-start.3 = (f32[2,16,64,128]{3,2,1,0:T(8,128)S(1)}, f32[2,16,64,128]{3,2,1,0:T(8,128)}, u32[]{:S(2)}) copy-start(f32[2,16,64,128]{3,2,1,0:T(8,128)} %param.12) | copy-start | bytes 3145732
  43.2 42.8 %copy-start.4 = (s32[2,128]{1,0:T(2,128)S(1)}, s32[2,128]{1,0:T(2,128)}, u32[]{:S(2)}) copy-start(s32[2,128]{1,0:T(2,128)} %param.7) | copy-start | bytes 3076
  43.2 70.6 %all-gather.5.cloned.1.call-start = ((), (), s32[]{:S(2)}) async-start(), calls=%async_computation.2 | async-start | bytes 2359296 | tf_op jit(solution)/shard_map/all_gather | solution.py:47
  85.8 74.9 %all-reduce.5.cloned.1.call-start = ((), (), s32[]{:S(2)}) async-start(), calls=%async_computation.3 | async-start | bytes 1048576 | tf_op jit(solution)/shard_map/psum | solution.py:22
  87.0 2.0 %copy-start = (bf16[64,64,128]{2,1,0:T(8,128)(2,1)S(1)}, bf16[64,64,128]{2,1,0:T(8,128)(2,1)}, u32[]{:S(2)}) copy-start(bf16[64,64,128]{2,1,0:T(8,128)(2,1)} %all-gather.3.cloned.1.call-done) | copy-start | bytes 3145732
  122.2 41.8 %copy-start.2 = (f32[16,64,128]{2,1,0:T(8,128)S(1)}, f32[16,64,128]{2,1,0:T(8,128)}, u32[]{:S(2)}) copy-start(f32[16,64,128]{2,1,0:T(8,128)} %get-tuple-element.12) | copy-start | bytes 1572868
Sparse Core Ops, SparseCore 0:
  9.2 26.1 all-gather.2
  43.4 38.2 all-reduce.2
  85.9 27.8 all-gather.4
  122.4 38.2 all-reduce.4
where the time goes:
time: 172 us
  waiting for transfers between devices  127 us (74%)
  matrix products  16.8 us (10%)
  between operations  13.3 us (8%)
  local copies, waits for them, and re-layouts  12.9 us (8%)
  other arithmetic  1.87 us (1%)
    psum x2, waiting for transfers between devices, finish(): total = lax.psum(partial_value, 'cols')  76.8 us
    all_gather x1, waiting for transfers between devices, shards(): prior_all = lax.all_gather(prior, 'rows', axis=0, tiled=True)  26.3 us
    all_gather x1, waiting for transfers between devices, shards(): whole_front = lax.all_gather(first_low, 'rows', axis=0, tiled=True)  22.8 us
    dot_general x2, matrix products, block_products(): jnp.einsum('rjcb,rjpb->rpc', blk, values, preferred_element_type=jnp.floa...  9.45 us
    dot_general x2, matrix products, solve_diag(): jnp.einsum('rpb,rcb->rpc', resid, inverse, precision=lax.Precision.HIGHES...  7.36 us
    gather x1, local copies, waits for them, and re-layouts, shards(): recent_values = whole_front[slot_pos]  3.54 us
  transfers between devices with their start and end apart: 4, of which 4 were waited for; matrix products, arithmetic and copies ran while one was open for 4% of the time, Pallas kernels for 0%

commit v1 on v0

v1 whole, which is shorter than its diff:
```python
import functools

import jax
import jax.numpy as jnp
from jax import lax
from jax.experimental import pallas as pl
from jax.experimental.pallas import tpu as pltpu
from jax.sharding import PartitionSpec as P

F32, BF16, I32, I16 = jnp.float32, jnp.bfloat16, jnp.int32, jnp.int16
VMEM = pl.BlockSpec(memory_space=pltpu.VMEM)
SMEM = pl.BlockSpec(memory_space=pltpu.SMEM)
ANY = pl.BlockSpec(memory_space=pl.ANY)
STEPS = 128.0
TAIL = 16


def encode_blocks(values, msg_ref, probes):
    rows = lax.broadcasted_iota(I32, (TAIL, msg_ref.shape[1]), 0)
    tail = jnp.zeros((TAIL, msg_ref.shape[1]), F32)
    for k, value in enumerate(values):
        peak = jnp.maximum(jnp.max(jnp.abs(value), keepdims=True), 2.0**-100)
        level = jnp.ceil(jnp.log2(peak) * STEPS)
        scaled = jnp.round(value * jnp.exp2(15.0 - level * (1.0 / STEPS)))
        scaled = jnp.clip(scaled, -32767.0, 32767.0)
        msg_ref[k * probes : (k + 1) * probes] = scaled.astype(I32).astype(I16)
        tail = jnp.where(rows == k, level, tail)
    msg_ref[len(values) * probes :] = tail.astype(I32).astype(I16)


def decode_blocks(msg_ref, count, probes):
    tail = msg_ref[count * probes :].astype(I32).astype(F32)
    factor = jnp.exp2(tail * (1.0 / STEPS) - 15.0)
    return [
        msg_ref[k * probes : (k + 1) * probes].astype(I32).astype(F32) * factor[k : k + 1]
        for k in range(count)
    ]


def partial_kernel(front, cols, n_in, idx_ref, blocks_ref, *refs):
    ins, own_ref, msgs = refs[:n_in], refs[n_in], refs[n_in + 1 : n_in + cols]
    blk, known, sems = refs[n_in + cols :]
    _, rows_dev, slots, order, _ = blocks_ref.shape
    part = rows_dev // cols
    probes = own_ref.shape[1]
    here = idx_ref[rows_dev * slots]
    copies = []
    for s in range(cols):
        first = lax.rem(here + s, cols) * part
        copy = pltpu.make_async_copy(
            blocks_ref.at[front, pl.ds(first, part)], blk.at[pl.ds(s * part, part)], sems.at[s]
        )
        copy.start()
        copies.append(copy)
    at = 0
    for ref in ins:
        known[at : at + ref.shape[0]] = ref[...]
        at += ref.shape[0]
    known[at] = jnp.zeros(known.shape[1:], known.dtype)
    for s in list(range(1, cols)) + [0]:
        copies[s].wait()
        first = lax.rem(here + s, cols) * part
        sums = []
        for k in range(part):
            xs = [known[idx_ref[(first + k) * slots + j]] for j in range(slots)]
            ws = [blk[s * part + k, j] for j in range(slots)]
            sums.append(
                lax.dot_general(
                    jnp.concatenate(xs, axis=1),
                    jnp.concatenate(ws, axis=1),
                    (((1,), (1,)), ((), ())),
                    preferred_element_type=F32,
                )
            )
        if s == 0:
            for k in range(part):
                own_ref[k] = sums[k]
        else:
            encode_blocks(sums, msgs[s - 1], probes)


def partial_products(front, cols, idx, blocks, ins):
    _, rows_dev, slots, order, _ = blocks.shape
    part = rows_dev // cols
    probes = ins[0].shape[1]
    known_rows = sum(a.shape[0] for a in ins) + 1
    msg = jax.ShapeDtypeStruct((part * probes + TAIL, order), I16)
    out = pl.pallas_call(
        functools.partial(partial_kernel, front, cols, len(ins)),
        out_shape=[jax.ShapeDtypeStruct((part, probes, order), F32)] + [msg] * (cols - 1),
        in_specs=[SMEM, ANY] + [VMEM] * len(ins),
        out_specs=[VMEM] * cols,
        scratch_shapes=[
            pltpu.VMEM((rows_dev, slots, order, order), BF16),
            pltpu.VMEM((known_rows, probes, order), BF16),
            pltpu.SemaphoreType.DMA((cols,)),
        ],
        compiler_params=pltpu.CompilerParams(vmem_limit_bytes=32 * 2**20),
        name=f"partial_{front}",
    )(idx, blocks, *ins)
    return out[0], out[1:]


def solve_kernel(cols, own_ref, *refs):
    msgs, rhs_ref, inv_ref, out_ref = refs[: cols - 1], refs[cols - 1], refs[cols], refs[cols + 1]
    part, probes, _ = own_ref.shape
    total = [own_ref[k] for k in range(part)]
    for msg in msgs:
        total = [a + b for a, b in zip(total, decode_blocks(msg, part, probes))]
    solved = [
        lax.dot_general(
            rhs_ref[k] - total[k],
            inv_ref[k],
            (((1,), (1,)), ((), ())),
            precision=lax.Precision.HIGHEST,
            preferred_element_type=F32,
        )
        for k in range(part)
    ]
    encode_blocks(solved, out_ref, probes)


def solve_part(cols, own, msgs, rhs, inverse):
    part, probes, order = own.shape
    return pl.pallas_call(
        functools.partial(solve_kernel, cols),
        out_shape=jax.ShapeDtypeStruct((part * probes + TAIL, order), I16),
        in_specs=[VMEM] * (cols + 2),
        out_specs=VMEM,
        name="solve",
    )(own, *msgs, rhs, inverse)


def pack_kernel(cols, groups, cap, sel_ref, *refs):
    msgs, out_ref, sends, rows = refs[:cols], refs[cols], refs[cols + 1 : -1], refs[-1]
    part = rows.shape[0] // cols
    probes = rows.shape[1]
    here = sel_ref[groups * cap]
    for s in range(cols):
        first = lax.rem(here + cols - s, cols) * part
        for k, value in enumerate(decode_blocks(msgs[s], part, probes)):
            out_ref[0, first + k] = value
            rows[first + k] = value.astype(BF16)
    for m in range(groups):
        for q in range(cap):
            sends[m][q] = rows[sel_ref[m * cap + q]]


def pack(cols, groups, cap, sel, msgs, shape):
    _, rows_dev, probes, order = shape
    out = pl.pallas_call(
        functools.partial(pack_kernel, cols, groups, cap),
        out_shape=[jax.ShapeDtypeStruct(shape, F32)]
        + [jax.ShapeDtypeStruct((cap, probes, order), BF16)] * groups,
        in_specs=[SMEM] + [VMEM] * cols,
        out_specs=[VMEM] * (groups + 1),
        scratch_shapes=[pltpu.VMEM((rows_dev, probes, order), BF16)],
        name="pack",
    )(sel, *msgs)
    return out[0], out[1:]


def last_kernel(cols, here_ref, first_ref, *refs):
    msgs, out_ref = refs[:cols], refs[cols]
    part = out_ref.shape[1] // cols
    probes = out_ref.shape[2]
    out_ref[0] = first_ref[0]
    for s in range(cols):
        first = lax.rem(here_ref[0] + cols - s, cols) * part
        for k, value in enumerate(decode_blocks(msgs[s], part, probes)):
            out_ref[1, first + k] = value


def last(cols, here, first, msgs, shape):
    return pl.pallas_call(
        functools.partial(last_kernel, cols),
        out_shape=jax.ShapeDtypeStruct(shape, F32),
        in_specs=[SMEM, VMEM] + [VMEM] * cols,
        out_specs=VMEM,
        name="last",
    )(here, first, *msgs)


def shards(groups, cols, owner_map, colidx, live, blocks, diag_inverse, right_side, prior):
    _, rows_dev, slots, order, _ = blocks.shape
    probes = right_side.shape[2]
    prior_dev = prior.shape[0]
    prior_count = groups * prior_dev
    half = groups // 2
    part = rows_dev // cols
    cap = -(-((slots + 1) // 2) * rows_dev // groups)
    me = lax.axis_index("rows")
    here = lax.axis_index("cols")

    def over_rows(x, mask):
        return lax.ppermute(x, "rows", [(i, i ^ mask) for i in range(groups)])

    def over_cols(x, step):
        return lax.ppermute(x, "cols", [(i, (i + step) % cols) for i in range(cols)])

    chips = jnp.concatenate([over_rows(prior, 2 * k) for k in range(1, half)])
    mate = over_rows(prior, 1)
    mate_chips = over_rows(chips, 1)
    early = [prior, chips, mate, mate_chips]

    slot_ids = here * slots + jnp.arange(slots, dtype=I32)
    is_live = slot_ids[None, None, :] < live[:, :, None]
    owner = lax.div(colidx, jnp.int32(prior_dev)) ^ me
    early_at = (
        (owner & 1) * (half * prior_dev)
        + lax.shift_right_logical(owner, jnp.int32(1)) * prior_dev
        + lax.rem(colidx, jnp.int32(prior_dev))
    )
    here_vec = here.astype(I32).reshape(1)
    zero_at = jnp.int32(prior_count)
    first_at = jnp.where(is_live[0], early_at[0], zero_at).reshape(-1)
    own0, msgs0 = partial_products(
        0, cols, jnp.concatenate([first_at, here_vec]), blocks, early
    )

    def find(refs):
        hit = owner_map[0][None, None, :] == (refs - prior_count)[:, :, None]
        ids = jnp.arange(owner_map.shape[1], dtype=I32)
        return jnp.sum(jnp.where(hit, ids[None, None, :], 0), axis=2, dtype=I32)

    flat, msgs0 = lax.optimization_barrier((colidx[1].reshape(1, -1), msgs0))
    near = jnp.concatenate([flat] + [over_rows(flat, 2 * k) for k in range(1, half)])
    refs = jnp.concatenate([near, over_rows(near, 1)])
    order_k = jnp.arange(rows_dev * slots, dtype=I32)
    before = order_k[None, :] < order_k[:, None]
    spots = find(refs)
    mine = (refs >= prior_count) & (lax.div(spots, jnp.int32(rows_dev)) == me)
    rank = jnp.sum(mine[:, None, :] & before[None], axis=2, dtype=I32)
    pick = mine[:, None, :] & (rank[:, None, :] == jnp.arange(cap, dtype=I32)[None, :, None])
    wanted = jnp.sum(
        jnp.where(pick, lax.rem(spots, jnp.int32(rows_dev))[:, None, :], 0), axis=2, dtype=I32
    )

    spot = spots[0]
    is_ref = refs[0] >= prior_count
    holder = lax.div(spot, jnp.int32(rows_dev)) ^ me
    same = (holder[:, None] == holder[None, :]) & is_ref[None, :] & before
    my_rank = jnp.sum(same, axis=1, dtype=I32)
    holder_at = (holder & 1) * half + lax.shift_right_logical(holder, jnp.int32(1))
    recent_at = prior_count + holder_at * cap + my_rank
    second_at = jnp.where(is_ref, recent_at, early_at[1].reshape(-1))
    second_at = jnp.where(is_live[1].reshape(-1), second_at, prior_count + groups * cap)

    rhs_part = lax.dynamic_slice_in_dim(right_side, here * part, part, axis=1)
    inv_part = lax.dynamic_slice_in_dim(diag_inverse, here * part, part, axis=1)

    got0 = [over_cols(m, s + 1) for s, m in enumerate(msgs0)]
    coded0 = solve_part(cols, own0, got0, rhs_part[0], inv_part[0])
    all0 = [coded0] + [over_cols(coded0, s) for s in range(1, cols)]

    first, sends = pack(
        cols,
        groups,
        cap,
        jnp.concatenate([wanted.reshape(-1), here_vec]),
        all0,
        (1,) + right_side.shape[1:],
    )
    masks = [2 * k for k in range(half)] + [2 * k + 1 for k in range(half)]
    recent = [x if m == 0 else over_rows(x, m) for m, x in zip(masks, sends)]

    own1, msgs1 = partial_products(
        1, cols, jnp.concatenate([second_at, here_vec]), blocks, early + recent
    )
    got1 = [over_cols(m, s + 1) for s, m in enumerate(msgs1)]
    coded1 = solve_part(cols, own1, got1, rhs_part[1], inv_part[1])
    all1 = [coded1] + [over_cols(coded1, s) for s in range(1, cols)]
    return last(cols, here_vec, first, all1, right_side.shape)


def solution(mesh):
    placed = (
        P(),
        P(None, "rows", "cols"),
        P(None, "rows"),
        P(None, "rows", "cols", None, None),
        P(None, "rows", None, None),
        P(None, "rows", None, None),
        P("rows", None, None),
    )
    body = functools.partial(shards, mesh.shape["rows"], mesh.shape["cols"])
    return jax.shard_map(
        body, mesh=mesh, in_specs=placed, out_specs=P(None, "rows", None, None), check_vma=False
    )
```

time: 172 us -> 99.7 us (0.58)
  waiting for transfers between devices: 127 us -> 35 us
  starting transfers between devices: 0.13 us -> 28.5 us
  matrix products: 16.8 us -> 0 us
  Pallas kernels: 0 us -> 15.3 us
  between operations: 13.3 us -> 0.26 us
  local copies, waits for them, and re-layouts: 12.9 us -> 16.9 us
    psum x2 -> x0, waiting for transfers between devices: 76.8 us -> none  [finish(): total = lax.psum(partial_value, 'cols')]
    all_gather x2 -> x0, waiting for transfers between devices: 49.1 us -> none  [the longest x1 26.3 us: shards(): prior_all = lax.all_gather(prior, 'rows', axis=0, tiled=True)]
    ppermute x0 -> x28, waiting for transfers between devices: none -> 35 us  [the longest x12 20.2 us: over_cols(): lax.ppermute(x, 'cols', [(i, (i + step) % cols) for i in range(cols)])]
    ppermute x0 -> x28, starting transfers between devices: none -> 28.5 us  [the longest x12 15.6 us: over_cols(): lax.ppermute(x, 'cols', [(i, (i + step) % cols) for i in range(cols)])]
    dot_general x4 -> x0, matrix products: 16.8 us -> none  [the longest x2 9.45 us: block_products(): jnp.einsum('rjcb,rjpb->rpc', blk, values, preferred_element_type=jnp.floa...]
    pallas_call x0 -> x6, Pallas kernels: none -> 15.3 us  [the longest x2 5.79 us: partial_products(): pl.pallas_call(functools.partial(partial_kernel, front, cols, len(ins)),...]
    unnamed x10 -> x38, local copies, waits for them, and re-layouts: 0.02 us -> 11 us
    gather x6 -> x0, local copies, waits for them, and re-layouts: 10.1 us -> none  [the longest x1 3.54 us: shards(): recent_values = whole_front[slot_pos]]
  transfers between devices with their start and end apart: 4 -> 28, of which waited for: 4 -> 17; matrix products, arithmetic and copies ran while one was open for 4% -> 9% of each run, Pallas kernels for 0% -> 0%
where the time goes in v1:
time: 99.7 us; the launch traced here: 99.2 us
  waiting for transfers between devices  35 us (35%)
  starting transfers between devices  28.5 us (29%)
  local copies, waits for them, and re-layouts  16.9 us (17%)
  Pallas kernels  15.3 us (15%)
  other arithmetic  3.28 us (3%)
    ppermute x12, waiting for transfers between devices, over_cols(): lax.ppermute(x, 'cols', [(i, (i + step) % cols) for i in range(cols)])  20.2 us
    ppermute x12, starting transfers between devices, over_cols(): lax.ppermute(x, 'cols', [(i, (i + step) % cols) for i in range(cols)])  15.6 us
    ppermute x16, waiting for transfers between devices, over_rows(): return lax.ppermute(x, 'rows', [(i, i ^ mask) for i in range(groups)])  14.8 us
    ppermute x16, starting transfers between devices, over_rows(): return lax.ppermute(x, 'rows', [(i, i ^ mask) for i in range(groups)])  12.9 us
    unnamed x38, local copies, waits for them, and re-layouts  11 us
    pallas_call x2, Pallas kernels, partial_products(): pl.pallas_call(functools.partial(partial_kernel, front, cols, len(ins)),...  5.79 us
    pallas_call x2, Pallas kernels, solve_part(): pl.pallas_call(functools.partial(solve_kernel, cols), out_shape=jax.Shape...  5.11 us
    squeeze x2, local copies, waits for them, and re-layouts, shards(): coded1 = solve_part(cols, own1, got1, rhs_part[1], inv_part[1])  3.56 us
  transfers between devices with their start and end apart: 28, of which 17 were waited for; matrix products, arithmetic and copies ran while one was open for 9% of the time, Pallas kernels for 0%

profile of v1, /device:TPU:0, one launch (start us, length us, event | category | flops | bytes accessed | tf_op | source)
XLA Modules:
  0.0 99.2 jit_solution(18247323056166383571)
XLA Ops:
  0.5 3.5 %collective-permute-start.2 = (bf16[8,64,128]{2,1,0:T(8,128)(2,1)}, bf16[8,64,128]{2,1,0:T(8,128)(2,1)S(1)}, u32[]{:S(2)}, u32[]{:S(2)}) collective-permute-start(bf16[8,64,128]{2,1,0:T(8,128)(2,1)} %refs_0_.3), channel_id=1, source_target_pairs={{0,24},{4,28},{8,16},{12,20},{16,8},{20,12},{24,0},{28,4},{1,25},{... | collective-permute-start | bytes 393224 | tf_op jit(solution)/shard_map/ppermute | solution.py:196
  6.8 4.6 %collective-permute-done = bf16[8,64,128]{2,1,0:T(8,128)(2,1)S(1)} collective-permute-done((bf16[8,64,128]{2,1,0:T(8,128)(2,1)}, bf16[8,64,128]{2,1,0:T(8,128)(2,1)S(1)}, u32[]{:S(2)}, u32[]{:S(2)}) %collective-permute-start) | collective-permute-done | bytes 131104 | tf_op jit(solution)/shard_map/ppermute | solution.py:196
  11.7 1.7 %dynamic-slice_bitcast_fusion.2 = (f32[4,64,128]{2,1,0:T(8,128)}, f32[4,64,128]{2,1,0:T(8,128)}) fusion(f32[2,16,64,128]{3,2,1,0:T(8,128)} %param.12, s32[]{:T(128)S(6)} %add.48, s32[]{:T(128)S(6)} %select_n.32), kind=kLoop, calls=%fused_computation.4 | loop fusion | bytes 524296 | tf_op jit(solution)/shard_map/squeeze | solution.py:271
  14.4 1.9 %dynamic-slice_bitcast_fusion = (f32[4,128,128]{2,1,0:T(8,128)}, f32[4,128,128]{2,1,0:T(8,128)}) fusion(f32[2,16,128,128]{3,2,1,0:T(8,128)} %param.11, s32[]{:T(128)S(6)} %add.48, s32[]{:T(128)S(6)} %select_n.32), kind=kLoop, calls=%fused_computation.2 | loop fusion | bytes 1048584 | tf_op jit(solution)/shard_map/squeeze | solution.py:271
  16.3 2.8 %copy-done = bf16[2,16,6,128,128]{4,3,2,1,0:T(8,128)(2,1)S(1)} copy-done((bf16[2,16,6,128,128]{4,3,2,1,0:T(8,128)(2,1)S(1)}, bf16[2,16,6,128,128]{4,3,2,1,0:T(8,128)(2,1)}, u32[]{:S(2)}) %copy-start) | copy-done | bytes 6291480
  19.1 2.9 %partial_0.1 = (f32[4,64,128]{2,1,0:T(8,128)S(1)}, s16[272,128]{1,0:T(8,128)(2,1)S(1)}, s16[272,128]{1,0:T(8,128)(2,1)S(1)}, s16[272,128]{1,0:T(8,128)(2,1)S(1)}) custom-call(s32[97]{0:T(128)S(1)} %pad_add_fusion.1.idx_ref, bf16[2,16,6,128,128]{4,3,2,1,0:T(8,128)(2,1)S(1)} %copy-done, bf16[8,64,128]{2,1,0:T(8,128)(2,1)S(1)} %copy-done.2, ...), custom_call_target="tpu_custom_call" | custom-call | tf_op jit(solution)/shard_map/partial_0/pallas_call | solution.py:88
  30.8 2.6 %collective-permute-start.10 = (s16[272,128]{1,0:T(8,128)(2,1)S(1)}, s16[272,128]{1,0:T(8,128)(2,1)S(1)}, u32[]{:S(2)}, u32[]{:S(2)}) collective-permute-start(s16[272,128]{1,0:T(8,128)(2,1)S(1)} %get-tuple-element.32), channel_id=1, source_target_pairs={{0,2},{1,3},{2,0},{3,1},{4,6},{5,7},{6,4},{7,5},{8,10},{9,11},{10,... | collective-permute-start | bytes 208904 | tf_op jit(solution)/shard_map/ppermute | solution.py:199
  36.0 2.7 %collective-permute-done.10.refs_1_ = s16[272,128]{1,0:T(8,128)(2,1)S(1)} collective-permute-done((s16[272,128]{1,0:T(8,128)(2,1)S(1)}, s16[272,128]{1,0:T(8,128)(2,1)S(1)}, u32[]{:S(2)}, u32[]{:S(2)}) %collective-permute-start.10) | collective-permute-done | bytes 69664 | tf_op jit(solution)/shard_map/ppermute | solution.py:199
  39.6 2.6 %solve.2.refs_0_ = s16[272,128]{1,0:T(8,128)(2,1)} custom-call(f32[4,64,128]{2,1,0:T(8,128)} %copy-done.3, s16[272,128]{1,0:T(8,128)(2,1)} %copy-done.6, s16[272,128]{1,0:T(8,128)(2,1)} %copy-done.7, s16[272,128]{1,0:T(8,128)(2,1)} %copy-done.8, f32[4,64,128]{2,1,0:T(8,128)} %get-tuple-element.50.refs_3_, f32[4,128,128]{2,1,0:T(8,128)} %get-tuple-element.48.refs_4_), custom_call_target="tpu_custom_call" | custom-call | tf_op jit(solution)/shard_map/solve/pallas_call | solution.py:125
  42.1 2.8 %collective-permute-start.14 = (s16[272,128]{1,0:T(8,128)(2,1)}, s16[272,128]{1,0:T(8,128)(2,1)S(1)}, u32[]{:S(2)}, u32[]{:S(2)}) collective-permute-start(s16[272,128]{1,0:T(8,128)(2,1)} %solve.2.refs_0_), channel_id=1, source_target_pairs={{0,3},{1,0},{2,1},{3,2},{4,7},{5,4},{6,5},{7,6},{8,11},{9,8},{10,9... | collective-permute-start | bytes 208904 | tf_op jit(solution)/shard_map/ppermute | solution.py:199
  46.2 1.7 %collective-permute-done.14.refs_3_ = s16[272,128]{1,0:T(8,128)(2,1)S(1)} collective-permute-done((s16[272,128]{1,0:T(8,128)(2,1)}, s16[272,128]{1,0:T(8,128)(2,1)S(1)}, u32[]{:S(2)}, u32[]{:S(2)}) %collective-permute-start.14) | collective-permute-done | bytes 69664 | tf_op jit(solution)/shard_map/ppermute | solution.py:199
  47.9 4.4 %collective-permute-done.13.refs_2_ = s16[272,128]{1,0:T(8,128)(2,1)S(1)} collective-permute-done((s16[272,128]{1,0:T(8,128)(2,1)}, s16[272,128]{1,0:T(8,128)(2,1)S(1)}, u32[]{:S(2)}, u32[]{:S(2)}) %collective-permute-start.13) | collective-permute-done | bytes 69664 | tf_op jit(solution)/shard_map/ppermute | solution.py:199
  53.5 2.2 %pack.1 = (f32[1,16,64,128]{3,2,1,0:T(8,128)}, bf16[6,64,128]{2,1,0:T(8,128)(2,1)}, bf16[6,64,128]{2,1,0:T(8,128)(2,1)}, bf16[6,64,128]{2,1,0:T(8,128)(2,1)}, bf...) custom-call(s32[49]{0:T(128)} %pad_add_fusion.2.sel_ref, ...), custom_call_target="tpu_custom_call" | custom-call | tf_op jit(solution)/shard_map/pack/pallas_call | solution.py:151
  64.4 3.7 %collective-permute-done.20.refs_10_ = bf16[6,64,128]{2,1,0:T(8,128)(2,1)S(1)} collective-permute-done((bf16[6,64,128]{2,1,0:T(8,128)(2,1)}, bf16[6,64,128]{2,1,0:T(8,128)(2,1)S(1)}, u32[]{:S(2)}, u32[]{:S(2)}) %collective-permute-start.20) | collective-permute-done | bytes 98336 | tf_op jit(solution)/shard_map/ppermute | solution.py:196
  68.0 2.8 %copy-done.1 = bf16[2,16,6,128,128]{4,3,2,1,0:T(8,128)(2,1)S(1)} copy-done((bf16[2,16,6,128,128]{4,3,2,1,0:T(8,128)(2,1)S(1)}, bf16[2,16,6,128,128]{4,3,2,1,0:T(8,128)(2,1)}, u32[]{:S(2)}) %copy-start.1) | copy-done | bytes 6291480
  71.7 2.9 %partial_1.1 = (f32[4,64,128]{2,1,0:T(8,128)S(1)}, s16[272,128]{1,0:T(8,128)(2,1)S(1)}, s16[272,128]{1,0:T(8,128)(2,1)S(1)}, s16[272,128]{1,0:T(8,128)(2,1)S(1)}) custom-call(s32[97]{0:T(128)S(1)} %pad_add_fusion.3.idx_ref, bf16[2,16,6,128,128]{4,3,2,1,0:T(8,128)(2,1)S(1)} %copy-done.1, bf16[8,64,128]{2,1,0:T(8,128)(2,1)S(1)} %copy-done.2, ...), custom_call_target="tpu_custom_call" | custom-call | tf_op jit(solution)/shard_map/partial_1/pallas_call | solution.py:88
  75.3 1.9 %collective-permute-start.23 = (s16[272,128]{1,0:T(8,128)(2,1)S(1)}, s16[272,128]{1,0:T(8,128)(2,1)S(1)}, u32[]{:S(2)}, u32[]{:S(2)}) collective-permute-start(s16[272,128]{1,0:T(8,128)(2,1)S(1)} %get-tuple-element.45), channel_id=1, source_target_pairs={{0,2},{1,3},{2,0},{3,1},{4,6},{5,7},{6,4},{7,5},{8,10},{9,11},{10,... | collective-permute-start | bytes 208904 | tf_op jit(solution)/shard_map/ppermute | solution.py:199
  77.2 1.9 %collective-permute-start.24 = (s16[272,128]{1,0:T(8,128)(2,1)S(1)}, s16[272,128]{1,0:T(8,128)(2,1)S(1)}, u32[]{:S(2)}, u32[]{:S(2)}) collective-permute-start(s16[272,128]{1,0:T(8,128)(2,1)S(1)} %get-tuple-element.46), channel_id=1, source_target_pairs={{0,3},{1,0},{2,1},{3,2},{4,7},{5,4},{6,5},{7,6},{8,11},{9,8},{10,9... | collective-permute-start | bytes 208904 | tf_op jit(solution)/shard_map/ppermute | solution.py:199
  79.1 3.1 %collective-permute-done.22.refs_0_ = s16[272,128]{1,0:T(8,128)(2,1)S(1)} collective-permute-done((s16[272,128]{1,0:T(8,128)(2,1)S(1)}, s16[272,128]{1,0:T(8,128)(2,1)S(1)}, u32[]{:S(2)}, u32[]{:S(2)}) %collective-permute-start.22) | collective-permute-done | bytes 69664 | tf_op jit(solution)/shard_map/ppermute | solution.py:199
  84.3 2.6 %solve.3.refs_0_ = s16[272,128]{1,0:T(8,128)(2,1)} custom-call(f32[4,64,128]{2,1,0:T(8,128)} %copy-done.4, s16[272,128]{1,0:T(8,128)(2,1)} %copy-done.9, s16[272,128]{1,0:T(8,128)(2,1)} %copy-done.10, s16[272,128]{1,0:T(8,128)(2,1)} %copy-done.12, f32[4,64,128]{2,1,0:T(8,128)} %get-tuple-element.49.refs_3_, f32[4,128,128]{2,1,0:T(8,128)} %get-tuple-element.47.refs_4_), custom_call_target="tpu_custom_call" | custom-call | tf_op jit(solution)/shard_map/solve/pallas_call | solution.py:125
  86.9 2.2 %collective-permute-start.27 = (s16[272,128]{1,0:T(8,128)(2,1)}, s16[272,128]{1,0:T(8,128)(2,1)S(1)}, u32[]{:S(2)}, u32[]{:S(2)}) collective-permute-start(s16[272,128]{1,0:T(8,128)(2,1)} %solve.3.refs_0_), channel_id=1, source_target_pairs={{0,3},{1,0},{2,1},{3,2},{4,7},{5,4},{6,5},{7,6},{8,11},{9,8},{10,9... | collective-permute-start | bytes 208904 | tf_op jit(solution)/shard_map/ppermute | solution.py:199
  89.7 2.4 %collective-permute-done.27.refs_3_ = s16[272,128]{1,0:T(8,128)(2,1)S(1)} collective-permute-done((s16[272,128]{1,0:T(8,128)(2,1)}, s16[272,128]{1,0:T(8,128)(2,1)S(1)}, u32[]{:S(2)}, u32[]{:S(2)}) %collective-permute-start.27) | collective-permute-done | bytes 69664 | tf_op jit(solution)/shard_map/ppermute | solution.py:199
  92.1 4.3 %collective-permute-done.26.refs_2_ = s16[272,128]{1,0:T(8,128)(2,1)S(1)} collective-permute-done((s16[272,128]{1,0:T(8,128)(2,1)}, s16[272,128]{1,0:T(8,128)(2,1)S(1)}, u32[]{:S(2)}, u32[]{:S(2)}) %collective-permute-start.26) | collective-permute-done | bytes 69664 | tf_op jit(solution)/shard_map/ppermute | solution.py:199
  97.0 2.2 %last.1 = f32[2,16,64,128]{3,2,1,0:T(8,128)} custom-call(s32[1]{0:T(128)} %bitcast.here_ref, f32[1,16,64,128]{3,2,1,0:T(8,128)} %get-tuple-element.34.first_ref, s16[272,128]{1,0:T(8,128)(2,1)} %solve.3.refs_0_, s16[272,128]{1,0:T(8,128)(2,1)} %copy-done.14, s16[272,128]{1,0:T(8,128)(2,1)} %copy-done.13, s16[272,128]{1,0:T(8,128)(2,1)} %copy-done.11), custom_call_target="tpu_custom_call" | custom-call | tf_op jit(solution)/shard_map/last/pallas_call | solution.py:175
  (113 shorter events, 32.8 us)
Async XLA Ops:
  0.0 16.3 %collective-permute-start.3 = (bf16[8,64,128]{2,1,0:T(8,128)(2,1)}, bf16[8,64,128]{2,1,0:T(8,128)(2,1)S(1)}, u32[]{:S(2)}, u32[]{:S(2)}) collective-permute-start(bf16[8,64,128]{2,1,0:T(8,128)(2,1)} %refs_0_.3), channel_id=1, source_target_pairs={{0,4},{4,0},{8,12},{12,8},{16,20},{20,16},{24,28},{28,24},{1,5},{5... | collective-permute-start | bytes 393224 | tf_op jit(solution)/shard_map/ppermute | solution.py:196
  0.5 11.0 %collective-permute-start.2 = (bf16[8,64,128]{2,1,0:T(8,128)(2,1)}, bf16[8,64,128]{2,1,0:T(8,128)(2,1)S(1)}, u32[]{:S(2)}, u32[]{:S(2)}) collective-permute-start(bf16[8,64,128]{2,1,0:T(8,128)(2,1)} %refs_0_.3), channel_id=1, source_target_pairs={{0,24},{4,28},{8,16},{12,20},{16,8},{20,12},{24,0},{28,4},{1,25},{... | collective-permute-start | bytes 393224 | tf_op jit(solution)/shard_map/ppermute | solution.py:196
  4.0 7.4 %collective-permute-start.1 = (bf16[8,64,128]{2,1,0:T(8,128)(2,1)}, bf16[8,64,128]{2,1,0:T(8,128)(2,1)S(1)}, u32[]{:S(2)}, u32[]{:S(2)}) collective-permute-start(bf16[8,64,128]{2,1,0:T(8,128)(2,1)} %refs_0_.3), channel_id=1, source_target_pairs={{0,16},{4,20},{8,24},{12,28},{16,0},{20,4},{24,8},{28,12},{1,17},{... | collective-permute-start | bytes 393224 | tf_op jit(solution)/shard_map/ppermute | solution.py:196
  4.5 6.9 %collective-permute-start = (bf16[8,64,128]{2,1,0:T(8,128)(2,1)}, bf16[8,64,128]{2,1,0:T(8,128)(2,1)S(1)}, u32[]{:S(2)}, u32[]{:S(2)}) collective-permute-start(bf16[8,64,128]{2,1,0:T(8,128)(2,1)} %refs_0_.3), channel_id=1, source_target_pairs={{0,8},{4,12},{8,0},{12,4},{16,24},{20,28},{24,16},{28,20},{1,9},{5... | collective-permute-start | bytes 393224 | tf_op jit(solution)/shard_map/ppermute | solution.py:196
  29.1 5.7 %collective-permute-start.8 = (s32[4,96]{1,0:T(4,128)S(1)}, s32[4,96]{1,0:T(4,128)S(1)}, u32[]{:S(2)}, u32[]{:S(2)}) collective-permute-start(s32[4,96]{1,0:T(4,128)S(1)} %pad_add_fusion), channel_id=1, source_target_pairs={{0,4},{4,0},{8,12},{12,8},{16,20},{20,16},{24,28},{28,24},{1,5},{5... | collective-permute-start | bytes 4616 | tf_op jit(solution)/shard_map/ppermute | solution.py:196
  29.2 6.8 %collective-permute-start.9 = (s16[272,128]{1,0:T(8,128)(2,1)S(1)}, s16[272,128]{1,0:T(8,128)(2,1)S(1)}, u32[]{:S(2)}, u32[]{:S(2)}) collective-permute-start(s16[272,128]{1,0:T(8,128)(2,1)S(1)} %get-tuple-element.31), channel_id=1, source_target_pairs={{0,1},{1,2},{2,3},{3,0},{4,5},{5,6},{6,7},{7,4},{8,9},{9,10},{10,1... | collective-permute-start | bytes 208904 | tf_op jit(solution)/shard_map/ppermute | solution.py:199
  30.8 7.9 %collective-permute-start.10 = (s16[272,128]{1,0:T(8,128)(2,1)S(1)}, s16[272,128]{1,0:T(8,128)(2,1)S(1)}, u32[]{:S(2)}, u32[]{:S(2)}) collective-permute-start(s16[272,128]{1,0:T(8,128)(2,1)S(1)} %get-tuple-element.32), channel_id=1, source_target_pairs={{0,2},{1,3},{2,0},{3,1},{4,6},{5,7},{6,4},{7,5},{8,10},{9,11},{10,... | collective-permute-start | bytes 208904 | tf_op jit(solution)/shard_map/ppermute | solution.py:199
  33.4 5.5 %collective-permute-start.11 = (s16[272,128]{1,0:T(8,128)(2,1)S(1)}, s16[272,128]{1,0:T(8,128)(2,1)S(1)}, u32[]{:S(2)}, u32[]{:S(2)}) collective-permute-start(s16[272,128]{1,0:T(8,128)(2,1)S(1)} %get-tuple-element.33), channel_id=1, source_target_pairs={{0,3},{1,0},{2,1},{3,2},{4,7},{5,4},{6,5},{7,6},{8,11},{9,8},{10,9... | collective-permute-start | bytes 208904 | tf_op jit(solution)/shard_map/ppermute | solution.py:199
  42.1 5.7 %collective-permute-start.14 = (s16[272,128]{1,0:T(8,128)(2,1)}, s16[272,128]{1,0:T(8,128)(2,1)S(1)}, u32[]{:S(2)}, u32[]{:S(2)}) collective-permute-start(s16[272,128]{1,0:T(8,128)(2,1)} %solve.2.refs_0_), channel_id=1, source_target_pairs={{0,3},{1,0},{2,1},{3,2},{4,7},{5,4},{6,5},{7,6},{8,11},{9,8},{10,9... | collective-permute-start | bytes 208904 | tf_op jit(solution)/shard_map/ppermute | solution.py:199
  45.0 7.3 %collective-permute-start.13 = (s16[272,128]{1,0:T(8,128)(2,1)}, s16[272,128]{1,0:T(8,128)(2,1)S(1)}, u32[]{:S(2)}, u32[]{:S(2)}) collective-permute-start(s16[272,128]{1,0:T(8,128)(2,1)} %solve.2.refs_0_), channel_id=1, source_target_pairs={{0,2},{1,3},{2,0},{3,1},{4,6},{5,7},{6,4},{7,5},{8,10},{9,11},{10,... | collective-permute-start | bytes 208904 | tf_op jit(solution)/shard_map/ppermute | solution.py:199
  45.3 7.0 %collective-permute-start.12 = (s16[272,128]{1,0:T(8,128)(2,1)}, s16[272,128]{1,0:T(8,128)(2,1)S(1)}, u32[]{:S(2)}, u32[]{:S(2)}) collective-permute-start(s16[272,128]{1,0:T(8,128)(2,1)} %solve.2.refs_0_), channel_id=1, source_target_pairs={{0,1},{1,2},{2,3},{3,0},{4,5},{5,6},{6,7},{7,4},{8,9},{9,10},{10,1... | collective-permute-start | bytes 208904 | tf_op jit(solution)/shard_map/ppermute | solution.py:199
  55.7 5.6 %collective-permute-start.15 = (bf16[6,64,128]{2,1,0:T(8,128)(2,1)}, bf16[6,64,128]{2,1,0:T(8,128)(2,1)S(1)}, u32[]{:S(2)}, u32[]{:S(2)}) collective-permute-start(bf16[6,64,128]{2,1,0:T(8,128)(2,1)} %get-tuple-element.36), channel_id=1, source_target_pairs={{0,8},{4,12},{8,0},{12,4},{16,24},{20,28},{24,16},{28,20},{1,9},{5... | collective-permute-start | bytes 294920 | tf_op jit(solution)/shard_map/ppermute | solution.py:196
  56.2 5.9 %collective-permute-start.16 = (bf16[6,64,128]{2,1,0:T(8,128)(2,1)}, bf16[6,64,128]{2,1,0:T(8,128)(2,1)S(1)}, u32[]{:S(2)}, u32[]{:S(2)}) collective-permute-start(bf16[6,64,128]{2,1,0:T(8,128)(2,1)} %get-tuple-element.37), channel_id=1, source_target_pairs={{0,16},{4,20},{8,24},{12,28},{16,0},{20,4},{24,8},{28,12},{1,17},{... | collective-permute-start | bytes 294920 | tf_op jit(solution)/shard_map/ppermute | solution.py:196
  57.7 6.6 %collective-permute-start.17 = (bf16[6,64,128]{2,1,0:T(8,128)(2,1)}, bf16[6,64,128]{2,1,0:T(8,128)(2,1)S(1)}, u32[]{:S(2)}, u32[]{:S(2)}) collective-permute-start(bf16[6,64,128]{2,1,0:T(8,128)(2,1)} %get-tuple-element.38), channel_id=1, source_target_pairs={{0,24},{4,28},{8,16},{12,20},{16,8},{20,12},{24,0},{28,4},{1,25},{... | collective-permute-start | bytes 294920 | tf_op jit(solution)/shard_map/ppermute | solution.py:196
  59.3 5.0 %collective-permute-start.18 = (bf16[6,64,128]{2,1,0:T(8,128)(2,1)}, bf16[6,64,128]{2,1,0:T(8,128)(2,1)S(1)}, u32[]{:S(2)}, u32[]{:S(2)}) collective-permute-start(bf16[6,64,128]{2,1,0:T(8,128)(2,1)} %get-tuple-element.39), channel_id=1, source_target_pairs={{0,4},{4,0},{8,12},{12,8},{16,20},{20,16},{24,28},{28,24},{1,5},{5... | collective-permute-start | bytes 294920 | tf_op jit(solution)/shard_map/ppermute | solution.py:196
  59.3 5.1 %collective-permute-start.19 = (bf16[6,64,128]{2,1,0:T(8,128)(2,1)}, bf16[6,64,128]{2,1,0:T(8,128)(2,1)S(1)}, u32[]{:S(2)}, u32[]{:S(2)}) collective-permute-start(bf16[6,64,128]{2,1,0:T(8,128)(2,1)} %get-tuple-element.40), channel_id=1, source_target_pairs={{0,12},{4,8},{8,4},{12,0},{16,28},{20,24},{24,20},{28,16},{1,13},{... | collective-permute-start | bytes 294920 | tf_op jit(solution)/shard_map/ppermute | solution.py:196
  61.3 6.7 %collective-permute-start.20 = (bf16[6,64,128]{2,1,0:T(8,128)(2,1)}, bf16[6,64,128]{2,1,0:T(8,128)(2,1)S(1)}, u32[]{:S(2)}, u32[]{:S(2)}) collective-permute-start(bf16[6,64,128]{2,1,0:T(8,128)(2,1)} %get-tuple-element.41), channel_id=1, source_target_pairs={{0,20},{4,16},{8,28},{12,24},{16,4},{20,0},{24,12},{28,8},{1,21},{... | collective-permute-start | bytes 294920 | tf_op jit(solution)/shard_map/ppermute | solution.py:196
  62.1 5.9 %collective-permute-start.21 = (bf16[6,64,128]{2,1,0:T(8,128)(2,1)}, bf16[6,64,128]{2,1,0:T(8,128)(2,1)S(1)}, u32[]{:S(2)}, u32[]{:S(2)}) collective-permute-start(bf16[6,64,128]{2,1,0:T(8,128)(2,1)} %get-tuple-element.42), channel_id=1, source_target_pairs={{0,28},{4,24},{8,20},{12,16},{16,12},{20,8},{24,4},{28,0},{1,29},{... | collective-permute-start | bytes 294920 | tf_op jit(solution)/shard_map/ppermute | solution.py:196
  75.3 6.9 %collective-permute-start.22 = (s16[272,128]{1,0:T(8,128)(2,1)S(1)}, s16[272,128]{1,0:T(8,128)(2,1)S(1)}, u32[]{:S(2)}, u32[]{:S(2)}) collective-permute-start(s16[272,128]{1,0:T(8,128)(2,1)S(1)} %get-tuple-element.44), channel_id=1, source_target_pairs={{0,1},{1,2},{2,3},{3,0},{4,5},{5,6},{6,7},{7,4},{8,9},{9,10},{10,1... | collective-permute-start | bytes 208904 | tf_op jit(solution)/shard_map/ppermute | solution.py:199
  75.3 8.3 %collective-permute-start.23 = (s16[272,128]{1,0:T(8,128)(2,1)S(1)}, s16[272,128]{1,0:T(8,128)(2,1)S(1)}, u32[]{:S(2)}, u32[]{:S(2)}) collective-permute-start(s16[272,128]{1,0:T(8,128)(2,1)S(1)} %get-tuple-element.45), channel_id=1, source_target_pairs={{0,2},{1,3},{2,0},{3,1},{4,6},{5,7},{6,4},{7,5},{8,10},{9,11},{10,... | collective-permute-start | bytes 208904 | tf_op jit(solution)/shard_map/ppermute | solution.py:199
  77.2 6.4 %collective-permute-start.24 = (s16[272,128]{1,0:T(8,128)(2,1)S(1)}, s16[272,128]{1,0:T(8,128)(2,1)S(1)}, u32[]{:S(2)}, u32[]{:S(2)}) collective-permute-start(s16[272,128]{1,0:T(8,128)(2,1)S(1)} %get-tuple-element.46), channel_id=1, source_target_pairs={{0,3},{1,0},{2,1},{3,2},{4,7},{5,4},{6,5},{7,6},{8,11},{9,8},{10,9... | collective-permute-start | bytes 208904 | tf_op jit(solution)/shard_map/ppermute | solution.py:199
  86.9 5.2 %collective-permute-start.27 = (s16[272,128]{1,0:T(8,128)(2,1)}, s16[272,128]{1,0:T(8,128)(2,1)S(1)}, u32[]{:S(2)}, u32[]{:S(2)}) collective-permute-start(s16[272,128]{1,0:T(8,128)(2,1)} %solve.3.refs_0_), channel_id=1, source_target_pairs={{0,3},{1,0},{2,1},{3,2},{4,7},{5,4},{6,5},{7,6},{8,11},{9,8},{10,9... | collective-permute-start | bytes 208904 | tf_op jit(solution)/shard_map/ppermute | solution.py:199
  89.1 7.2 %collective-permute-start.26 = (s16[272,128]{1,0:T(8,128)(2,1)}, s16[272,128]{1,0:T(8,128)(2,1)S(1)}, u32[]{:S(2)}, u32[]{:S(2)}) collective-permute-start(s16[272,128]{1,0:T(8,128)(2,1)} %solve.3.refs_0_), channel_id=1, source_target_pairs={{0,2},{1,3},{2,0},{3,1},{4,6},{5,7},{6,4},{7,5},{8,10},{9,11},{10,... | collective-permute-start | bytes 208904 | tf_op jit(solution)/shard_map/ppermute | solution.py:199
  89.7 6.7 %collective-permute-start.25 = (s16[272,128]{1,0:T(8,128)(2,1)}, s16[272,128]{1,0:T(8,128)(2,1)S(1)}, u32[]{:S(2)}, u32[]{:S(2)}) collective-permute-start(s16[272,128]{1,0:T(8,128)(2,1)} %solve.3.refs_0_), channel_id=1, source_target_pairs={{0,1},{1,2},{2,3},{3,0},{4,5},{5,6},{6,7},{7,4},{8,9},{9,10},{10,1... | collective-permute-start | bytes 208904 | tf_op jit(solution)/shard_map/ppermute | solution.py:199
  (22 other events, 58.6 us)

commit v2 on v1

v2 whole, which is shorter than its diff:
```python
import functools

import jax
import jax.numpy as jnp
from jax import lax
from jax.experimental import pallas as pl
from jax.experimental.pallas import tpu as pltpu
from jax.sharding import PartitionSpec as P

F32, BF16, I32, I16 = jnp.float32, jnp.bfloat16, jnp.int32, jnp.int16
VMEM = pl.BlockSpec(memory_space=pltpu.VMEM)
SMEM = pl.BlockSpec(memory_space=pltpu.SMEM)
HBM = pl.BlockSpec(memory_space=pltpu.HBM)
PARAMS = pltpu.CompilerParams(vmem_limit_bytes=16 * 2**20)
STEPS = 128.0
TAIL = 16
LANES = 128


def encode_blocks(values, msg_ref, probes):
    rows = lax.broadcasted_iota(I32, (TAIL, msg_ref.shape[1]), 0)
    tail = jnp.zeros((TAIL, msg_ref.shape[1]), F32)
    for k, value in enumerate(values):
        peak = jnp.maximum(jnp.max(jnp.abs(value), keepdims=True), 2.0**-100)
        level = jnp.ceil(jnp.log2(peak) * STEPS)
        scaled = jnp.round(value * jnp.exp2(15.0 - level * (1.0 / STEPS)))
        scaled = jnp.clip(scaled, -32767.0, 32767.0)
        msg_ref[k * probes : (k + 1) * probes] = scaled.astype(I32).astype(I16)
        tail = jnp.where(rows == k, level, tail)
    msg_ref[len(values) * probes :] = tail.astype(I32).astype(I16)


def decode_blocks(msg_ref, count, probes):
    tail = msg_ref[count * probes :].astype(I32).astype(F32)
    factor = jnp.exp2(tail * (1.0 / STEPS) - 15.0)
    return [
        msg_ref[k * probes : (k + 1) * probes].astype(I32).astype(F32) * factor[k : k + 1]
        for k in range(count)
    ]


def log2(n):
    return n.bit_length() - 1


def lanes_like(shape, dim):
    return lax.broadcasted_iota(I32, shape, dim)


def table_at(refs, me, prior_dev, half):
    owner = lax.shift_right_logical(refs, log2(prior_dev)) ^ me
    group = (owner & 1) * half + lax.shift_right_logical(owner, 1)
    return group * prior_dev + (refs & (prior_dev - 1))


def spread(values, rows_dev):
    repeat = (lanes_like((rows_dev, LANES), 1) & (rows_dev - 1)) == lanes_like((rows_dev, LANES), 0)
    return jnp.dot(
        values.astype(F32).astype(BF16), repeat.astype(F32).astype(BF16), preferred_element_type=F32
    )


def start_kernel(groups, colidx_ref, live_ref, prior_ref, msg_ref, first_ref, alive_ref, rows):
    slots, _, rows_dev = colidx_ref.shape
    prior_dev, probes, _ = prior_ref.shape
    for k in range(prior_dev):
        msg_ref[k * probes : (k + 1) * probes] = prior_ref[k]
    rows[...] = jnp.zeros(rows.shape, I32)
    for j in range(slots):
        rows[j : j + 1] = colidx_ref[j, 0:1]
        rows[8 + j : 9 + j] = lax.shift_right_logical(colidx_ref[j, 1:2], 4)
        rows[16 + j : 17 + j] = colidx_ref[j, 1:2] & 15
        rows[24 + j : 25 + j] = lax.shift_right_logical(colidx_ref[j, 0:1], 4)
        rows[32 + j : 33 + j] = colidx_ref[j, 0:1] & 15
    rows[40:42] = live_ref[...]
    wide = spread(rows[...], rows_dev)
    msg_ref[prior_dev * probes :] = wide[8:24].astype(BF16)
    me, here = lax.axis_index("rows"), lax.axis_index("cols")
    ids = here * slots + lanes_like((8, LANES), 0)
    refs = (wide[24:32] * 16.0 + wide[32:40]).astype(I32)
    live = wide[40:48].astype(I32)
    found = table_at(refs, me, prior_dev, groups // 2)
    first_ref[...] = jnp.where(ids < live[0:1], found, groups * prior_dev)
    alive_ref[...] = (ids < live[1:2]).astype(I32)


def start(groups, colidx, live, prior):
    rows_dev, slots = colidx.shape[1:]
    prior_dev, probes, order = prior.shape
    table = jax.ShapeDtypeStruct((8, LANES), I32)
    return pl.pallas_call(
        functools.partial(start_kernel, groups),
        out_shape=[jax.ShapeDtypeStruct((prior_dev * probes + TAIL, order), BF16), table, table],
        in_specs=[VMEM] * 3,
        out_specs=[VMEM] * 3,
        scratch_shapes=[pltpu.VMEM((48, rows_dev), I32)],
        compiler_params=PARAMS,
        name="start",
    )(jnp.transpose(colidx, (2, 0, 1)), live, prior)


def ranks(mask, within, slots):
    ones = mask.astype(F32).astype(BF16)
    before = jnp.dot(ones, within[0], preferred_element_type=F32)
    count = jnp.dot(ones, within[1], preferred_element_type=F32)
    above = jnp.zeros((1, LANES), F32)
    rows = lanes_like((8, LANES), 0)
    for j in range(slots):
        before = jnp.where(rows == j, before + above, before)
        above = above + count[j : j + 1]
    return before


def route_kernel(groups, cap, slots, prior_dev, owner_ref, alive_ref, *refs):
    tails, want_ref, second_ref = refs[:groups], refs[groups], refs[groups + 1]
    rows_front = owner_ref.shape[1]
    rows_dev = rows_front // groups
    half = groups // 2
    prior_count = groups * prior_dev
    me = lax.axis_index("rows")
    per = LANES // rows_dev
    lane = lanes_like((8, LANES), 1)
    group_of = lax.shift_right_logical(lane, log2(rows_dev))
    a, b = lanes_like((LANES, LANES), 0), lanes_like((LANES, LANES), 1)
    together = lax.shift_right_logical(a, log2(rows_dev)) == lax.shift_right_logical(b, log2(rows_dev))
    alike = (a & (rows_dev - 1)) == (b & (rows_dev - 1))
    as_bf16 = lambda x: x.astype(F32).astype(BF16)
    within = (as_bf16(together & (a < b)), as_bf16(together))

    def referred(g):
        tail = tails[g][tails[g].shape[0] - TAIL :].astype(F32)
        return (tail[:8] * 16.0 + tail[8:]).astype(I32)

    want_ref[...] = jnp.zeros(want_ref.shape, I32)
    for block in range(groups // per):
        named = referred(block * per)
        for g in range(1, per):
            named = jnp.where(group_of == g, referred(block * per + g), named)
        spot = jnp.full((8, LANES), -1, I32)
        for t in range(rows_dev):
            spot = jnp.where(named == prior_count + owner_ref[0, me * rows_dev + t], t, spot)
        mine = spot >= 0
        rank = ranks(mine, within, slots).astype(I32)
        for q in range(cap):
            held = jnp.where(mine & (rank == q), spot, 0).astype(F32).astype(BF16)
            total = jnp.dot(held, within[1], preferred_element_type=F32)
            want_ref[q : q + 1, block * LANES : (block + 1) * LANES] = jnp.sum(
                total, axis=0, keepdims=True
            ).astype(I32)

    own = referred(0)
    recent = own >= prior_count
    spot = jnp.zeros((8, LANES), I32)
    for t in range(rows_front):
        spot = jnp.where(own == prior_count + owner_ref[0, t], t, spot)
    holder = lax.shift_right_logical(spot, log2(rows_dev)) ^ me
    group = (holder & 1) * half + lax.shift_right_logical(holder, 1)
    rank = jnp.zeros((8, LANES), F32)
    for block in range(groups // per):
        mask = recent & (group == group_of + block * per)
        found = jnp.where(mask, ranks(mask, within, slots), 0.0)
        rank = rank + jnp.dot(found.astype(BF16), as_bf16(alike), preferred_element_type=F32)
    at = jnp.where(
        recent,
        prior_count + group * cap + rank.astype(I32),
        table_at(own, me, prior_dev, half),
    )
    second_ref[...] = jnp.where(alive_ref[...] > 0, at, prior_count + groups * cap)


def route(groups, cap, slots, prior_dev, owner_map, alive, pieces):
    rows_dev = owner_map.shape[1] // groups
    return pl.pallas_call(
        functools.partial(route_kernel, groups, cap, slots, prior_dev),
        out_shape=[
            jax.ShapeDtypeStruct((-(-cap // 8) * 8, groups * rows_dev), I32),
            jax.ShapeDtypeStruct((8, LANES), I32),
        ],
        in_specs=[SMEM] + [VMEM] * (groups + 1),
        out_specs=[VMEM] * 2,
        compiler_params=PARAMS,
        name="route",
    )(owner_map, alive, *pieces)


def load_kernel(blocks, right_side, inverse, *refs):
    outs, sems = refs[:-1], refs[-1]
    part = outs[2].shape[1]
    first = lax.axis_index("cols") * part
    sources = [
        blocks.at[0],
        blocks.at[1],
        right_side.at[:, pl.ds(first, part)],
        inverse.at[:, pl.ds(first, part)],
    ]
    copies = [pltpu.make_async_copy(a, b, sems.at[i]) for i, (a, b) in enumerate(zip(sources, outs))]
    for copy in copies:
        copy.start()
    for copy in copies:
        copy.wait()


def load(cols, blocks, right_side, inverse):
    part = blocks.shape[1] // cols
    shapes = [blocks.shape[1:]] * 2
    shapes += [a.shape[:1] + (part,) + a.shape[2:] for a in (right_side, inverse)]
    kinds = [BF16, BF16, F32, F32]
    return pl.pallas_call(
        load_kernel,
        out_shape=[pltpu.VMEM(a, b) for a, b in zip(shapes, kinds)],
        in_specs=[HBM] * 3,
        out_specs=[VMEM] * 4,
        scratch_shapes=[pltpu.SemaphoreType.DMA((4,))],
        compiler_params=PARAMS,
        name="load",
    )(*(pltpu.with_memory_space_constraint(x, pltpu.HBM) for x in (blocks, right_side, inverse)))


def partial_kernel(cols, n_early, probes, idx_ref, blk, *refs):
    ins, own_ref, msgs, known = refs[:-cols - 1], refs[-cols - 1], refs[-cols:-1], refs[-1]
    rows_dev, slots, order, _ = blk.shape
    part = rows_dev // cols
    here = lax.axis_index("cols")
    at = 0
    for i, ref in enumerate(ins):
        for k in range((ref.shape[0] - (TAIL if i < n_early else 0)) // probes):
            known[at] = ref[k * probes : (k + 1) * probes]
            at += 1
    known[at] = jnp.zeros(known.shape[1:], known.dtype)
    for s in list(range(1, cols)) + [0]:
        first = lax.rem(here + s, cols) * part
        sums = []
        for k in range(part):
            xs = [known[idx_ref[j, first + k]] for j in range(slots)]
            ws = [blk[first + k, j] for j in range(slots)]
            sums.append(
                lax.dot_general(
                    jnp.concatenate(xs, axis=1),
                    jnp.concatenate(ws, axis=1),
                    (((1,), (1,)), ((), ())),
                    preferred_element_type=F32,
                )
            )
        if s == 0:
            for k in range(part):
                own_ref[k] = sums[k]
        else:
            encode_blocks(sums, msgs[s - 1], probes)


def partial_products(name, cols, probes, idx, blocks, early, recent):
    rows_dev, slots, order, _ = blocks.shape
    part = rows_dev // cols
    rows = sum(a.shape[0] - TAIL for a in early) + sum(a.shape[0] for a in recent)
    msg = jax.ShapeDtypeStruct((part * probes + TAIL, order), I16)
    out = pl.pallas_call(
        functools.partial(partial_kernel, cols, len(early), probes),
        out_shape=[jax.ShapeDtypeStruct((part, probes, order), F32)] + [msg] * (cols - 1),
        in_specs=[SMEM] + [VMEM] * (len(early) + len(recent) + 1),
        out_specs=[VMEM] * cols,
        scratch_shapes=[pltpu.VMEM((rows // probes + 1, probes, order), BF16)],
        compiler_params=PARAMS,
        name=name,
    )(idx, blocks, *early, *recent)
    return out[0], out[1:]


def solve_kernel(front, cols, own_ref, *refs):
    msgs, rhs_ref, inv_ref, out_ref = refs[: cols - 1], refs[cols - 1], refs[cols], refs[cols + 1]
    part, probes, _ = own_ref.shape
    total = [own_ref[k] for k in range(part)]
    for msg in msgs:
        total = [a + b for a, b in zip(total, decode_blocks(msg, part, probes))]
    solved = [
        lax.dot_general(
            rhs_ref[front, k] - total[k],
            inv_ref[front, k],
            (((1,), (1,)), ((), ())),
            precision=lax.Precision.HIGHEST,
            preferred_element_type=F32,
        )
        for k in range(part)
    ]
    encode_blocks(solved, out_ref, probes)


def solve_part(front, cols, own, msgs, rhs, inverse):
    part, probes, order = own.shape
    return pl.pallas_call(
        functools.partial(solve_kernel, front, cols),
        out_shape=jax.ShapeDtypeStruct((part * probes + TAIL, order), I16),
        in_specs=[VMEM] * (cols + 2),
        out_specs=VMEM,
        compiler_params=PARAMS,
        name=f"solve_{front}",
    )(own, *msgs, rhs, inverse)


def pack_kernel(cols, groups, cap, sel_ref, *refs):
    msgs, sends, rows = refs[:cols], refs[cols:-1], refs[-1]
    rows_dev, probes, _ = rows.shape
    part = rows_dev // cols
    here = lax.axis_index("cols")
    for s in range(cols):
        first = lax.rem(here + cols - s, cols) * part
        for k, value in enumerate(decode_blocks(msgs[s], part, probes)):
            rows[first + k] = value.astype(BF16)
    for m in range(groups):
        for q in range(cap):
            sends[m][q * probes : (q + 1) * probes] = rows[sel_ref[q, m * rows_dev]]


def pack(cols, groups, cap, sel, msgs, shape):
    rows_dev, probes, order = shape
    return pl.pallas_call(
        functools.partial(pack_kernel, cols, groups, cap),
        out_shape=[jax.ShapeDtypeStruct((cap * probes, order), BF16)] * groups,
        in_specs=[SMEM] + [VMEM] * cols,
        out_specs=[VMEM] * groups,
        scratch_shapes=[pltpu.VMEM((rows_dev, probes, order), BF16)],
        compiler_params=PARAMS,
        name="pack",
    )(sel, *msgs)


def unpack_kernel(front, cols, *refs):
    msgs, out_ref, rows, sems = refs[:cols], refs[-3], refs[-2], refs[-1]
    part, probes, _ = rows.shape[1:]
    here = lax.axis_index("cols")
    copies = []
    for s in range(cols):
        first = lax.rem(here + cols - s, cols) * part
        for k, value in enumerate(decode_blocks(msgs[s], part, probes)):
            rows[s, k] = value
        copy = pltpu.make_async_copy(rows.at[s], out_ref.at[front, pl.ds(first, part)], sems.at[s])
        copy.start()
        copies.append(copy)
    for copy in copies:
        copy.wait()


def unpack(front, cols, msgs, shape, base=None):
    _, rows_dev, probes, order = shape
    rest = [] if base is None else [base]
    return pl.pallas_call(
        functools.partial(unpack_kernel, front, cols),
        out_shape=jax.ShapeDtypeStruct(shape, F32),
        in_specs=[VMEM] * cols + [HBM] * len(rest),
        out_specs=HBM,
        input_output_aliases={} if base is None else {cols: 0},
        scratch_shapes=[
            pltpu.VMEM((cols, rows_dev // cols, probes, order), F32),
            pltpu.SemaphoreType.DMA((cols,)),
        ],
        compiler_params=PARAMS,
        name=f"unpack_{front}",
    )(*msgs, *rest)


def shards(groups, cols, owner_map, colidx, live, blocks, diag_inverse, right_side, prior):
    _, rows_dev, slots, order, _ = blocks.shape
    probes = right_side.shape[2]
    prior_dev = prior.shape[0]
    half = groups // 2
    cap = -(-((slots + 1) // 2) * rows_dev // groups)
    def over_rows(x, mask):
        return lax.ppermute(x, "rows", [(i, i ^ mask) for i in range(groups)])

    def over_cols(x, step):
        return lax.ppermute(x, "cols", [(i, (i + step) % cols) for i in range(cols)])

    own, first_at, alive = start(groups, colidx, live, prior)
    pieces = [own] + [over_rows(own, 2 * k) for k in range(1, half)]
    pieces += [over_rows(x, 1) for x in pieces]
    blocks0, blocks1, rhs, inverse = load(cols, blocks, right_side, diag_inverse)
    want, second_at = route(groups, cap, slots, prior_dev, owner_map, alive, pieces)

    own0, msgs0 = partial_products("partial_0", cols, probes, first_at, blocks0, pieces, [])
    got0 = [over_cols(m, s + 1) for s, m in enumerate(msgs0)]
    coded0 = solve_part(0, cols, own0, got0, rhs, inverse)
    all0 = [coded0] + [over_cols(coded0, s) for s in range(1, cols)]

    sends = pack(cols, groups, cap, want, all0, right_side.shape[1:])
    masks = [2 * k for k in range(half)] + [2 * k + 1 for k in range(half)]
    recent = [x if m == 0 else over_rows(x, m) for m, x in zip(masks, sends)]
    solved = unpack(0, cols, all0, right_side.shape)

    own1, msgs1 = partial_products("partial_1", cols, probes, second_at, blocks1, pieces, recent)
    got1 = [over_cols(m, s + 1) for s, m in enumerate(msgs1)]
    coded1 = solve_part(1, cols, own1, got1, rhs, inverse)
    all1 = [coded1] + [over_cols(coded1, s) for s in range(1, cols)]
    return unpack(1, cols, all1, right_side.shape, solved)


def solution(mesh):
    placed = (
        P(),
        P(None, "rows", "cols"),
        P(None, "rows"),
        P(None, "rows", "cols", None, None),
        P(None, "rows", None, None),
        P(None, "rows", None, None),
        P("rows", None, None),
    )
    body = functools.partial(shards, mesh.shape["rows"], mesh.shape["cols"])
    return jax.shard_map(
        body, mesh=mesh, in_specs=placed, out_specs=P(None, "rows", None, None), check_vma=False
    )
```

time: 99.7 us -> 73.1 us (0.73)
  local copies, waits for them, and re-layouts: 16.9 us -> 2.28 us
  waiting for transfers between devices: 35 us -> 30 us
  Pallas kernels: 15.3 us -> 11.8 us
  other arithmetic: 3.28 us -> 0 us
    unnamed x38 -> x8, local copies, waits for them, and re-layouts: 11 us -> 2.28 us
    ppermute x12, waiting for transfers between devices: 20.2 us -> 15.6 us  [over_cols(): lax.ppermute(x, 'cols', [(i, (i + step) % cols) for i in range(cols)])]
    squeeze x2 -> x0, local copies, waits for them, and re-layouts: 3.56 us -> none  [shards(): coded1 = solve_part(cols, own1, got1, rhs_part[1], inv_part[1])]
    ppermute x12, starting transfers between devices: 15.6 us -> 18.3 us  [over_cols(): lax.ppermute(x, 'cols', [(i, (i + step) % cols) for i in range(cols)])]
    ppermute x16 -> x14, starting transfers between devices: 12.9 us -> 10.4 us  [over_rows(): return lax.ppermute(x, 'rows', [(i, i ^ mask) for i in range(groups)])]
    pallas_call x5 -> x9, Pallas kernels: 13.1 us -> 11 us  [the longest x2 3.73 us: partial_products(): pl.pallas_call(functools.partial(partial_kernel, cols, len(early), probes...]
    pallas_call x1, Pallas kernels: 2.19 us -> 0.72 us  [pack(): pl.pallas_call(functools.partial(pack_kernel, cols, groups, cap), out_sha...]
    ppermute x16 -> x14, waiting for transfers between devices: 14.8 us -> 14.5 us  [over_rows(): return lax.ppermute(x, 'rows', [(i, i ^ mask) for i in range(groups)])]
  transfers between devices with their start and end apart: 28 -> 26, of which waited for: 17 -> 17; matrix products, arithmetic and copies ran while one was open for 9% -> 0% of each run, Pallas kernels for 0% -> 7%
where the time goes in v2:
time: 73.1 us; the launch traced here: 72.9 us
  waiting for transfers between devices  30 us (41%)
  starting transfers between devices  28.7 us (39%)
  Pallas kernels  11.8 us (16%)
  local copies, waits for them, and re-layouts  2.28 us (3%)
    ppermute x12, starting transfers between devices, over_cols(): lax.ppermute(x, 'cols', [(i, (i + step) % cols) for i in range(cols)])  18.3 us
    ppermute x12, waiting for transfers between devices, over_cols(): lax.ppermute(x, 'cols', [(i, (i + step) % cols) for i in range(cols)])  15.6 us
    ppermute x14, waiting for transfers between devices, over_rows(): return lax.ppermute(x, 'rows', [(i, i ^ mask) for i in range(groups)])  14.5 us
    ppermute x14, starting transfers between devices, over_rows(): return lax.ppermute(x, 'rows', [(i, i ^ mask) for i in range(groups)])  10.4 us
    pallas_call x2, Pallas kernels, partial_products(): pl.pallas_call(functools.partial(partial_kernel, cols, len(early), probes...  3.73 us
    pallas_call x1, Pallas kernels, load(): pl.pallas_call(load_kernel, out_shape=[pltpu.VMEM(a, b) for a, b in zip(s...  3 us
    unnamed x8, local copies, waits for them, and re-layouts  2.28 us
    pallas_call x2, Pallas kernels, unpack(): pl.pallas_call(functools.partial(unpack_kernel, front, cols), out_shape=j...  1.68 us
  transfers between devices with their start and end apart: 26, of which 17 were waited for; matrix products, arithmetic and copies ran while one was open for 0% of the time, Pallas kernels for 7%

profile of v2, /device:TPU:0, one launch (start us, length us, event | category | flops | bytes accessed | tf_op | source)
XLA Modules:
  0.0 72.9 jit_solution(7956625595669054591)
XLA Ops:
  2.4 3.0 %collective-permute-start = (bf16[528,128]{1,0:T(8,128)(2,1)S(1)}, bf16[528,128]{1,0:T(8,128)(2,1)S(1)}, u32[]{:S(2)}, u32[]{:S(2)}) collective-permute-start(bf16[528,128]{1,0:T(8,128)(2,1)S(1)} %get-tuple-element.31.refs_0_), channel_id=1, source_target_pairs={{0,8},{4,12},{8,0},{12,4},{16,24},{20,28},{24,16},{28,20},{1,9},{5... | collective-permute-start | bytes 405512 | tf_op jit(solution)/shard_map/ppermute | solution.py:367
  5.4 1.5 %collective-permute-start.1 = (bf16[528,128]{1,0:T(8,128)(2,1)S(1)}, bf16[528,128]{1,0:T(8,128)(2,1)S(1)}, u32[]{:S(2)}, u32[]{:S(2)}) collective-permute-start(bf16[528,128]{1,0:T(8,128)(2,1)S(1)} %get-tuple-element.31.refs_0_), channel_id=1, source_target_pairs={{0,16},{4,20},{8,24},{12,28},{16,0},{20,4},{24,8},{28,12},{1,17},{... | collective-permute-start | bytes 405512 | tf_op jit(solution)/shard_map/ppermute | solution.py:367
  7.0 2.4 %collective-permute-done.refs_1_ = bf16[528,128]{1,0:T(8,128)(2,1)S(1)} collective-permute-done((bf16[528,128]{1,0:T(8,128)(2,1)S(1)}, bf16[528,128]{1,0:T(8,128)(2,1)S(1)}, u32[]{:S(2)}, u32[]{:S(2)}) %collective-permute-start) | collective-permute-done | bytes 135200 | tf_op jit(solution)/shard_map/ppermute | solution.py:367
  9.4 3.9 %collective-permute-done.1.refs_2_ = bf16[528,128]{1,0:T(8,128)(2,1)S(1)} collective-permute-done((bf16[528,128]{1,0:T(8,128)(2,1)S(1)}, bf16[528,128]{1,0:T(8,128)(2,1)S(1)}, u32[]{:S(2)}, u32[]{:S(2)}) %collective-permute-start.1) | collective-permute-done | bytes 135200 | tf_op jit(solution)/shard_map/ppermute | solution.py:367
  13.9 3.0 %load.1 = (bf16[16,6,128,128]{3,2,1,0:T(8,128)(2,1)S(1)}, bf16[16,6,128,128]{3,2,1,0:T(8,128)(2,1)S(1)}, f32[2,4,64,128]{3,2,1,0:T(8,128)S(1)}, f32[2,4,128,128]{3,2,1,0:T(8,128)S(1)}) custom-call(bf16[2,16,6,128,128]{4,3,2,1,0:T(8,128)(2,1)} %blocks.1, f32[2,16,64,128]{3,2,1,0:T(8,128)} %right_side.1, f32[2,16,128,128]{3,2,1,0:T(8,128)} %inverse.1), custom_call_target="tpu_custom_call" | custom-call | tf_op jit(solution)/shard_map/load/pallas_call | solution.py:208
  16.9 1.8 %partial_0.1 = (f32[4,64,128]{2,1,0:T(8,128)S(1)}, s16[272,128]{1,0:T(8,128)(2,1)S(1)}, s16[272,128]{1,0:T(8,128)(2,1)S(1)}, s16[272,128]{1,0:T(8,128)(2,1)S(1)}) custom-call(s32[8,128]{1,0:T(8,128)S(1)} %get-tuple-element.35.idx_ref, bf16[16,6,128,128]{3,2,1,0:T(8,128)(2,1)S(1)} %get-tuple-element.36.blk, bf16[528,128]{1,0:T(8,128)(2,1)S(1)} %get-tuple-element.31.refs_0_, ...), custom_call_target="tpu_custom_call" | custom-call | tf_op jit(solution)/shard_map/partial_0/pallas_call | solution.py:256
  18.8 1.6 %collective-permute-start.7 = (s16[272,128]{1,0:T(8,128)(2,1)S(1)}, s16[272,128]{1,0:T(8,128)(2,1)S(1)}, u32[]{:S(2)}, u32[]{:S(2)}) collective-permute-start(s16[272,128]{1,0:T(8,128)(2,1)S(1)} %get-tuple-element.38), channel_id=1, source_target_pairs={{0,1},{1,2},{2,3},{3,0},{4,5},{5,6},{6,7},{7,4},{8,9},{9,10},{10,1... | collective-permute-start | bytes 208904 | tf_op jit(solution)/shard_map/ppermute | solution.py:370
  20.4 2.6 %collective-permute-start.8 = (s16[272,128]{1,0:T(8,128)(2,1)S(1)}, s16[272,128]{1,0:T(8,128)(2,1)S(1)}, u32[]{:S(2)}, u32[]{:S(2)}) collective-permute-start(s16[272,128]{1,0:T(8,128)(2,1)S(1)} %get-tuple-element.39), channel_id=1, source_target_pairs={{0,2},{1,3},{2,0},{3,1},{4,6},{5,7},{6,4},{7,5},{8,10},{9,11},{10,... | collective-permute-start | bytes 208904 | tf_op jit(solution)/shard_map/ppermute | solution.py:370
  25.3 2.6 %collective-permute-done.8.refs_1_ = s16[272,128]{1,0:T(8,128)(2,1)S(1)} collective-permute-done((s16[272,128]{1,0:T(8,128)(2,1)S(1)}, s16[272,128]{1,0:T(8,128)(2,1)S(1)}, u32[]{:S(2)}, u32[]{:S(2)}) %collective-permute-start.8) | collective-permute-done | bytes 69664 | tf_op jit(solution)/shard_map/ppermute | solution.py:370
  28.9 1.8 %collective-permute-start.10 = (s16[272,128]{1,0:T(8,128)(2,1)S(1)}, s16[272,128]{1,0:T(8,128)(2,1)S(1)}, u32[]{:S(2)}, u32[]{:S(2)}) collective-permute-start(s16[272,128]{1,0:T(8,128)(2,1)S(1)} %solve_0.1.refs_0_), channel_id=1, source_target_pairs={{0,1},{1,2},{2,3},{3,0},{4,5},{5,6},{6,7},{7,4},{8,9},{9,10},{10,1... | collective-permute-start | bytes 208904 | tf_op jit(solution)/shard_map/ppermute | solution.py:370
  30.6 1.8 %collective-permute-start.11 = (s16[272,128]{1,0:T(8,128)(2,1)S(1)}, s16[272,128]{1,0:T(8,128)(2,1)S(1)}, u32[]{:S(2)}, u32[]{:S(2)}) collective-permute-start(s16[272,128]{1,0:T(8,128)(2,1)S(1)} %solve_0.1.refs_0_), channel_id=1, source_target_pairs={{0,2},{1,3},{2,0},{3,1},{4,6},{5,7},{6,4},{7,5},{8,10},{9,11},{10,... | collective-permute-start | bytes 208904 | tf_op jit(solution)/shard_map/ppermute | solution.py:370
  35.4 2.1 %collective-permute-done.11.refs_2_ = s16[272,128]{1,0:T(8,128)(2,1)S(1)} collective-permute-done((s16[272,128]{1,0:T(8,128)(2,1)S(1)}, s16[272,128]{1,0:T(8,128)(2,1)S(1)}, u32[]{:S(2)}, u32[]{:S(2)}) %collective-permute-start.11) | collective-permute-done | bytes 69664 | tf_op jit(solution)/shard_map/ppermute | solution.py:370
  40.6 1.4 %collective-permute-start.15 = (bf16[384,128]{1,0:T(8,128)(2,1)S(1)}, bf16[384,128]{1,0:T(8,128)(2,1)S(1)}, u32[]{:S(2)}, u32[]{:S(2)}) collective-permute-start(bf16[384,128]{1,0:T(8,128)(2,1)S(1)} %get-tuple-element.46), channel_id=1, source_target_pairs={{0,24},{4,28},{8,16},{12,20},{16,8},{20,12},{24,0},{28,4},{1,25},{... | collective-permute-start | bytes 294920 | tf_op jit(solution)/shard_map/ppermute | solution.py:367
  43.8 2.6 %collective-permute-done.14.refs_10_ = bf16[384,128]{1,0:T(8,128)(2,1)S(1)} collective-permute-done((bf16[384,128]{1,0:T(8,128)(2,1)S(1)}, bf16[384,128]{1,0:T(8,128)(2,1)S(1)}, u32[]{:S(2)}, u32[]{:S(2)}) %collective-permute-start.14) | collective-permute-done | bytes 98336 | tf_op jit(solution)/shard_map/ppermute | solution.py:367
  47.9 4.0 %collective-permute-done.19.refs_15_ = bf16[384,128]{1,0:T(8,128)(2,1)S(1)} collective-permute-done((bf16[384,128]{1,0:T(8,128)(2,1)S(1)}, bf16[384,128]{1,0:T(8,128)(2,1)S(1)}, u32[]{:S(2)}, u32[]{:S(2)}) %collective-permute-start.19) | collective-permute-done | bytes 98336 | tf_op jit(solution)/shard_map/ppermute | solution.py:367
  51.9 1.9 %partial_1.1 = (f32[4,64,128]{2,1,0:T(8,128)S(1)}, s16[272,128]{1,0:T(8,128)(2,1)S(1)}, s16[272,128]{1,0:T(8,128)(2,1)S(1)}, s16[272,128]{1,0:T(8,128)(2,1)S(1)}) custom-call(s32[8,128]{1,0:T(8,128)S(1)} %get-tuple-element.32.idx_ref, bf16[16,6,128,128]{3,2,1,0:T(8,128)(2,1)S(1)} %get-tuple-element.33.blk, bf16[528,128]{1,0:T(8,128)(2,1)S(1)} %get-tuple-element.31.refs_0_, ...), custom_call_target="tpu_custom_call" | custom-call | tf_op jit(solution)/shard_map/partial_1/pallas_call | solution.py:256
  53.7 1.7 %collective-permute-start.20 = (s16[272,128]{1,0:T(8,128)(2,1)S(1)}, s16[272,128]{1,0:T(8,128)(2,1)S(1)}, u32[]{:S(2)}, u32[]{:S(2)}) collective-permute-start(s16[272,128]{1,0:T(8,128)(2,1)S(1)} %get-tuple-element.52), channel_id=1, source_target_pairs={{0,1},{1,2},{2,3},{3,0},{4,5},{5,6},{6,7},{7,4},{8,9},{9,10},{10,1... | collective-permute-start | bytes 208904 | tf_op jit(solution)/shard_map/ppermute | solution.py:370
  55.9 2.0 %collective-permute-start.22 = (s16[272,128]{1,0:T(8,128)(2,1)S(1)}, s16[272,128]{1,0:T(8,128)(2,1)S(1)}, u32[]{:S(2)}, u32[]{:S(2)}) collective-permute-start(s16[272,128]{1,0:T(8,128)(2,1)S(1)} %get-tuple-element.54), channel_id=1, source_target_pairs={{0,3},{1,0},{2,1},{3,2},{4,7},{5,4},{6,5},{7,6},{8,11},{9,8},{10,9... | collective-permute-start | bytes 208904 | tf_op jit(solution)/shard_map/ppermute | solution.py:370
  57.9 2.8 %collective-permute-done.20.refs_0_ = s16[272,128]{1,0:T(8,128)(2,1)S(1)} collective-permute-done((s16[272,128]{1,0:T(8,128)(2,1)S(1)}, s16[272,128]{1,0:T(8,128)(2,1)S(1)}, u32[]{:S(2)}, u32[]{:S(2)}) %collective-permute-start.20) | collective-permute-done | bytes 69664 | tf_op jit(solution)/shard_map/ppermute | solution.py:370
  60.7 1.8 %collective-permute-done.21.refs_1_ = s16[272,128]{1,0:T(8,128)(2,1)S(1)} collective-permute-done((s16[272,128]{1,0:T(8,128)(2,1)S(1)}, s16[272,128]{1,0:T(8,128)(2,1)S(1)}, u32[]{:S(2)}, u32[]{:S(2)}) %collective-permute-start.21) | collective-permute-done | bytes 69664 | tf_op jit(solution)/shard_map/ppermute | solution.py:370
  63.3 1.9 %collective-permute-start.23 = (s16[272,128]{1,0:T(8,128)(2,1)S(1)}, s16[272,128]{1,0:T(8,128)(2,1)S(1)}, u32[]{:S(2)}, u32[]{:S(2)}) collective-permute-start(s16[272,128]{1,0:T(8,128)(2,1)S(1)} %solve_1.1.refs_0_), channel_id=1, source_target_pairs={{0,1},{1,2},{2,3},{3,0},{4,5},{5,6},{6,7},{7,4},{8,9},{9,10},{10,1... | collective-permute-start | bytes 208904 | tf_op jit(solution)/shard_map/ppermute | solution.py:370
  66.0 1.7 %collective-permute-start.25 = (s16[272,128]{1,0:T(8,128)(2,1)S(1)}, s16[272,128]{1,0:T(8,128)(2,1)S(1)}, u32[]{:S(2)}, u32[]{:S(2)}) collective-permute-start(s16[272,128]{1,0:T(8,128)(2,1)S(1)} %solve_1.1.refs_0_), channel_id=1, source_target_pairs={{0,3},{1,0},{2,1},{3,2},{4,7},{5,4},{6,5},{7,6},{8,11},{9,8},{10,9... | collective-permute-start | bytes 208904 | tf_op jit(solution)/shard_map/ppermute | solution.py:370
  68.5 1.4 %collective-permute-done.23.refs_1_ = s16[272,128]{1,0:T(8,128)(2,1)S(1)} collective-permute-done((s16[272,128]{1,0:T(8,128)(2,1)S(1)}, s16[272,128]{1,0:T(8,128)(2,1)S(1)}, u32[]{:S(2)}, u32[]{:S(2)}) %collective-permute-start.23) | collective-permute-done | bytes 69664 | tf_op jit(solution)/shard_map/ppermute | solution.py:370
  70.0 2.1 %collective-permute-done.24.refs_2_ = s16[272,128]{1,0:T(8,128)(2,1)S(1)} collective-permute-done((s16[272,128]{1,0:T(8,128)(2,1)S(1)}, s16[272,128]{1,0:T(8,128)(2,1)S(1)}, u32[]{:S(2)}, u32[]{:S(2)}) %collective-permute-start.24) | collective-permute-done | bytes 69664 | tf_op jit(solution)/shard_map/ppermute | solution.py:370
  (46 shorter events, 19.2 us)
Async XLA Ops:
  2.4 7.0 %collective-permute-start = (bf16[528,128]{1,0:T(8,128)(2,1)S(1)}, bf16[528,128]{1,0:T(8,128)(2,1)S(1)}, u32[]{:S(2)}, u32[]{:S(2)}) collective-permute-start(bf16[528,128]{1,0:T(8,128)(2,1)S(1)} %get-tuple-element.31.refs_0_), channel_id=1, source_target_pairs={{0,8},{4,12},{8,0},{12,4},{16,24},{20,28},{24,16},{28,20},{1,9},{5... | collective-permute-start | bytes 405512 | tf_op jit(solution)/shard_map/ppermute | solution.py:367
  5.4 7.9 %collective-permute-start.1 = (bf16[528,128]{1,0:T(8,128)(2,1)S(1)}, bf16[528,128]{1,0:T(8,128)(2,1)S(1)}, u32[]{:S(2)}, u32[]{:S(2)}) collective-permute-start(bf16[528,128]{1,0:T(8,128)(2,1)S(1)} %get-tuple-element.31.refs_0_), channel_id=1, source_target_pairs={{0,16},{4,20},{8,24},{12,28},{16,0},{20,4},{24,8},{28,12},{1,17},{... | collective-permute-start | bytes 405512 | tf_op jit(solution)/shard_map/ppermute | solution.py:367
  6.9 6.4 %collective-permute-start.2 = (bf16[528,128]{1,0:T(8,128)(2,1)S(1)}, bf16[528,128]{1,0:T(8,128)(2,1)S(1)}, u32[]{:S(2)}, u32[]{:S(2)}) collective-permute-start(bf16[528,128]{1,0:T(8,128)(2,1)S(1)} %get-tuple-element.31.refs_0_), channel_id=1, source_target_pairs={{0,24},{4,28},{8,16},{12,20},{16,8},{20,12},{24,0},{28,4},{1,25},{... | collective-permute-start | bytes 405512 | tf_op jit(solution)/shard_map/ppermute | solution.py:367
  7.0 9.9 %collective-permute-start.3 = (bf16[528,128]{1,0:T(8,128)(2,1)S(1)}, bf16[528,128]{1,0:T(8,128)(2,1)S(1)}, u32[]{:S(2)}, u32[]{:S(2)}) collective-permute-start(bf16[528,128]{1,0:T(8,128)(2,1)S(1)} %get-tuple-element.31.refs_0_), channel_id=1, source_target_pairs={{0,4},{4,0},{8,12},{12,8},{16,20},{20,16},{24,28},{28,24},{1,5},{5... | collective-permute-start | bytes 405512 | tf_op jit(solution)/shard_map/ppermute | solution.py:367
  9.4 7.5 %collective-permute-start.4 = (bf16[528,128]{1,0:T(8,128)(2,1)S(1)}, bf16[528,128]{1,0:T(8,128)(2,1)S(1)}, u32[]{:S(2)}, u32[]{:S(2)}) collective-permute-start(bf16[528,128]{1,0:T(8,128)(2,1)S(1)} %collective-permute-done.refs_1_), channel_id=1, source_target_pairs={{0,4},{4,0},{8,12},{12,8},{16,20},{20,16},{24,28},{28,24},{1,5},{5... | collective-permute-start | bytes 405512 | tf_op jit(solution)/shard_map/ppermute | solution.py:367
  18.8 6.5 %collective-permute-start.7 = (s16[272,128]{1,0:T(8,128)(2,1)S(1)}, s16[272,128]{1,0:T(8,128)(2,1)S(1)}, u32[]{:S(2)}, u32[]{:S(2)}) collective-permute-start(s16[272,128]{1,0:T(8,128)(2,1)S(1)} %get-tuple-element.38), channel_id=1, source_target_pairs={{0,1},{1,2},{2,3},{3,0},{4,5},{5,6},{6,7},{7,4},{8,9},{9,10},{10,1... | collective-permute-start | bytes 208904 | tf_op jit(solution)/shard_map/ppermute | solution.py:370
  20.4 7.5 %collective-permute-start.8 = (s16[272,128]{1,0:T(8,128)(2,1)S(1)}, s16[272,128]{1,0:T(8,128)(2,1)S(1)}, u32[]{:S(2)}, u32[]{:S(2)}) collective-permute-start(s16[272,128]{1,0:T(8,128)(2,1)S(1)} %get-tuple-element.39), channel_id=1, source_target_pairs={{0,2},{1,3},{2,0},{3,1},{4,6},{5,7},{6,4},{7,5},{8,10},{9,11},{10,... | collective-permute-start | bytes 208904 | tf_op jit(solution)/shard_map/ppermute | solution.py:370
  23.0 5.1 %collective-permute-start.9 = (s16[272,128]{1,0:T(8,128)(2,1)S(1)}, s16[272,128]{1,0:T(8,128)(2,1)S(1)}, u32[]{:S(2)}, u32[]{:S(2)}) collective-permute-start(s16[272,128]{1,0:T(8,128)(2,1)S(1)} %get-tuple-element.40), channel_id=1, source_target_pairs={{0,3},{1,0},{2,1},{3,2},{4,7},{5,4},{6,5},{7,6},{8,11},{9,8},{10,9... | collective-permute-start | bytes 208904 | tf_op jit(solution)/shard_map/ppermute | solution.py:370
  28.9 6.6 %collective-permute-start.10 = (s16[272,128]{1,0:T(8,128)(2,1)S(1)}, s16[272,128]{1,0:T(8,128)(2,1)S(1)}, u32[]{:S(2)}, u32[]{:S(2)}) collective-permute-start(s16[272,128]{1,0:T(8,128)(2,1)S(1)} %solve_0.1.refs_0_), channel_id=1, source_target_pairs={{0,1},{1,2},{2,3},{3,0},{4,5},{5,6},{6,7},{7,4},{8,9},{9,10},{10,1... | collective-permute-start | bytes 208904 | tf_op jit(solution)/shard_map/ppermute | solution.py:370
  30.6 6.9 %collective-permute-start.11 = (s16[272,128]{1,0:T(8,128)(2,1)S(1)}, s16[272,128]{1,0:T(8,128)(2,1)S(1)}, u32[]{:S(2)}, u32[]{:S(2)}) collective-permute-start(s16[272,128]{1,0:T(8,128)(2,1)S(1)} %solve_0.1.refs_0_), channel_id=1, source_target_pairs={{0,2},{1,3},{2,0},{3,1},{4,6},{5,7},{6,4},{7,5},{8,10},{9,11},{10,... | collective-permute-start | bytes 208904 | tf_op jit(solution)/shard_map/ppermute | solution.py:370
  32.5 5.3 %collective-permute-start.12 = (s16[272,128]{1,0:T(8,128)(2,1)S(1)}, s16[272,128]{1,0:T(8,128)(2,1)S(1)}, u32[]{:S(2)}, u32[]{:S(2)}) collective-permute-start(s16[272,128]{1,0:T(8,128)(2,1)S(1)} %solve_0.1.refs_0_), channel_id=1, source_target_pairs={{0,3},{1,0},{2,1},{3,2},{4,7},{5,4},{6,5},{7,6},{8,11},{9,8},{10,9... | collective-permute-start | bytes 208904 | tf_op jit(solution)/shard_map/ppermute | solution.py:370
  38.5 4.9 %collective-permute-start.13 = (bf16[384,128]{1,0:T(8,128)(2,1)S(1)}, bf16[384,128]{1,0:T(8,128)(2,1)S(1)}, u32[]{:S(2)}, u32[]{:S(2)}) collective-permute-start(bf16[384,128]{1,0:T(8,128)(2,1)S(1)} %get-tuple-element.44), channel_id=1, source_target_pairs={{0,8},{4,12},{8,0},{12,4},{16,24},{20,28},{24,16},{28,20},{1,9},{5... | collective-permute-start | bytes 294920 | tf_op jit(solution)/shard_map/ppermute | solution.py:367
  39.8 6.6 %collective-permute-start.14 = (bf16[384,128]{1,0:T(8,128)(2,1)S(1)}, bf16[384,128]{1,0:T(8,128)(2,1)S(1)}, u32[]{:S(2)}, u32[]{:S(2)}) collective-permute-start(bf16[384,128]{1,0:T(8,128)(2,1)S(1)} %get-tuple-element.45), channel_id=1, source_target_pairs={{0,16},{4,20},{8,24},{12,28},{16,0},{20,4},{24,8},{28,12},{1,17},{... | collective-permute-start | bytes 294920 | tf_op jit(solution)/shard_map/ppermute | solution.py:367
  40.6 5.9 %collective-permute-start.15 = (bf16[384,128]{1,0:T(8,128)(2,1)S(1)}, bf16[384,128]{1,0:T(8,128)(2,1)S(1)}, u32[]{:S(2)}, u32[]{:S(2)}) collective-permute-start(bf16[384,128]{1,0:T(8,128)(2,1)S(1)} %get-tuple-element.46), channel_id=1, source_target_pairs={{0,24},{4,28},{8,16},{12,20},{16,8},{20,12},{24,0},{28,4},{1,25},{... | collective-permute-start | bytes 294920 | tf_op jit(solution)/shard_map/ppermute | solution.py:367
  42.0 4.5 %collective-permute-start.16 = (bf16[384,128]{1,0:T(8,128)(2,1)S(1)}, bf16[384,128]{1,0:T(8,128)(2,1)S(1)}, u32[]{:S(2)}, u32[]{:S(2)}) collective-permute-start(bf16[384,128]{1,0:T(8,128)(2,1)S(1)} %get-tuple-element.47), channel_id=1, source_target_pairs={{0,4},{4,0},{8,12},{12,8},{16,20},{20,16},{24,28},{28,24},{1,5},{5... | collective-permute-start | bytes 294920 | tf_op jit(solution)/shard_map/ppermute | solution.py:367
  42.0 5.1 %collective-permute-start.17 = (bf16[384,128]{1,0:T(8,128)(2,1)S(1)}, bf16[384,128]{1,0:T(8,128)(2,1)S(1)}, u32[]{:S(2)}, u32[]{:S(2)}) collective-permute-start(bf16[384,128]{1,0:T(8,128)(2,1)S(1)} %get-tuple-element.48), channel_id=1, source_target_pairs={{0,12},{4,8},{8,4},{12,0},{16,28},{20,24},{24,20},{28,16},{1,13},{... | collective-permute-start | bytes 294920 | tf_op jit(solution)/shard_map/ppermute | solution.py:367
  43.4 4.5 %collective-permute-start.18 = (bf16[384,128]{1,0:T(8,128)(2,1)S(1)}, bf16[384,128]{1,0:T(8,128)(2,1)S(1)}, u32[]{:S(2)}, u32[]{:S(2)}) collective-permute-start(bf16[384,128]{1,0:T(8,128)(2,1)S(1)} %get-tuple-element.49), channel_id=1, source_target_pairs={{0,20},{4,16},{8,28},{12,24},{16,4},{20,0},{24,12},{28,8},{1,21},{... | collective-permute-start | bytes 294920 | tf_op jit(solution)/shard_map/ppermute | solution.py:367
  46.4 5.5 %collective-permute-start.19 = (bf16[384,128]{1,0:T(8,128)(2,1)S(1)}, bf16[384,128]{1,0:T(8,128)(2,1)S(1)}, u32[]{:S(2)}, u32[]{:S(2)}) collective-permute-start(bf16[384,128]{1,0:T(8,128)(2,1)S(1)} %get-tuple-element.50), channel_id=1, source_target_pairs={{0,28},{4,24},{8,20},{12,16},{16,12},{20,8},{24,4},{28,0},{1,29},{... | collective-permute-start | bytes 294920 | tf_op jit(solution)/shard_map/ppermute | solution.py:367
  53.7 7.0 %collective-permute-start.20 = (s16[272,128]{1,0:T(8,128)(2,1)S(1)}, s16[272,128]{1,0:T(8,128)(2,1)S(1)}, u32[]{:S(2)}, u32[]{:S(2)}) collective-permute-start(s16[272,128]{1,0:T(8,128)(2,1)S(1)} %get-tuple-element.52), channel_id=1, source_target_pairs={{0,1},{1,2},{2,3},{3,0},{4,5},{5,6},{6,7},{7,4},{8,9},{9,10},{10,1... | collective-permute-start | bytes 208904 | tf_op jit(solution)/shard_map/ppermute | solution.py:370
  55.5 7.1 %collective-permute-start.21 = (s16[272,128]{1,0:T(8,128)(2,1)S(1)}, s16[272,128]{1,0:T(8,128)(2,1)S(1)}, u32[]{:S(2)}, u32[]{:S(2)}) collective-permute-start(s16[272,128]{1,0:T(8,128)(2,1)S(1)} %get-tuple-element.53), channel_id=1, source_target_pairs={{0,2},{1,3},{2,0},{3,1},{4,6},{5,7},{6,4},{7,5},{8,10},{9,11},{10,... | collective-permute-start | bytes 208904 | tf_op jit(solution)/shard_map/ppermute | solution.py:370
  55.9 6.6 %collective-permute-start.22 = (s16[272,128]{1,0:T(8,128)(2,1)S(1)}, s16[272,128]{1,0:T(8,128)(2,1)S(1)}, u32[]{:S(2)}, u32[]{:S(2)}) collective-permute-start(s16[272,128]{1,0:T(8,128)(2,1)S(1)} %get-tuple-element.54), channel_id=1, source_target_pairs={{0,3},{1,0},{2,1},{3,2},{4,7},{5,4},{6,5},{7,6},{8,11},{9,8},{10,9... | collective-permute-start | bytes 208904 | tf_op jit(solution)/shard_map/ppermute | solution.py:370
  63.3 6.6 %collective-permute-start.23 = (s16[272,128]{1,0:T(8,128)(2,1)S(1)}, s16[272,128]{1,0:T(8,128)(2,1)S(1)}, u32[]{:S(2)}, u32[]{:S(2)}) collective-permute-start(s16[272,128]{1,0:T(8,128)(2,1)S(1)} %solve_1.1.refs_0_), channel_id=1, source_target_pairs={{0,1},{1,2},{2,3},{3,0},{4,5},{5,6},{6,7},{7,4},{8,9},{9,10},{10,1... | collective-permute-start | bytes 208904 | tf_op jit(solution)/shard_map/ppermute | solution.py:370
  65.2 6.8 %collective-permute-start.24 = (s16[272,128]{1,0:T(8,128)(2,1)S(1)}, s16[272,128]{1,0:T(8,128)(2,1)S(1)}, u32[]{:S(2)}, u32[]{:S(2)}) collective-permute-start(s16[272,128]{1,0:T(8,128)(2,1)S(1)} %solve_1.1.refs_0_), channel_id=1, source_target_pairs={{0,2},{1,3},{2,0},{3,1},{4,6},{5,7},{6,4},{7,5},{8,10},{9,11},{10,... | collective-permute-start | bytes 208904 | tf_op jit(solution)/shard_map/ppermute | solution.py:370
  66.0 6.1 %collective-permute-start.25 = (s16[272,128]{1,0:T(8,128)(2,1)S(1)}, s16[272,128]{1,0:T(8,128)(2,1)S(1)}, u32[]{:S(2)}, u32[]{:S(2)}) collective-permute-start(s16[272,128]{1,0:T(8,128)(2,1)S(1)} %solve_1.1.refs_0_), channel_id=1, source_target_pairs={{0,3},{1,0},{2,1},{3,2},{4,7},{5,4},{6,5},{7,6},{8,11},{9,8},{10,9... | collective-permute-start | bytes 208904 | tf_op jit(solution)/shard_map/ppermute | solution.py:370
  (6 other events, 25.6 us)

commit v3 on v2

--- a/solution.py
+++ b/solution.py
@@ -39,6 +39,14 @@
     ]
 
 
+def in_hbm(x):
+    return pltpu.with_memory_space_constraint(x, pltpu.HBM)
+
+
+def in_smem(x):
+    return pltpu.with_memory_space_constraint(x, pltpu.SMEM)
+
+
 def log2(n):
     return n.bit_length() - 1
 
@@ -60,12 +68,19 @@
     )
 
 
-def start_kernel(groups, colidx_ref, live_ref, prior_ref, msg_ref, first_ref, alive_ref, rows):
+def start_kernel(groups, prior_dev, colidx, live, prior, msg_ref, first_ref, alive_ref, *scratch):
+    colidx_ref, live_ref, rows, sems = scratch
     slots, _, rows_dev = colidx_ref.shape
-    prior_dev, probes, _ = prior_ref.shape
-    for k in range(prior_dev):
-        msg_ref[k * probes : (k + 1) * probes] = prior_ref[k]
+    copies = [
+        pltpu.make_async_copy(prior, msg_ref.at[pl.ds(0, prior.shape[0])], sems.at[0]),
+        pltpu.make_async_copy(colidx, colidx_ref, sems.at[1]),
+        pltpu.make_async_copy(live, live_ref, sems.at[2]),
+    ]
+    for copy in copies:
+        copy.start()
     rows[...] = jnp.zeros(rows.shape, I32)
+    copies[1].wait()
+    copies[2].wait()
     for j in range(slots):
         rows[j : j + 1] = colidx_ref[j, 0:1]
         rows[8 + j : 9 + j] = lax.shift_right_logical(colidx_ref[j, 1:2], 4)
@@ -74,7 +89,7 @@
         rows[32 + j : 33 + j] = colidx_ref[j, 0:1] & 15
     rows[40:42] = live_ref[...]
     wide = spread(rows[...], rows_dev)
-    msg_ref[prior_dev * probes :] = wide[8:24].astype(BF16)
+    msg_ref[prior.shape[0] :] = wide[8:24].astype(BF16)
     me, here = lax.axis_index("rows"), lax.axis_index("cols")
     ids = here * slots + lanes_like((8, LANES), 0)
     refs = (wide[24:32] * 16.0 + wide[32:40]).astype(I32)
@@ -82,6 +97,7 @@
     found = table_at(refs, me, prior_dev, groups // 2)
     first_ref[...] = jnp.where(ids < live[0:1], found, groups * prior_dev)
     alive_ref[...] = (ids < live[1:2]).astype(I32)
+    copies[0].wait()
 
 
 def start(groups, colidx, live, prior):
@@ -89,14 +105,19 @@
     prior_dev, probes, order = prior.shape
     table = jax.ShapeDtypeStruct((8, LANES), I32)
     return pl.pallas_call(
-        functools.partial(start_kernel, groups),
+        functools.partial(start_kernel, groups, prior_dev),
         out_shape=[jax.ShapeDtypeStruct((prior_dev * probes + TAIL, order), BF16), table, table],
-        in_specs=[VMEM] * 3,
+        in_specs=[HBM] * 3,
         out_specs=[VMEM] * 3,
-        scratch_shapes=[pltpu.VMEM((48, rows_dev), I32)],
+        scratch_shapes=[
+            pltpu.VMEM((slots, 2, rows_dev), I32),
+            pltpu.VMEM((2, rows_dev), I32),
+            pltpu.VMEM((48, rows_dev), I32),
+            pltpu.SemaphoreType.DMA((3,)),
+        ],
         compiler_params=PARAMS,
         name="start",
-    )(jnp.transpose(colidx, (2, 0, 1)), live, prior)
+    )(*(in_hbm(x) for x in (jnp.transpose(colidx, (2, 0, 1)), live, prior.reshape(-1, order))))
 
 
 def ranks(mask, within, slots):
@@ -112,7 +133,8 @@
 
 
 def route_kernel(groups, cap, slots, prior_dev, owner_ref, alive_ref, *refs):
-    tails, want_ref, second_ref = refs[:groups], refs[groups], refs[groups + 1]
+    tails, outs = refs[:groups], refs[groups : groups + 2]
+    want_ref, second_ref, sems = refs[groups + 2 :]
     rows_front = owner_ref.shape[1]
     rows_dev = rows_front // groups
     half = groups // 2
@@ -166,54 +188,91 @@
         table_at(own, me, prior_dev, half),
     )
     second_ref[...] = jnp.where(alive_ref[...] > 0, at, prior_count + groups * cap)
-
-
-def route(groups, cap, slots, prior_dev, owner_map, alive, pieces):
-    rows_dev = owner_map.shape[1] // groups
-    return pl.pallas_call(
-        functools.partial(route_kernel, groups, cap, slots, prior_dev),
-        out_shape=[
-            jax.ShapeDtypeStruct((-(-cap // 8) * 8, groups * rows_dev), I32),
-            jax.ShapeDtypeStruct((8, LANES), I32),
-        ],
-        in_specs=[SMEM] + [VMEM] * (groups + 1),
-        out_specs=[VMEM] * 2,
-        compiler_params=PARAMS,
-        name="route",
-    )(owner_map, alive, *pieces)
-
-
-def load_kernel(blocks, right_side, inverse, *refs):
-    outs, sems = refs[:-1], refs[-1]
-    part = outs[2].shape[1]
-    first = lax.axis_index("cols") * part
-    sources = [
-        blocks.at[0],
-        blocks.at[1],
-        right_side.at[:, pl.ds(first, part)],
-        inverse.at[:, pl.ds(first, part)],
+    copies = [
+        pltpu.make_async_copy(x, out, sems.at[i])
+        for i, (x, out) in enumerate(zip((want_ref, second_ref), outs))
     ]
-    copies = [pltpu.make_async_copy(a, b, sems.at[i]) for i, (a, b) in enumerate(zip(sources, outs))]
     for copy in copies:
         copy.start()
     for copy in copies:
         copy.wait()
 
 
-def load(cols, blocks, right_side, inverse):
+def route(groups, cap, slots, prior_dev, owner_map, alive, pieces):
+    shapes = [(-(-cap // 8) * 8, owner_map.shape[1]), (8, LANES)]
+    return pl.pallas_call(
+        functools.partial(route_kernel, groups, cap, slots, prior_dev),
+        out_shape=[pltpu.SMEM(a, I32) for a in shapes],
+        in_specs=[SMEM] + [VMEM] * (groups + 1),
+        out_specs=[SMEM] * 2,
+        scratch_shapes=[pltpu.VMEM(a, I32) for a in shapes] + [pltpu.SemaphoreType.DMA((2,))],
+        compiler_params=PARAMS,
+        name="route",
+    )(owner_map, alive, *pieces)
+
+
+def load_kernel(cols, first_at, blocks, right_side, inverse, *refs):
+    outs, at_ref, raw, raw_inverse, sems = refs[:4], refs[4], refs[5], refs[6], refs[7]
+    fronts, rows_dev, slots = blocks.shape[:3]
+    part = rows_dev // cols
+    first = lax.axis_index("cols") * part
+    names = pltpu.make_async_copy(first_at, at_ref, sems.at[fronts * cols + 2])
+    names.start()
+    copies = []
+    for f in range(fronts):
+        for s in range(cols):
+            rows = pl.ds(s * part, part)
+            copies.append(
+                pltpu.make_async_copy(
+                    blocks.at[f, rows], raw.at[f, rows], sems.at[f * cols + s]
+                )
+            )
+    copies += [
+        pltpu.make_async_copy(
+            inverse.at[:, pl.ds(first, part)], raw_inverse, sems.at[fronts * cols]
+        ),
+        pltpu.make_async_copy(
+            right_side.at[:, pl.ds(first, part)], outs[2], sems.at[fronts * cols + 1]
+        ),
+    ]
+    for copy in copies:
+        copy.start()
+    for f in range(fronts):
+        for s in range(cols):
+            copies[f * cols + s].wait()
+            for i in range(s * part, (s + 1) * part):
+                for j in range(slots):
+                    outs[f][i, j] = raw[f, i, j].T
+    copies[-2].wait()
+    for f in range(fronts):
+        for k in range(part):
+            outs[3][f, k] = raw_inverse[f, k].T
+    copies[-1].wait()
+    names.wait()
+
+
+def load(cols, first_at, blocks, right_side, inverse):
     part = blocks.shape[1] // cols
     shapes = [blocks.shape[1:]] * 2
     shapes += [a.shape[:1] + (part,) + a.shape[2:] for a in (right_side, inverse)]
     kinds = [BF16, BF16, F32, F32]
     return pl.pallas_call(
-        load_kernel,
-        out_shape=[pltpu.VMEM(a, b) for a, b in zip(shapes, kinds)],
-        in_specs=[HBM] * 3,
-        out_specs=[VMEM] * 4,
-        scratch_shapes=[pltpu.SemaphoreType.DMA((4,))],
-        compiler_params=PARAMS,
+        functools.partial(load_kernel, cols),
+        out_shape=[pltpu.VMEM(a, b) for a, b in zip(shapes, kinds)]
+        + [pltpu.SMEM(first_at.shape, I32)],
+        in_specs=[VMEM] + [HBM] * 3,
+        out_specs=[VMEM] * 4 + [SMEM],
+        scratch_shapes=[
+            pltpu.VMEM(blocks.shape, BF16),
+            pltpu.VMEM(shapes[3], F32),
+            pltpu.SemaphoreType.DMA((2 * cols + 3,)),
+        ],
+        compiler_params=PARAMS,
+        cost_estimate=pl.CostEstimate(
+            flops=0, transcendentals=0, bytes_accessed=2 * blocks.size * blocks.dtype.itemsize
+        ),
         name="load",
-    )(*(pltpu.with_memory_space_constraint(x, pltpu.HBM) for x in (blocks, right_side, inverse)))
+    )(first_at, *(in_hbm(x) for x in (blocks, right_side, inverse)))
 
 
 def partial_kernel(cols, n_early, probes, idx_ref, blk, *refs):
@@ -236,8 +295,8 @@
             sums.append(
                 lax.dot_general(
                     jnp.concatenate(xs, axis=1),
-                    jnp.concatenate(ws, axis=1),
-                    (((1,), (1,)), ((), ())),
+                    jnp.concatenate(ws, axis=0),
+                    (((1,), (0,)), ((), ())),
                     preferred_element_type=F32,
                 )
             )
@@ -261,7 +320,7 @@
         scratch_shapes=[pltpu.VMEM((rows // probes + 1, probes, order), BF16)],
         compiler_params=PARAMS,
         name=name,
-    )(idx, blocks, *early, *recent)
+    )(in_smem(idx), blocks, *early, *recent)
     return out[0], out[1:]
 
 
@@ -275,7 +334,7 @@
         lax.dot_general(
             rhs_ref[front, k] - total[k],
             inv_ref[front, k],
-            (((1,), (1,)), ((), ())),
+            (((1,), (0,)), ((), ())),
             precision=lax.Precision.HIGHEST,
             preferred_element_type=F32,
         )
@@ -320,7 +379,7 @@
         scratch_shapes=[pltpu.VMEM((rows_dev, probes, order), BF16)],
         compiler_params=PARAMS,
         name="pack",
-    )(sel, *msgs)
+    )(in_smem(sel), *msgs)
 
 
 def unpack_kernel(front, cols, *refs):
@@ -370,9 +429,13 @@
         return lax.ppermute(x, "cols", [(i, (i + step) % cols) for i in range(cols)])
 
     own, first_at, alive = start(groups, colidx, live, prior)
-    pieces = [own] + [over_rows(own, 2 * k) for k in range(1, half)]
+    chips = [over_rows(own, 2 * k) for k in range(1, half)]
+    blocks0, blocks1, rhs, inverse, first_at = load(
+        cols, first_at, blocks, right_side, diag_inverse
+    )
+    chips, blocks0 = lax.optimization_barrier((chips, blocks0))
+    pieces = [own] + chips
     pieces += [over_rows(x, 1) for x in pieces]
-    blocks0, blocks1, rhs, inverse = load(cols, blocks, right_side, diag_inverse)
     want, second_at = route(groups, cap, slots, prior_dev, owner_map, alive, pieces)
 
     own0, msgs0 = partial_products("partial_0", cols, probes, first_at, blocks0, pieces, [])

time: 73.1 us -> 67.3 us (0.921)
  local copies, waits for them, and re-layouts: 2.28 us -> 0.01 us
  Pallas kernels: 11.8 us -> 10.6 us
  starting transfers between devices: 28.7 us -> 27.5 us
  waiting for transfers between devices: 30 us -> 29 us
    ppermute x14, waiting for transfers between devices: 14.5 us -> 11.4 us  [over_rows(): return lax.ppermute(x, 'rows', [(i, i ^ mask) for i in range(groups)])]
    unnamed x8 -> x2, local copies, waits for them, and re-layouts: 2.28 us -> 0.01 us
    pallas_call x2, Pallas kernels: 3.73 us -> 1.7 us  [partial_products(): pl.pallas_call(functools.partial(partial_kernel, cols, len(early), probes...]
    ppermute x12, waiting for transfers between devices: 15.6 us -> 17.5 us  [over_cols(): lax.ppermute(x, 'cols', [(i, (i + step) % cols) for i in range(cols)])]
    ppermute x12, starting transfers between devices: 18.3 us -> 16.7 us  [over_cols(): lax.ppermute(x, 'cols', [(i, (i + step) % cols) for i in range(cols)])]
    pallas_call x2, Pallas kernels: 3.14 us -> 4.44 us  [the longest x1 3.51 us: load(): pl.pallas_call(functools.partial(load_kernel, cols), out_shape=[pltpu.VME...]
  transfers between devices with their start and end apart: 26 -> 26, of which waited for: 17 -> 18; matrix products, arithmetic and copies ran while one was open for 0% -> 0% of each run, Pallas kernels for 7% -> 9%
where the time goes in v3:
time: 67.3 us; the launch traced here: 67.2 us
  waiting for transfers between devices  29 us (43%)
  starting transfers between devices  27.5 us (41%)
  Pallas kernels  10.6 us (16%)
    ppermute x12, waiting for transfers between devices, over_cols(): lax.ppermute(x, 'cols', [(i, (i + step) % cols) for i in range(cols)])  17.5 us
    ppermute x12, starting transfers between devices, over_cols(): lax.ppermute(x, 'cols', [(i, (i + step) % cols) for i in range(cols)])  16.7 us
    ppermute x14, waiting for transfers between devices, over_rows(): return lax.ppermute(x, 'rows', [(i, i ^ mask) for i in range(groups)])  11.4 us
    ppermute x14, starting transfers between devices, over_rows(): return lax.ppermute(x, 'rows', [(i, i ^ mask) for i in range(groups)])  10.8 us
    pallas_call x1, Pallas kernels, load(): pl.pallas_call(functools.partial(load_kernel, cols), out_shape=[pltpu.VME...  3.51 us
    pallas_call x2, Pallas kernels, partial_products(): pl.pallas_call(functools.partial(partial_kernel, cols, len(early), probes...  1.7 us
    pallas_call x2, Pallas kernels, unpack(): pl.pallas_call(functools.partial(unpack_kernel, front, cols), out_shape=j...  1.68 us
    pallas_call x1, Pallas kernels, route(): pl.pallas_call(functools.partial(route_kernel, groups, cap, slots, prior_...  1.62 us
  transfers between devices with their start and end apart: 26, of which 18 were waited for; matrix products, arithmetic and copies ran while one was open for 0% of the time, Pallas kernels for 9%

profile of v3, /device:TPU:0, one launch (start us, length us, event | category | flops | bytes accessed | tf_op | source)
XLA Modules:
  0.0 67.2 jit_solution(13540451282707417237)
XLA Ops:
  0.0 0.9 %start.1 = (bf16[528,128]{1,0:T(8,128)(2,1)S(1)}, s32[8,128]{1,0:T(8,128)S(1)}, s32[8,128]{1,0:T(8,128)S(1)}) custom-call(s32[6,2,16]{2,1,0:T(2,128)} %bitcast.3, s32[2,16]{1,0:T(2,128)} %live.1, bf16[512,128]{1,0:T(8,128)(2,1)} %bitcast.2), custom_call_target="tpu_custom_call" | custom-call | tf_op jit(solution)/shard_map/start/pallas_call | solution.py:107
  0.9 4.0 %collective-permute-start.2 = (bf16[528,128]{1,0:T(8,128)(2,1)S(1)}, bf16[528,128]{1,0:T(8,128)(2,1)S(1)}, u32[]{:S(2)}, u32[]{:S(2)}) collective-permute-start(bf16[528,128]{1,0:T(8,128)(2,1)S(1)} %get-tuple-element.36.refs_0_), channel_id=1, source_target_pairs={{0,24},{4,28},{8,16},{12,20},{16,8},{20,12},{24,0},{28,4},{1,25},{... | collective-permute-start | bytes 405512 | tf_op jit(solution)/shard_map/ppermute | solution.py:426
  5.5 3.5 %load.1 = (bf16[16,6,128,128]{3,2,1,0:T(8,128)(2,1)S(1)}, bf16[16,6,128,128]{3,2,1,0:T(8,128)(2,1)S(1)}, f32[2,4,64,128]{3,2,1,0:T(8,128)S(1)}, f32[2,4,128,128]{3,2,1,0:T(8,128)S(1)}, s32[8,128]{1,0:T(8,128)S(4)}) custom-call(s32[8,128]{1,0:T(8,128)S(1)} %get-tuple-element.37.first_at, bf16[2,16,6,128,128]{4,3,2,1,0:T(8,128)(2,1)} %blocks.1, ...), custom_call_target="tpu_custom_call" | custom-call | bytes 12582912 | tf_op jit(solution)/shard_map/load/pallas_call | solution.py:259
  9.1 2.3 %collective-permute-done.1.refs_2_ = bf16[528,128]{1,0:T(8,128)(2,1)S(1)} collective-permute-done((bf16[528,128]{1,0:T(8,128)(2,1)S(1)}, bf16[528,128]{1,0:T(8,128)(2,1)S(1)}, u32[]{:S(2)}, u32[]{:S(2)}) %collective-permute-start.1) | collective-permute-done | bytes 135200 | tf_op jit(solution)/shard_map/ppermute | solution.py:426
  14.3 1.6 %collective-permute-start.7 = (s16[272,128]{1,0:T(8,128)(2,1)S(1)}, s16[272,128]{1,0:T(8,128)(2,1)S(1)}, u32[]{:S(2)}, u32[]{:S(2)}) collective-permute-start(s16[272,128]{1,0:T(8,128)(2,1)S(1)} %get-tuple-element.48), channel_id=1, source_target_pairs={{0,1},{1,2},{2,3},{3,0},{4,5},{5,6},{6,7},{7,4},{8,9},{9,10},{10,1... | collective-permute-start | bytes 208904 | tf_op jit(solution)/shard_map/ppermute | solution.py:429
  16.0 2.6 %collective-permute-start.8 = (s16[272,128]{1,0:T(8,128)(2,1)S(1)}, s16[272,128]{1,0:T(8,128)(2,1)S(1)}, u32[]{:S(2)}, u32[]{:S(2)}) collective-permute-start(s16[272,128]{1,0:T(8,128)(2,1)S(1)} %get-tuple-element.49), channel_id=1, source_target_pairs={{0,2},{1,3},{2,0},{3,1},{4,6},{5,7},{6,4},{7,5},{8,10},{9,11},{10,... | collective-permute-start | bytes 208904 | tf_op jit(solution)/shard_map/ppermute | solution.py:429
  18.5 1.3 %collective-permute-start.9 = (s16[272,128]{1,0:T(8,128)(2,1)S(1)}, s16[272,128]{1,0:T(8,128)(2,1)S(1)}, u32[]{:S(2)}, u32[]{:S(2)}) collective-permute-start(s16[272,128]{1,0:T(8,128)(2,1)S(1)} %get-tuple-element.50), channel_id=1, source_target_pairs={{0,3},{1,0},{2,1},{3,2},{4,7},{5,4},{6,5},{7,6},{8,11},{9,8},{10,9... | collective-permute-start | bytes 208904 | tf_op jit(solution)/shard_map/ppermute | solution.py:429
  19.9 0.9 %collective-permute-done.7.refs_0_ = s16[272,128]{1,0:T(8,128)(2,1)S(1)} collective-permute-done((s16[272,128]{1,0:T(8,128)(2,1)S(1)}, s16[272,128]{1,0:T(8,128)(2,1)S(1)}, u32[]{:S(2)}, u32[]{:S(2)}) %collective-permute-start.7) | collective-permute-done | bytes 69664 | tf_op jit(solution)/shard_map/ppermute | solution.py:429
  20.8 2.8 %collective-permute-done.8.refs_1_ = s16[272,128]{1,0:T(8,128)(2,1)S(1)} collective-permute-done((s16[272,128]{1,0:T(8,128)(2,1)S(1)}, s16[272,128]{1,0:T(8,128)(2,1)S(1)}, u32[]{:S(2)}, u32[]{:S(2)}) %collective-permute-start.8) | collective-permute-done | bytes 69664 | tf_op jit(solution)/shard_map/ppermute | solution.py:429
  24.4 2.9 %collective-permute-start.12 = (s16[272,128]{1,0:T(8,128)(2,1)S(1)}, s16[272,128]{1,0:T(8,128)(2,1)S(1)}, u32[]{:S(2)}, u32[]{:S(2)}) collective-permute-start(s16[272,128]{1,0:T(8,128)(2,1)S(1)} %solve_0.1.refs_0_), channel_id=1, source_target_pairs={{0,3},{1,0},{2,1},{3,2},{4,7},{5,4},{6,5},{7,6},{8,11},{9,8},{10,9... | collective-permute-start | bytes 208904 | tf_op jit(solution)/shard_map/ppermute | solution.py:429
  27.9 1.6 %route.1 = (s32[8,128]{1,0:T(8,128)S(4)}, s32[8,128]{1,0:T(8,128)S(4)}) custom-call(s32[2,128]{1,0:T(2,128)S(1)} %copy-done, s32[8,128]{1,0:T(8,128)S(1)} %get-tuple-element.35.alive_ref, bf16[528,128]{1,0:T(8,128)(2,1)S(1)} %get-tuple-element.36.refs_0_, bf16[528,128]{1,0:T(8,128)(2,1)S(1)} %collective-permute-done.refs_1_, ...), custom_call_target="tpu_custom_call" | custom-call | tf_op jit(solution)/shard_map/route/pallas_call | solution.py:203
  29.9 4.5 %collective-permute-done.11.refs_2_ = s16[272,128]{1,0:T(8,128)(2,1)S(1)} collective-permute-done((s16[272,128]{1,0:T(8,128)(2,1)S(1)}, s16[272,128]{1,0:T(8,128)(2,1)S(1)}, u32[]{:S(2)}, u32[]{:S(2)}) %collective-permute-start.11) | collective-permute-done | bytes 69664 | tf_op jit(solution)/shard_map/ppermute | solution.py:429
  34.5 1.6 %collective-permute-start.13 = (bf16[384,128]{1,0:T(8,128)(2,1)S(1)}, bf16[384,128]{1,0:T(8,128)(2,1)S(1)}, u32[]{:S(2)}, u32[]{:S(2)}) collective-permute-start(bf16[384,128]{1,0:T(8,128)(2,1)S(1)} %get-tuple-element.54), channel_id=1, source_target_pairs={{0,8},{4,12},{8,0},{12,4},{16,24},{20,28},{24,16},{28,20},{1,9},{5... | collective-permute-start | bytes 294920 | tf_op jit(solution)/shard_map/ppermute | solution.py:426
  36.8 1.2 %collective-permute-start.15 = (bf16[384,128]{1,0:T(8,128)(2,1)S(1)}, bf16[384,128]{1,0:T(8,128)(2,1)S(1)}, u32[]{:S(2)}, u32[]{:S(2)}) collective-permute-start(bf16[384,128]{1,0:T(8,128)(2,1)S(1)} %get-tuple-element.56), channel_id=1, source_target_pairs={{0,24},{4,28},{8,16},{12,20},{16,8},{20,12},{24,0},{28,4},{1,25},{... | collective-permute-start | bytes 294920 | tf_op jit(solution)/shard_map/ppermute | solution.py:426
  38.1 1.6 %collective-permute-start.17 = (bf16[384,128]{1,0:T(8,128)(2,1)S(1)}, bf16[384,128]{1,0:T(8,128)(2,1)S(1)}, u32[]{:S(2)}, u32[]{:S(2)}) collective-permute-start(bf16[384,128]{1,0:T(8,128)(2,1)S(1)} %get-tuple-element.58), channel_id=1, source_target_pairs={{0,12},{4,8},{8,4},{12,0},{16,28},{20,24},{24,20},{28,16},{1,13},{... | collective-permute-start | bytes 294920 | tf_op jit(solution)/shard_map/ppermute | solution.py:426
  40.0 2.6 %collective-permute-done.14.refs_10_ = bf16[384,128]{1,0:T(8,128)(2,1)S(1)} collective-permute-done((bf16[384,128]{1,0:T(8,128)(2,1)S(1)}, bf16[384,128]{1,0:T(8,128)(2,1)S(1)}, u32[]{:S(2)}, u32[]{:S(2)}) %collective-permute-start.14) | collective-permute-done | bytes 98336 | tf_op jit(solution)/shard_map/ppermute | solution.py:426
  43.1 1.6 %collective-permute-done.18.refs_14_ = bf16[384,128]{1,0:T(8,128)(2,1)S(1)} collective-permute-done((bf16[384,128]{1,0:T(8,128)(2,1)S(1)}, bf16[384,128]{1,0:T(8,128)(2,1)S(1)}, u32[]{:S(2)}, u32[]{:S(2)}) %collective-permute-start.18) | collective-permute-done | bytes 98336 | tf_op jit(solution)/shard_map/ppermute | solution.py:426
  44.7 3.0 %collective-permute-done.19.refs_15_ = bf16[384,128]{1,0:T(8,128)(2,1)S(1)} collective-permute-done((bf16[384,128]{1,0:T(8,128)(2,1)S(1)}, bf16[384,128]{1,0:T(8,128)(2,1)S(1)}, u32[]{:S(2)}, u32[]{:S(2)}) %collective-permute-start.19) | collective-permute-done | bytes 98336 | tf_op jit(solution)/shard_map/ppermute | solution.py:426
  48.7 1.3 %collective-permute-start.21 = (s16[272,128]{1,0:T(8,128)(2,1)S(1)}, s16[272,128]{1,0:T(8,128)(2,1)S(1)}, u32[]{:S(2)}, u32[]{:S(2)}) collective-permute-start(s16[272,128]{1,0:T(8,128)(2,1)S(1)} %get-tuple-element.63), channel_id=1, source_target_pairs={{0,2},{1,3},{2,0},{3,1},{4,6},{5,7},{6,4},{7,5},{8,10},{9,11},{10,... | collective-permute-start | bytes 208904 | tf_op jit(solution)/shard_map/ppermute | solution.py:429
  50.0 2.8 %collective-permute-start.22 = (s16[272,128]{1,0:T(8,128)(2,1)S(1)}, s16[272,128]{1,0:T(8,128)(2,1)S(1)}, u32[]{:S(2)}, u32[]{:S(2)}) collective-permute-start(s16[272,128]{1,0:T(8,128)(2,1)S(1)} %get-tuple-element.64), channel_id=1, source_target_pairs={{0,3},{1,0},{2,1},{3,2},{4,7},{5,4},{6,5},{7,6},{8,11},{9,8},{10,9... | collective-permute-start | bytes 208904 | tf_op jit(solution)/shard_map/ppermute | solution.py:429
  52.8 2.4 %collective-permute-done.20.refs_0_ = s16[272,128]{1,0:T(8,128)(2,1)S(1)} collective-permute-done((s16[272,128]{1,0:T(8,128)(2,1)S(1)}, s16[272,128]{1,0:T(8,128)(2,1)S(1)}, u32[]{:S(2)}, u32[]{:S(2)}) %collective-permute-start.20) | collective-permute-done | bytes 69664 | tf_op jit(solution)/shard_map/ppermute | solution.py:429
  55.3 1.4 %collective-permute-done.21.refs_1_ = s16[272,128]{1,0:T(8,128)(2,1)S(1)} collective-permute-done((s16[272,128]{1,0:T(8,128)(2,1)S(1)}, s16[272,128]{1,0:T(8,128)(2,1)S(1)}, u32[]{:S(2)}, u32[]{:S(2)}) %collective-permute-start.21) | collective-permute-done | bytes 69664 | tf_op jit(solution)/shard_map/ppermute | solution.py:429
  57.2 2.7 %collective-permute-start.25 = (s16[272,128]{1,0:T(8,128)(2,1)S(1)}, s16[272,128]{1,0:T(8,128)(2,1)S(1)}, u32[]{:S(2)}, u32[]{:S(2)}) collective-permute-start(s16[272,128]{1,0:T(8,128)(2,1)S(1)} %solve_1.1.refs_0_), channel_id=1, source_target_pairs={{0,3},{1,0},{2,1},{3,2},{4,7},{5,4},{6,5},{7,6},{8,11},{9,8},{10,9... | collective-permute-start | bytes 208904 | tf_op jit(solution)/shard_map/ppermute | solution.py:429
  61.9 4.4 %collective-permute-done.24.refs_2_ = s16[272,128]{1,0:T(8,128)(2,1)S(1)} collective-permute-done((s16[272,128]{1,0:T(8,128)(2,1)S(1)}, s16[272,128]{1,0:T(8,128)(2,1)S(1)}, u32[]{:S(2)}, u32[]{:S(2)}) %collective-permute-start.24) | collective-permute-done | bytes 69664 | tf_op jit(solution)/shard_map/ppermute | solution.py:429
  (40 shorter events, 11.2 us)
Async XLA Ops:
  0.9 8.1 %collective-permute-start.2 = (bf16[528,128]{1,0:T(8,128)(2,1)S(1)}, bf16[528,128]{1,0:T(8,128)(2,1)S(1)}, u32[]{:S(2)}, u32[]{:S(2)}) collective-permute-start(bf16[528,128]{1,0:T(8,128)(2,1)S(1)} %get-tuple-element.36.refs_0_), channel_id=1, source_target_pairs={{0,24},{4,28},{8,16},{12,20},{16,8},{20,12},{24,0},{28,4},{1,25},{... | collective-permute-start | bytes 405512 | tf_op jit(solution)/shard_map/ppermute | solution.py:426
  4.9 6.5 %collective-permute-start.1 = (bf16[528,128]{1,0:T(8,128)(2,1)S(1)}, bf16[528,128]{1,0:T(8,128)(2,1)S(1)}, u32[]{:S(2)}, u32[]{:S(2)}) collective-permute-start(bf16[528,128]{1,0:T(8,128)(2,1)S(1)} %get-tuple-element.36.refs_0_), channel_id=1, source_target_pairs={{0,16},{4,20},{8,24},{12,28},{16,0},{20,4},{24,8},{28,12},{1,17},{... | collective-permute-start | bytes 405512 | tf_op jit(solution)/shard_map/ppermute | solution.py:426
  5.4 6.2 %collective-permute-start = (bf16[528,128]{1,0:T(8,128)(2,1)S(1)}, bf16[528,128]{1,0:T(8,128)(2,1)S(1)}, u32[]{:S(2)}, u32[]{:S(2)}) collective-permute-start(bf16[528,128]{1,0:T(8,128)(2,1)S(1)} %get-tuple-element.36.refs_0_), channel_id=1, source_target_pairs={{0,8},{4,12},{8,0},{12,4},{16,24},{20,28},{24,16},{28,20},{1,9},{5... | collective-permute-start | bytes 405512 | tf_op jit(solution)/shard_map/ppermute | solution.py:426
  5.5 6.6 %collective-permute-start.3 = (bf16[528,128]{1,0:T(8,128)(2,1)S(1)}, bf16[528,128]{1,0:T(8,128)(2,1)S(1)}, u32[]{:S(2)}, u32[]{:S(2)}) collective-permute-start(bf16[528,128]{1,0:T(8,128)(2,1)S(1)} %get-tuple-element.36.refs_0_), channel_id=1, source_target_pairs={{0,4},{4,0},{8,12},{12,8},{16,20},{20,16},{24,28},{28,24},{1,5},{5... | collective-permute-start | bytes 405512 | tf_op jit(solution)/shard_map/ppermute | solution.py:426
  11.6 1.5 %collective-permute-start.5 = (bf16[528,128]{1,0:T(8,128)(2,1)S(1)}, bf16[528,128]{1,0:T(8,128)(2,1)S(1)}, u32[]{:S(2)}, u32[]{:S(2)}) collective-permute-start(bf16[528,128]{1,0:T(8,128)(2,1)S(1)} %collective-permute-done.1.refs_2_), channel_id=1, source_target_pairs={{0,4},{4,0},{8,12},{12,8},{16,20},{20,16},{24,28},{28,24},{1,5},{5... | collective-permute-start | bytes 405512 | tf_op jit(solution)/shard_map/ppermute | solution.py:426
  14.3 6.5 %collective-permute-start.7 = (s16[272,128]{1,0:T(8,128)(2,1)S(1)}, s16[272,128]{1,0:T(8,128)(2,1)S(1)}, u32[]{:S(2)}, u32[]{:S(2)}) collective-permute-start(s16[272,128]{1,0:T(8,128)(2,1)S(1)} %get-tuple-element.48), channel_id=1, source_target_pairs={{0,1},{1,2},{2,3},{3,0},{4,5},{5,6},{6,7},{7,4},{8,9},{9,10},{10,1... | collective-permute-start | bytes 208904 | tf_op jit(solution)/shard_map/ppermute | solution.py:429
  16.0 7.6 %collective-permute-start.8 = (s16[272,128]{1,0:T(8,128)(2,1)S(1)}, s16[272,128]{1,0:T(8,128)(2,1)S(1)}, u32[]{:S(2)}, u32[]{:S(2)}) collective-permute-start(s16[272,128]{1,0:T(8,128)(2,1)S(1)} %get-tuple-element.49), channel_id=1, source_target_pairs={{0,2},{1,3},{2,0},{3,1},{4,6},{5,7},{6,4},{7,5},{8,10},{9,11},{10,... | collective-permute-start | bytes 208904 | tf_op jit(solution)/shard_map/ppermute | solution.py:429
  18.5 5.3 %collective-permute-start.9 = (s16[272,128]{1,0:T(8,128)(2,1)S(1)}, s16[272,128]{1,0:T(8,128)(2,1)S(1)}, u32[]{:S(2)}, u32[]{:S(2)}) collective-permute-start(s16[272,128]{1,0:T(8,128)(2,1)S(1)} %get-tuple-element.50), channel_id=1, source_target_pairs={{0,3},{1,0},{2,1},{3,2},{4,7},{5,4},{6,5},{7,6},{8,11},{9,8},{10,9... | collective-permute-start | bytes 208904 | tf_op jit(solution)/shard_map/ppermute | solution.py:429
  24.4 5.5 %collective-permute-start.12 = (s16[272,128]{1,0:T(8,128)(2,1)S(1)}, s16[272,128]{1,0:T(8,128)(2,1)S(1)}, u32[]{:S(2)}, u32[]{:S(2)}) collective-permute-start(s16[272,128]{1,0:T(8,128)(2,1)S(1)} %solve_0.1.refs_0_), channel_id=1, source_target_pairs={{0,3},{1,0},{2,1},{3,2},{4,7},{5,4},{6,5},{7,6},{8,11},{9,8},{10,9... | collective-permute-start | bytes 208904 | tf_op jit(solution)/shard_map/ppermute | solution.py:429
  27.3 7.1 %collective-permute-start.11 = (s16[272,128]{1,0:T(8,128)(2,1)S(1)}, s16[272,128]{1,0:T(8,128)(2,1)S(1)}, u32[]{:S(2)}, u32[]{:S(2)}) collective-permute-start(s16[272,128]{1,0:T(8,128)(2,1)S(1)} %solve_0.1.refs_0_), channel_id=1, source_target_pairs={{0,2},{1,3},{2,0},{3,1},{4,6},{5,7},{6,4},{7,5},{8,10},{9,11},{10,... | collective-permute-start | bytes 208904 | tf_op jit(solution)/shard_map/ppermute | solution.py:429
  27.6 6.8 %collective-permute-start.10 = (s16[272,128]{1,0:T(8,128)(2,1)S(1)}, s16[272,128]{1,0:T(8,128)(2,1)S(1)}, u32[]{:S(2)}, u32[]{:S(2)}) collective-permute-start(s16[272,128]{1,0:T(8,128)(2,1)S(1)} %solve_0.1.refs_0_), channel_id=1, source_target_pairs={{0,1},{1,2},{2,3},{3,0},{4,5},{5,6},{6,7},{7,4},{8,9},{9,10},{10,1... | collective-permute-start | bytes 208904 | tf_op jit(solution)/shard_map/ppermute | solution.py:429
  34.5 5.2 %collective-permute-start.13 = (bf16[384,128]{1,0:T(8,128)(2,1)S(1)}, bf16[384,128]{1,0:T(8,128)(2,1)S(1)}, u32[]{:S(2)}, u32[]{:S(2)}) collective-permute-start(bf16[384,128]{1,0:T(8,128)(2,1)S(1)} %get-tuple-element.54), channel_id=1, source_target_pairs={{0,8},{4,12},{8,0},{12,4},{16,24},{20,28},{24,16},{28,20},{1,9},{5... | collective-permute-start | bytes 294920 | tf_op jit(solution)/shard_map/ppermute | solution.py:426
  36.1 6.5 %collective-permute-start.14 = (bf16[384,128]{1,0:T(8,128)(2,1)S(1)}, bf16[384,128]{1,0:T(8,128)(2,1)S(1)}, u32[]{:S(2)}, u32[]{:S(2)}) collective-permute-start(bf16[384,128]{1,0:T(8,128)(2,1)S(1)} %get-tuple-element.55), channel_id=1, source_target_pairs={{0,16},{4,20},{8,24},{12,28},{16,0},{20,4},{24,8},{28,12},{1,17},{... | collective-permute-start | bytes 294920 | tf_op jit(solution)/shard_map/ppermute | solution.py:426
  36.8 6.0 %collective-permute-start.15 = (bf16[384,128]{1,0:T(8,128)(2,1)S(1)}, bf16[384,128]{1,0:T(8,128)(2,1)S(1)}, u32[]{:S(2)}, u32[]{:S(2)}) collective-permute-start(bf16[384,128]{1,0:T(8,128)(2,1)S(1)} %get-tuple-element.56), channel_id=1, source_target_pairs={{0,24},{4,28},{8,16},{12,20},{16,8},{20,12},{24,0},{28,4},{1,25},{... | collective-permute-start | bytes 294920 | tf_op jit(solution)/shard_map/ppermute | solution.py:426
  38.1 4.7 %collective-permute-start.16 = (bf16[384,128]{1,0:T(8,128)(2,1)S(1)}, bf16[384,128]{1,0:T(8,128)(2,1)S(1)}, u32[]{:S(2)}, u32[]{:S(2)}) collective-permute-start(bf16[384,128]{1,0:T(8,128)(2,1)S(1)} %get-tuple-element.57), channel_id=1, source_target_pairs={{0,4},{4,0},{8,12},{12,8},{16,20},{20,16},{24,28},{28,24},{1,5},{5... | collective-permute-start | bytes 294920 | tf_op jit(solution)/shard_map/ppermute | solution.py:426
  38.1 5.0 %collective-permute-start.17 = (bf16[384,128]{1,0:T(8,128)(2,1)S(1)}, bf16[384,128]{1,0:T(8,128)(2,1)S(1)}, u32[]{:S(2)}, u32[]{:S(2)}) collective-permute-start(bf16[384,128]{1,0:T(8,128)(2,1)S(1)} %get-tuple-element.58), channel_id=1, source_target_pairs={{0,12},{4,8},{8,4},{12,0},{16,28},{20,24},{24,20},{28,16},{1,13},{... | collective-permute-start | bytes 294920 | tf_op jit(solution)/shard_map/ppermute | solution.py:426
  39.7 5.0 %collective-permute-start.18 = (bf16[384,128]{1,0:T(8,128)(2,1)S(1)}, bf16[384,128]{1,0:T(8,128)(2,1)S(1)}, u32[]{:S(2)}, u32[]{:S(2)}) collective-permute-start(bf16[384,128]{1,0:T(8,128)(2,1)S(1)} %get-tuple-element.59), channel_id=1, source_target_pairs={{0,20},{4,16},{8,28},{12,24},{16,4},{20,0},{24,12},{28,8},{1,21},{... | collective-permute-start | bytes 294920 | tf_op jit(solution)/shard_map/ppermute | solution.py:426
  42.6 5.1 %collective-permute-start.19 = (bf16[384,128]{1,0:T(8,128)(2,1)S(1)}, bf16[384,128]{1,0:T(8,128)(2,1)S(1)}, u32[]{:S(2)}, u32[]{:S(2)}) collective-permute-start(bf16[384,128]{1,0:T(8,128)(2,1)S(1)} %get-tuple-element.60), channel_id=1, source_target_pairs={{0,28},{4,24},{8,20},{12,16},{16,12},{20,8},{24,4},{28,0},{1,29},{... | collective-permute-start | bytes 294920 | tf_op jit(solution)/shard_map/ppermute | solution.py:426
  48.6 6.7 %collective-permute-start.20 = (s16[272,128]{1,0:T(8,128)(2,1)S(1)}, s16[272,128]{1,0:T(8,128)(2,1)S(1)}, u32[]{:S(2)}, u32[]{:S(2)}) collective-permute-start(s16[272,128]{1,0:T(8,128)(2,1)S(1)} %get-tuple-element.62), channel_id=1, source_target_pairs={{0,1},{1,2},{2,3},{3,0},{4,5},{5,6},{6,7},{7,4},{8,9},{9,10},{10,1... | collective-permute-start | bytes 208904 | tf_op jit(solution)/shard_map/ppermute | solution.py:429
  48.7 8.0 %collective-permute-start.21 = (s16[272,128]{1,0:T(8,128)(2,1)S(1)}, s16[272,128]{1,0:T(8,128)(2,1)S(1)}, u32[]{:S(2)}, u32[]{:S(2)}) collective-permute-start(s16[272,128]{1,0:T(8,128)(2,1)S(1)} %get-tuple-element.63), channel_id=1, source_target_pairs={{0,2},{1,3},{2,0},{3,1},{4,6},{5,7},{6,4},{7,5},{8,10},{9,11},{10,... | collective-permute-start | bytes 208904 | tf_op jit(solution)/shard_map/ppermute | solution.py:429
  50.0 6.7 %collective-permute-start.22 = (s16[272,128]{1,0:T(8,128)(2,1)S(1)}, s16[272,128]{1,0:T(8,128)(2,1)S(1)}, u32[]{:S(2)}, u32[]{:S(2)}) collective-permute-start(s16[272,128]{1,0:T(8,128)(2,1)S(1)} %get-tuple-element.64), channel_id=1, source_target_pairs={{0,3},{1,0},{2,1},{3,2},{4,7},{5,4},{6,5},{7,6},{8,11},{9,8},{10,9... | collective-permute-start | bytes 208904 | tf_op jit(solution)/shard_map/ppermute | solution.py:429
  57.2 4.7 %collective-permute-start.25 = (s16[272,128]{1,0:T(8,128)(2,1)S(1)}, s16[272,128]{1,0:T(8,128)(2,1)S(1)}, u32[]{:S(2)}, u32[]{:S(2)}) collective-permute-start(s16[272,128]{1,0:T(8,128)(2,1)S(1)} %solve_1.1.refs_0_), channel_id=1, source_target_pairs={{0,3},{1,0},{2,1},{3,2},{4,7},{5,4},{6,5},{7,6},{8,11},{9,8},{10,9... | collective-permute-start | bytes 208904 | tf_op jit(solution)/shard_map/ppermute | solution.py:429
  59.9 6.4 %collective-permute-start.24 = (s16[272,128]{1,0:T(8,128)(2,1)S(1)}, s16[272,128]{1,0:T(8,128)(2,1)S(1)}, u32[]{:S(2)}, u32[]{:S(2)}) collective-permute-start(s16[272,128]{1,0:T(8,128)(2,1)S(1)} %solve_1.1.refs_0_), channel_id=1, source_target_pairs={{0,2},{1,3},{2,0},{3,1},{4,6},{5,7},{6,4},{7,5},{8,10},{9,11},{10,... | collective-permute-start | bytes 208904 | tf_op jit(solution)/shard_map/ppermute | solution.py:429
  60.1 6.3 %collective-permute-start.23 = (s16[272,128]{1,0:T(8,128)(2,1)S(1)}, s16[272,128]{1,0:T(8,128)(2,1)S(1)}, u32[]{:S(2)}, u32[]{:S(2)}) collective-permute-start(s16[272,128]{1,0:T(8,128)(2,1)S(1)} %solve_1.1.refs_0_), channel_id=1, source_target_pairs={{0,1},{1,2},{2,3},{3,0},{4,5},{5,6},{6,7},{7,4},{8,9},{9,10},{10,1... | collective-permute-start | bytes 208904 | tf_op jit(solution)/shard_map/ppermute | solution.py:429
  (3 other events, 21.5 us)

commit v4 on v3

--- a/solution.py
+++ b/solution.py
@@ -275,19 +275,17 @@
     )(first_at, *(in_hbm(x) for x in (blocks, right_side, inverse)))
 
 
-def partial_kernel(cols, n_early, probes, idx_ref, blk, *refs):
+def partial_kernel(cols, n_early, probes, places, idx_ref, blk, *refs):
     ins, own_ref, msgs, known = refs[:-cols - 1], refs[-cols - 1], refs[-cols:-1], refs[-1]
     rows_dev, slots, order, _ = blk.shape
     part = rows_dev // cols
     here = lax.axis_index("cols")
-    at = 0
-    for i, ref in enumerate(ins):
+    for i, (ref, at) in enumerate(zip(ins, places)):
         for k in range((ref.shape[0] - (TAIL if i < n_early else 0)) // probes):
-            known[at] = ref[k * probes : (k + 1) * probes]
-            at += 1
-    known[at] = jnp.zeros(known.shape[1:], known.dtype)
+            known[at + k] = ref[k * probes : (k + 1) * probes]
+    known[known.shape[0] - 1] = jnp.zeros(known.shape[1:], known.dtype)
     for s in list(range(1, cols)) + [0]:
-        first = lax.rem(here + s, cols) * part
+        first = (here ^ s) * part
         sums = []
         for k in range(part):
             xs = [known[idx_ref[j, first + k]] for j in range(slots)]
@@ -307,13 +305,13 @@
             encode_blocks(sums, msgs[s - 1], probes)
 
 
-def partial_products(name, cols, probes, idx, blocks, early, recent):
+def partial_products(name, cols, probes, idx, blocks, early, recent, places):
     rows_dev, slots, order, _ = blocks.shape
     part = rows_dev // cols
     rows = sum(a.shape[0] - TAIL for a in early) + sum(a.shape[0] for a in recent)
     msg = jax.ShapeDtypeStruct((part * probes + TAIL, order), I16)
     out = pl.pallas_call(
-        functools.partial(partial_kernel, cols, len(early), probes),
+        functools.partial(partial_kernel, cols, len(early), probes, places),
         out_shape=[jax.ShapeDtypeStruct((part, probes, order), F32)] + [msg] * (cols - 1),
         in_specs=[SMEM] + [VMEM] * (len(early) + len(recent) + 1),
         out_specs=[VMEM] * cols,
@@ -355,26 +353,27 @@
     )(own, *msgs, rhs, inverse)
 
 
-def pack_kernel(cols, groups, cap, sel_ref, *refs):
+def pack_kernel(sources, groups, cap, sel_ref, *refs):
+    cols = len(sources)
     msgs, sends, rows = refs[:cols], refs[cols:-1], refs[-1]
     rows_dev, probes, _ = rows.shape
     part = rows_dev // cols
     here = lax.axis_index("cols")
-    for s in range(cols):
-        first = lax.rem(here + cols - s, cols) * part
-        for k, value in enumerate(decode_blocks(msgs[s], part, probes)):
+    for mask, msg in zip(sources, msgs):
+        first = (here ^ mask) * part
+        for k, value in enumerate(decode_blocks(msg, part, probes)):
             rows[first + k] = value.astype(BF16)
     for m in range(groups):
         for q in range(cap):
             sends[m][q * probes : (q + 1) * probes] = rows[sel_ref[q, m * rows_dev]]
 
 
-def pack(cols, groups, cap, sel, msgs, shape):
+def pack(sources, groups, cap, sel, msgs, shape):
     rows_dev, probes, order = shape
     return pl.pallas_call(
-        functools.partial(pack_kernel, cols, groups, cap),
+        functools.partial(pack_kernel, sources, groups, cap),
         out_shape=[jax.ShapeDtypeStruct((cap * probes, order), BF16)] * groups,
-        in_specs=[SMEM] + [VMEM] * cols,
+        in_specs=[SMEM] + [VMEM] * len(msgs),
         out_specs=[VMEM] * groups,
         scratch_shapes=[pltpu.VMEM((rows_dev, probes, order), BF16)],
         compiler_params=PARAMS,
@@ -382,27 +381,27 @@
     )(in_smem(sel), *msgs)
 
 
-def unpack_kernel(front, cols, *refs):
-    msgs, out_ref, rows, sems = refs[:cols], refs[-3], refs[-2], refs[-1]
+def unpack_kernel(front, sources, *refs):
+    msgs, out_ref, rows, sems = refs[: len(sources)], refs[-3], refs[-2], refs[-1]
     part, probes, _ = rows.shape[1:]
     here = lax.axis_index("cols")
     copies = []
-    for s in range(cols):
-        first = lax.rem(here + cols - s, cols) * part
-        for k, value in enumerate(decode_blocks(msgs[s], part, probes)):
+    for s, (mask, msg) in enumerate(zip(sources, msgs)):
+        for k, value in enumerate(decode_blocks(msg, part, probes)):
             rows[s, k] = value
-        copy = pltpu.make_async_copy(rows.at[s], out_ref.at[front, pl.ds(first, part)], sems.at[s])
-        copy.start()
-        copies.append(copy)
+        to = out_ref.at[front, pl.ds((here ^ mask) * part, part)]
+        copies.append(pltpu.make_async_copy(rows.at[s], to, sems.at[s]))
+        copies[-1].start()
     for copy in copies:
         copy.wait()
 
 
-def unpack(front, cols, msgs, shape, base=None):
+def unpack(front, sources, msgs, shape, base=None):
     _, rows_dev, probes, order = shape
+    cols = len(sources)
     rest = [] if base is None else [base]
     return pl.pallas_call(
-        functools.partial(unpack_kernel, front, cols),
+        functools.partial(unpack_kernel, front, sources),
         out_shape=jax.ShapeDtypeStruct(shape, F32),
         in_specs=[VMEM] * cols + [HBM] * len(rest),
         out_specs=HBM,
@@ -425,34 +424,49 @@
     def over_rows(x, mask):
         return lax.ppermute(x, "rows", [(i, i ^ mask) for i in range(groups)])
 
-    def over_cols(x, step):
-        return lax.ppermute(x, "cols", [(i, (i + step) % cols) for i in range(cols)])
+    def over_cols(x, mask):
+        return lax.ppermute(x, "cols", [(i, i ^ mask) for i in range(cols)])
+
+    col_order = list(range(cols - 1, 0, -2)) + list(range(cols - 2, 0, -2))
+    row_order = list(range(2, groups, 2)) + list(range(3, groups, 2)) + [1]
+
+    def scatter(xs):
+        return [over_cols(xs[m - 1], m) for m in col_order]
+
+    def gather(x):
+        masks = [0] + col_order[::-1]
+        return masks, [over_cols(x, m) if m else x for m in masks]
 
     own, first_at, alive = start(groups, colidx, live, prior)
-    chips = [over_rows(own, 2 * k) for k in range(1, half)]
+    peers = [m for m in row_order if m % 2 == 0][::-1]
+    chips = [over_rows(own, m) for m in peers]
     blocks0, blocks1, rhs, inverse, first_at = load(
         cols, first_at, blocks, right_side, diag_inverse
     )
     chips, blocks0 = lax.optimization_barrier((chips, blocks0))
-    pieces = [own] + chips
-    pieces += [over_rows(x, 1) for x in pieces]
+    chips = [own] + [chips[peers.index(2 * k)] for k in range(1, half)]
+    pieces = chips + [over_rows(x, 1) for x in chips]
+    early_at = [g * prior_dev for g in range(groups)]
     want, second_at = route(groups, cap, slots, prior_dev, owner_map, alive, pieces)
 
-    own0, msgs0 = partial_products("partial_0", cols, probes, first_at, blocks0, pieces, [])
-    got0 = [over_cols(m, s + 1) for s, m in enumerate(msgs0)]
-    coded0 = solve_part(0, cols, own0, got0, rhs, inverse)
-    all0 = [coded0] + [over_cols(coded0, s) for s in range(1, cols)]
-
-    sends = pack(cols, groups, cap, want, all0, right_side.shape[1:])
-    masks = [2 * k for k in range(half)] + [2 * k + 1 for k in range(half)]
-    recent = [x if m == 0 else over_rows(x, m) for m, x in zip(masks, sends)]
-    solved = unpack(0, cols, all0, right_side.shape)
-
-    own1, msgs1 = partial_products("partial_1", cols, probes, second_at, blocks1, pieces, recent)
-    got1 = [over_cols(m, s + 1) for s, m in enumerate(msgs1)]
-    coded1 = solve_part(1, cols, own1, got1, rhs, inverse)
-    all1 = [coded1] + [over_cols(coded1, s) for s in range(1, cols)]
-    return unpack(1, cols, all1, right_side.shape, solved)
+    own0, msgs0 = partial_products(
+        "partial_0", cols, probes, first_at, blocks0, pieces, [], early_at
+    )
+    coded0 = solve_part(0, cols, own0, scatter(msgs0), rhs, inverse)
+    sources, all0 = gather(coded0)
+
+    place = {m: (m & 1) * half + (m >> 1) for m in range(groups)}
+    sends = pack(sources, groups, cap, want, all0, right_side.shape[1:])
+    recent = [sends[0]] + [over_rows(sends[place[m]], m) for m in row_order]
+    recent_at = [groups * prior_dev + place[m] * cap for m in [0] + row_order]
+    solved = unpack(0, sources, all0, right_side.shape)
+
+    own1, msgs1 = partial_products(
+        "partial_1", cols, probes, second_at, blocks1, pieces, recent, early_at + recent_at
+    )
+    coded1 = solve_part(1, cols, own1, scatter(msgs1), rhs, inverse)
+    sources, all1 = gather(coded1)
+    return unpack(1, sources, all1, right_side.shape, solved)
 
 
 def solution(mesh):

time: 67.3 us -> 65 us (0.966)
  waiting for transfers between devices: 29 us -> 24.1 us
  starting transfers between devices: 27.5 us -> 30 us
    ppermute x14, waiting for transfers between devices: 11.4 us -> 8.74 us  [over_rows(): return lax.ppermute(x, 'rows', [(i, i ^ mask) for i in range(groups)])]
    ppermute x12, waiting for transfers between devices: 17.5 us -> 15.3 us  [over_cols(): return lax.ppermute(x, 'cols', [(i, i ^ mask) for i in range(cols)])]
    ppermute x14, starting transfers between devices: 10.8 us -> 12.2 us  [over_rows(): return lax.ppermute(x, 'rows', [(i, i ^ mask) for i in range(groups)])]
    ppermute x12, starting transfers between devices: 16.7 us -> 17.8 us  [over_cols(): return lax.ppermute(x, 'cols', [(i, i ^ mask) for i in range(cols)])]
  transfers between devices with their start and end apart: 26 -> 26, of which waited for: 18 -> 21; matrix products, arithmetic and copies ran while one was open for 0% -> 0% of each run, Pallas kernels for 9% -> 9%
where the time goes in v4:
time: 65 us; the launch traced here: 64.9 us
  starting transfers between devices  30 us (46%)
  waiting for transfers between devices  24.1 us (37%)
  Pallas kernels  10.6 us (16%)
    ppermute x12, starting transfers between devices, over_cols(): return lax.ppermute(x, 'cols', [(i, i ^ mask) for i in range(cols)])  17.8 us
    ppermute x12, waiting for transfers between devices, over_cols(): return lax.ppermute(x, 'cols', [(i, i ^ mask) for i in range(cols)])  15.3 us
    ppermute x14, starting transfers between devices, over_rows(): return lax.ppermute(x, 'rows', [(i, i ^ mask) for i in range(groups)])  12.2 us
    ppermute x14, waiting for transfers between devices, over_rows(): return lax.ppermute(x, 'rows', [(i, i ^ mask) for i in range(groups)])  8.74 us
    pallas_call x1, Pallas kernels, load(): pl.pallas_call(functools.partial(load_kernel, cols), out_shape=[pltpu.VME...  3.51 us
    pallas_call x2, Pallas kernels, partial_products(): pl.pallas_call(functools.partial(partial_kernel, cols, len(early), probes...  1.73 us
    pallas_call x2, Pallas kernels, unpack(): pl.pallas_call(functools.partial(unpack_kernel, front, sources), out_shap...  1.68 us
    pallas_call x1, Pallas kernels, route(): pl.pallas_call(functools.partial(route_kernel, groups, cap, slots, prior_...  1.62 us
  transfers between devices with their start and end apart: 26, of which 21 were waited for; matrix products, arithmetic and copies ran while one was open for 0% of the time, Pallas kernels for 9%

profile of v4, /device:TPU:0, one launch (start us, length us, event | category | flops | bytes accessed | tf_op | source)
XLA Modules:
  0.0 64.9 jit_solution(13341847334847991962)
XLA Ops:
  0.9 3.0 %collective-permute-start.2 = (bf16[528,128]{1,0:T(8,128)(2,1)S(1)}, bf16[528,128]{1,0:T(8,128)(2,1)S(1)}, u32[]{:S(2)}, u32[]{:S(2)}) collective-permute-start(bf16[528,128]{1,0:T(8,128)(2,1)S(1)} %get-tuple-element.36.refs_0_), channel_id=1, source_target_pairs={{0,8},{4,12},{8,0},{12,4},{16,24},{20,28},{24,16},{28,20},{1,9},{5... | collective-permute-start | bytes 405512 | tf_op jit(solution)/shard_map/ppermute | solution.py:425
  3.9 1.5 %collective-permute-start.1 = (bf16[528,128]{1,0:T(8,128)(2,1)S(1)}, bf16[528,128]{1,0:T(8,128)(2,1)S(1)}, u32[]{:S(2)}, u32[]{:S(2)}) collective-permute-start(bf16[528,128]{1,0:T(8,128)(2,1)S(1)} %get-tuple-element.36.refs_0_), channel_id=1, source_target_pairs={{0,16},{4,20},{8,24},{12,28},{16,0},{20,4},{24,8},{28,12},{1,17},{... | collective-permute-start | bytes 405512 | tf_op jit(solution)/shard_map/ppermute | solution.py:425
  5.5 3.5 %load.1 = (bf16[16,6,128,128]{3,2,1,0:T(8,128)(2,1)S(1)}, bf16[16,6,128,128]{3,2,1,0:T(8,128)(2,1)S(1)}, f32[2,4,64,128]{3,2,1,0:T(8,128)S(1)}, f32[2,4,128,128]{3,2,1,0:T(8,128)S(1)}, s32[8,128]{1,0:T(8,128)S(4)}) custom-call(s32[8,128]{1,0:T(8,128)S(1)} %get-tuple-element.37.first_at, bf16[2,16,6,128,128]{4,3,2,1,0:T(8,128)(2,1)} %blocks.1, ...), custom_call_target="tpu_custom_call" | custom-call | bytes 12582912 | tf_op jit(solution)/shard_map/load/pallas_call | solution.py:259
  9.0 2.9 %collective-permute-done.1.refs_2_ = bf16[528,128]{1,0:T(8,128)(2,1)S(1)} collective-permute-done((bf16[528,128]{1,0:T(8,128)(2,1)S(1)}, bf16[528,128]{1,0:T(8,128)(2,1)S(1)}, u32[]{:S(2)}, u32[]{:S(2)}) %collective-permute-start.1) | collective-permute-done | bytes 135200 | tf_op jit(solution)/shard_map/ppermute | solution.py:425
  14.6 3.7 %collective-permute-start.7 = (s16[272,128]{1,0:T(8,128)(2,1)S(1)}, s16[272,128]{1,0:T(8,128)(2,1)S(1)}, u32[]{:S(2)}, u32[]{:S(2)}) collective-permute-start(s16[272,128]{1,0:T(8,128)(2,1)S(1)} %get-tuple-element.48), channel_id=1, source_target_pairs={{0,3},{1,2},{2,1},{3,0},{4,7},{5,6},{6,5},{7,4},{8,11},{9,10},{10,... | collective-permute-start | bytes 208904 | tf_op jit(solution)/shard_map/ppermute | solution.py:428
  19.0 2.4 %collective-permute-done.7.refs_0_ = s16[272,128]{1,0:T(8,128)(2,1)S(1)} collective-permute-done((s16[272,128]{1,0:T(8,128)(2,1)S(1)}, s16[272,128]{1,0:T(8,128)(2,1)S(1)}, u32[]{:S(2)}, u32[]{:S(2)}) %collective-permute-start.7) | collective-permute-done | bytes 69664 | tf_op jit(solution)/shard_map/ppermute | solution.py:428
  21.5 2.1 %collective-permute-done.8.refs_1_ = s16[272,128]{1,0:T(8,128)(2,1)S(1)} collective-permute-done((s16[272,128]{1,0:T(8,128)(2,1)S(1)}, s16[272,128]{1,0:T(8,128)(2,1)S(1)}, u32[]{:S(2)}, u32[]{:S(2)}) %collective-permute-start.8) | collective-permute-done | bytes 69664 | tf_op jit(solution)/shard_map/ppermute | solution.py:428
  24.8 2.4 %collective-permute-start.12 = (s16[272,128]{1,0:T(8,128)(2,1)S(1)}, s16[272,128]{1,0:T(8,128)(2,1)S(1)}, u32[]{:S(2)}, u32[]{:S(2)}) collective-permute-start(s16[272,128]{1,0:T(8,128)(2,1)S(1)} %solve_0.1.refs_0_), channel_id=1, source_target_pairs={{0,3},{1,2},{2,1},{3,0},{4,7},{5,6},{6,5},{7,4},{8,11},{9,10},{10,... | collective-permute-start | bytes 208904 | tf_op jit(solution)/shard_map/ppermute | solution.py:428
  27.6 1.6 %collective-permute-start.10 = (s16[272,128]{1,0:T(8,128)(2,1)S(1)}, s16[272,128]{1,0:T(8,128)(2,1)S(1)}, u32[]{:S(2)}, u32[]{:S(2)}) collective-permute-start(s16[272,128]{1,0:T(8,128)(2,1)S(1)} %solve_0.1.refs_0_), channel_id=1, source_target_pairs={{0,2},{1,3},{2,0},{3,1},{4,6},{5,7},{6,4},{7,5},{8,10},{9,11},{10,... | collective-permute-start | bytes 208904 | tf_op jit(solution)/shard_map/ppermute | solution.py:428
  29.2 1.6 %route.1 = (s32[8,128]{1,0:T(8,128)S(4)}, s32[8,128]{1,0:T(8,128)S(4)}) custom-call(s32[2,128]{1,0:T(2,128)S(1)} %copy-done, s32[8,128]{1,0:T(8,128)S(1)} %get-tuple-element.35.alive_ref, bf16[528,128]{1,0:T(8,128)(2,1)S(1)} %get-tuple-element.36.refs_0_, bf16[528,128]{1,0:T(8,128)(2,1)S(1)} %collective-permute-done.2.refs_1_, ...), custom_call_target="tpu_custom_call" | custom-call | tf_op jit(solution)/shard_map/route/pallas_call | solution.py:203
  31.1 1.2 %collective-permute-done.11.refs_2_ = s16[272,128]{1,0:T(8,128)(2,1)S(1)} collective-permute-done((s16[272,128]{1,0:T(8,128)(2,1)S(1)}, s16[272,128]{1,0:T(8,128)(2,1)S(1)}, u32[]{:S(2)}, u32[]{:S(2)}) %collective-permute-start.11) | collective-permute-done | bytes 69664 | tf_op jit(solution)/shard_map/ppermute | solution.py:428
  33.2 1.3 %collective-permute-start.13 = (bf16[384,128]{1,0:T(8,128)(2,1)S(1)}, bf16[384,128]{1,0:T(8,128)(2,1)S(1)}, u32[]{:S(2)}, u32[]{:S(2)}) collective-permute-start(bf16[384,128]{1,0:T(8,128)(2,1)S(1)} %get-tuple-element.54), channel_id=1, source_target_pairs={{0,8},{4,12},{8,0},{12,4},{16,24},{20,28},{24,16},{28,20},{1,9},{5... | collective-permute-start | bytes 294920 | tf_op jit(solution)/shard_map/ppermute | solution.py:425
  35.3 1.4 %collective-permute-start.15 = (bf16[384,128]{1,0:T(8,128)(2,1)S(1)}, bf16[384,128]{1,0:T(8,128)(2,1)S(1)}, u32[]{:S(2)}, u32[]{:S(2)}) collective-permute-start(bf16[384,128]{1,0:T(8,128)(2,1)S(1)} %get-tuple-element.56), channel_id=1, source_target_pairs={{0,24},{4,28},{8,16},{12,20},{16,8},{20,12},{24,0},{28,4},{1,25},{... | collective-permute-start | bytes 294920 | tf_op jit(solution)/shard_map/ppermute | solution.py:425
  36.7 1.8 %collective-permute-start.17 = (bf16[384,128]{1,0:T(8,128)(2,1)S(1)}, bf16[384,128]{1,0:T(8,128)(2,1)S(1)}, u32[]{:S(2)}, u32[]{:S(2)}) collective-permute-start(bf16[384,128]{1,0:T(8,128)(2,1)S(1)} %get-tuple-element.58), channel_id=1, source_target_pairs={{0,20},{4,16},{8,28},{12,24},{16,4},{20,0},{24,12},{28,8},{1,21},{... | collective-permute-start | bytes 294920 | tf_op jit(solution)/shard_map/ppermute | solution.py:425
  39.4 1.0 %collective-permute-start.19 = (bf16[384,128]{1,0:T(8,128)(2,1)S(1)}, bf16[384,128]{1,0:T(8,128)(2,1)S(1)}, u32[]{:S(2)}, u32[]{:S(2)}) collective-permute-start(bf16[384,128]{1,0:T(8,128)(2,1)S(1)} %get-tuple-element.60), channel_id=1, source_target_pairs={{0,4},{4,0},{8,12},{12,8},{16,20},{20,16},{24,28},{28,24},{1,5},{5... | collective-permute-start | bytes 294920 | tf_op jit(solution)/shard_map/ppermute | solution.py:425
  42.4 2.5 %collective-permute-done.18.refs_14_ = bf16[384,128]{1,0:T(8,128)(2,1)S(1)} collective-permute-done((bf16[384,128]{1,0:T(8,128)(2,1)S(1)}, bf16[384,128]{1,0:T(8,128)(2,1)S(1)}, u32[]{:S(2)}, u32[]{:S(2)}) %collective-permute-start.18) | collective-permute-done | bytes 98336 | tf_op jit(solution)/shard_map/ppermute | solution.py:425
  45.8 3.3 %collective-permute-start.20 = (s16[272,128]{1,0:T(8,128)(2,1)S(1)}, s16[272,128]{1,0:T(8,128)(2,1)S(1)}, u32[]{:S(2)}, u32[]{:S(2)}) collective-permute-start(s16[272,128]{1,0:T(8,128)(2,1)S(1)} %get-tuple-element.62), channel_id=1, source_target_pairs={{0,3},{1,2},{2,1},{3,0},{4,7},{5,6},{6,5},{7,4},{8,11},{9,10},{10,... | collective-permute-start | bytes 208904 | tf_op jit(solution)/shard_map/ppermute | solution.py:428
  49.1 1.1 %collective-permute-start.22 = (s16[272,128]{1,0:T(8,128)(2,1)S(1)}, s16[272,128]{1,0:T(8,128)(2,1)S(1)}, u32[]{:S(2)}, u32[]{:S(2)}) collective-permute-start(s16[272,128]{1,0:T(8,128)(2,1)S(1)} %get-tuple-element.64), channel_id=1, source_target_pairs={{0,2},{1,3},{2,0},{3,1},{4,6},{5,7},{6,4},{7,5},{8,10},{9,11},{10,... | collective-permute-start | bytes 208904 | tf_op jit(solution)/shard_map/ppermute | solution.py:428
  50.2 2.5 %collective-permute-done.20.refs_0_ = s16[272,128]{1,0:T(8,128)(2,1)S(1)} collective-permute-done((s16[272,128]{1,0:T(8,128)(2,1)S(1)}, s16[272,128]{1,0:T(8,128)(2,1)S(1)}, u32[]{:S(2)}, u32[]{:S(2)}) %collective-permute-start.20) | collective-permute-done | bytes 69664 | tf_op jit(solution)/shard_map/ppermute | solution.py:428
  52.7 1.8 %collective-permute-done.21.refs_1_ = s16[272,128]{1,0:T(8,128)(2,1)S(1)} collective-permute-done((s16[272,128]{1,0:T(8,128)(2,1)S(1)}, s16[272,128]{1,0:T(8,128)(2,1)S(1)}, u32[]{:S(2)}, u32[]{:S(2)}) %collective-permute-start.21) | collective-permute-done | bytes 69664 | tf_op jit(solution)/shard_map/ppermute | solution.py:428
  55.6 3.1 %collective-permute-start.25 = (s16[272,128]{1,0:T(8,128)(2,1)S(1)}, s16[272,128]{1,0:T(8,128)(2,1)S(1)}, u32[]{:S(2)}, u32[]{:S(2)}) collective-permute-start(s16[272,128]{1,0:T(8,128)(2,1)S(1)} %solve_1.1.refs_0_), channel_id=1, source_target_pairs={{0,3},{1,2},{2,1},{3,0},{4,7},{5,6},{6,5},{7,4},{8,11},{9,10},{10,... | collective-permute-start | bytes 208904 | tf_op jit(solution)/shard_map/ppermute | solution.py:428
  58.7 1.4 %collective-permute-start.23 = (s16[272,128]{1,0:T(8,128)(2,1)S(1)}, s16[272,128]{1,0:T(8,128)(2,1)S(1)}, u32[]{:S(2)}, u32[]{:S(2)}) collective-permute-start(s16[272,128]{1,0:T(8,128)(2,1)S(1)} %solve_1.1.refs_0_), channel_id=1, source_target_pairs={{0,2},{1,3},{2,0},{3,1},{4,6},{5,7},{6,4},{7,5},{8,10},{9,11},{10,... | collective-permute-start | bytes 208904 | tf_op jit(solution)/shard_map/ppermute | solution.py:428
  60.9 1.0 %collective-permute-done.25.refs_3_ = s16[272,128]{1,0:T(8,128)(2,1)S(1)} collective-permute-done((s16[272,128]{1,0:T(8,128)(2,1)S(1)}, s16[272,128]{1,0:T(8,128)(2,1)S(1)}, u32[]{:S(2)}, u32[]{:S(2)}) %collective-permute-start.25) | collective-permute-done | bytes 69664 | tf_op jit(solution)/shard_map/ppermute | solution.py:428
  61.9 1.3 %collective-permute-done.24.refs_2_ = s16[272,128]{1,0:T(8,128)(2,1)S(1)} collective-permute-done((s16[272,128]{1,0:T(8,128)(2,1)S(1)}, s16[272,128]{1,0:T(8,128)(2,1)S(1)}, u32[]{:S(2)}, u32[]{:S(2)}) %collective-permute-start.24) | collective-permute-done | bytes 69664 | tf_op jit(solution)/shard_map/ppermute | solution.py:428
  (40 shorter events, 15.5 us)
Async XLA Ops:
  0.9 8.1 %collective-permute-start.2 = (bf16[528,128]{1,0:T(8,128)(2,1)S(1)}, bf16[528,128]{1,0:T(8,128)(2,1)S(1)}, u32[]{:S(2)}, u32[]{:S(2)}) collective-permute-start(bf16[528,128]{1,0:T(8,128)(2,1)S(1)} %get-tuple-element.36.refs_0_), channel_id=1, source_target_pairs={{0,8},{4,12},{8,0},{12,4},{16,24},{20,28},{24,16},{28,20},{1,9},{5... | collective-permute-start | bytes 405512 | tf_op jit(solution)/shard_map/ppermute | solution.py:425
  3.9 7.9 %collective-permute-start.1 = (bf16[528,128]{1,0:T(8,128)(2,1)S(1)}, bf16[528,128]{1,0:T(8,128)(2,1)S(1)}, u32[]{:S(2)}, u32[]{:S(2)}) collective-permute-start(bf16[528,128]{1,0:T(8,128)(2,1)S(1)} %get-tuple-element.36.refs_0_), channel_id=1, source_target_pairs={{0,16},{4,20},{8,24},{12,28},{16,0},{20,4},{24,8},{28,12},{1,17},{... | collective-permute-start | bytes 405512 | tf_op jit(solution)/shard_map/ppermute | solution.py:425
  5.5 6.4 %collective-permute-start = (bf16[528,128]{1,0:T(8,128)(2,1)S(1)}, bf16[528,128]{1,0:T(8,128)(2,1)S(1)}, u32[]{:S(2)}, u32[]{:S(2)}) collective-permute-start(bf16[528,128]{1,0:T(8,128)(2,1)S(1)} %get-tuple-element.36.refs_0_), channel_id=1, source_target_pairs={{0,24},{4,28},{8,16},{12,20},{16,8},{20,12},{24,0},{28,4},{1,25},{... | collective-permute-start | bytes 405512 | tf_op jit(solution)/shard_map/ppermute | solution.py:425
  5.5 6.9 %collective-permute-start.3 = (bf16[528,128]{1,0:T(8,128)(2,1)S(1)}, bf16[528,128]{1,0:T(8,128)(2,1)S(1)}, u32[]{:S(2)}, u32[]{:S(2)}) collective-permute-start(bf16[528,128]{1,0:T(8,128)(2,1)S(1)} %get-tuple-element.36.refs_0_), channel_id=1, source_target_pairs={{0,4},{4,0},{8,12},{12,8},{16,20},{20,16},{24,28},{28,24},{1,5},{5... | collective-permute-start | bytes 405512 | tf_op jit(solution)/shard_map/ppermute | solution.py:425
  11.9 1.5 %collective-permute-start.5 = (bf16[528,128]{1,0:T(8,128)(2,1)S(1)}, bf16[528,128]{1,0:T(8,128)(2,1)S(1)}, u32[]{:S(2)}, u32[]{:S(2)}) collective-permute-start(bf16[528,128]{1,0:T(8,128)(2,1)S(1)} %collective-permute-done.1.refs_2_), channel_id=1, source_target_pairs={{0,4},{4,0},{8,12},{12,8},{16,20},{20,16},{24,28},{28,24},{1,5},{5... | collective-permute-start | bytes 405512 | tf_op jit(solution)/shard_map/ppermute | solution.py:425
  14.6 6.9 %collective-permute-start.7 = (s16[272,128]{1,0:T(8,128)(2,1)S(1)}, s16[272,128]{1,0:T(8,128)(2,1)S(1)}, u32[]{:S(2)}, u32[]{:S(2)}) collective-permute-start(s16[272,128]{1,0:T(8,128)(2,1)S(1)} %get-tuple-element.48), channel_id=1, source_target_pairs={{0,3},{1,2},{2,1},{3,0},{4,7},{5,6},{6,5},{7,4},{8,11},{9,10},{10,... | collective-permute-start | bytes 208904 | tf_op jit(solution)/shard_map/ppermute | solution.py:428
  18.3 5.3 %collective-permute-start.8 = (s16[272,128]{1,0:T(8,128)(2,1)S(1)}, s16[272,128]{1,0:T(8,128)(2,1)S(1)}, u32[]{:S(2)}, u32[]{:S(2)}) collective-permute-start(s16[272,128]{1,0:T(8,128)(2,1)S(1)} %get-tuple-element.49), channel_id=1, source_target_pairs={{0,1},{1,0},{2,3},{3,2},{4,5},{5,4},{6,7},{7,6},{8,9},{9,8},{10,11... | collective-permute-start | bytes 208904 | tf_op jit(solution)/shard_map/ppermute | solution.py:428
  18.3 6.0 %collective-permute-start.9 = (s16[272,128]{1,0:T(8,128)(2,1)S(1)}, s16[272,128]{1,0:T(8,128)(2,1)S(1)}, u32[]{:S(2)}, u32[]{:S(2)}) collective-permute-start(s16[272,128]{1,0:T(8,128)(2,1)S(1)} %get-tuple-element.50), channel_id=1, source_target_pairs={{0,2},{1,3},{2,0},{3,1},{4,6},{5,7},{6,4},{7,5},{8,10},{9,11},{10,... | collective-permute-start | bytes 208904 | tf_op jit(solution)/shard_map/ppermute | solution.py:428
  24.8 6.3 %collective-permute-start.12 = (s16[272,128]{1,0:T(8,128)(2,1)S(1)}, s16[272,128]{1,0:T(8,128)(2,1)S(1)}, u32[]{:S(2)}, u32[]{:S(2)}) collective-permute-start(s16[272,128]{1,0:T(8,128)(2,1)S(1)} %solve_0.1.refs_0_), channel_id=1, source_target_pairs={{0,3},{1,2},{2,1},{3,0},{4,7},{5,6},{6,5},{7,4},{8,11},{9,10},{10,... | collective-permute-start | bytes 208904 | tf_op jit(solution)/shard_map/ppermute | solution.py:428
  27.2 5.1 %collective-permute-start.11 = (s16[272,128]{1,0:T(8,128)(2,1)S(1)}, s16[272,128]{1,0:T(8,128)(2,1)S(1)}, u32[]{:S(2)}, u32[]{:S(2)}) collective-permute-start(s16[272,128]{1,0:T(8,128)(2,1)S(1)} %solve_0.1.refs_0_), channel_id=1, source_target_pairs={{0,1},{1,0},{2,3},{3,2},{4,5},{5,4},{6,7},{7,6},{8,9},{9,8},{10,11... | collective-permute-start | bytes 208904 | tf_op jit(solution)/shard_map/ppermute | solution.py:428
  27.6 5.5 %collective-permute-start.10 = (s16[272,128]{1,0:T(8,128)(2,1)S(1)}, s16[272,128]{1,0:T(8,128)(2,1)S(1)}, u32[]{:S(2)}, u32[]{:S(2)}) collective-permute-start(s16[272,128]{1,0:T(8,128)(2,1)S(1)} %solve_0.1.refs_0_), channel_id=1, source_target_pairs={{0,2},{1,3},{2,0},{3,1},{4,6},{5,7},{6,4},{7,5},{8,10},{9,11},{10,... | collective-permute-start | bytes 208904 | tf_op jit(solution)/shard_map/ppermute | solution.py:428
  33.2 5.4 %collective-permute-start.13 = (bf16[384,128]{1,0:T(8,128)(2,1)S(1)}, bf16[384,128]{1,0:T(8,128)(2,1)S(1)}, u32[]{:S(2)}, u32[]{:S(2)}) collective-permute-start(bf16[384,128]{1,0:T(8,128)(2,1)S(1)} %get-tuple-element.54), channel_id=1, source_target_pairs={{0,8},{4,12},{8,0},{12,4},{16,24},{20,28},{24,16},{28,20},{1,9},{5... | collective-permute-start | bytes 294920 | tf_op jit(solution)/shard_map/ppermute | solution.py:425
  34.5 5.0 %collective-permute-start.14 = (bf16[384,128]{1,0:T(8,128)(2,1)S(1)}, bf16[384,128]{1,0:T(8,128)(2,1)S(1)}, u32[]{:S(2)}, u32[]{:S(2)}) collective-permute-start(bf16[384,128]{1,0:T(8,128)(2,1)S(1)} %get-tuple-element.55), channel_id=1, source_target_pairs={{0,16},{4,20},{8,24},{12,28},{16,0},{20,4},{24,8},{28,12},{1,17},{... | collective-permute-start | bytes 294920 | tf_op jit(solution)/shard_map/ppermute | solution.py:425
  35.3 5.7 %collective-permute-start.15 = (bf16[384,128]{1,0:T(8,128)(2,1)S(1)}, bf16[384,128]{1,0:T(8,128)(2,1)S(1)}, u32[]{:S(2)}, u32[]{:S(2)}) collective-permute-start(bf16[384,128]{1,0:T(8,128)(2,1)S(1)} %get-tuple-element.56), channel_id=1, source_target_pairs={{0,24},{4,28},{8,16},{12,20},{16,8},{20,12},{24,0},{28,4},{1,25},{... | collective-permute-start | bytes 294920 | tf_op jit(solution)/shard_map/ppermute | solution.py:425
  36.7 5.1 %collective-permute-start.16 = (bf16[384,128]{1,0:T(8,128)(2,1)S(1)}, bf16[384,128]{1,0:T(8,128)(2,1)S(1)}, u32[]{:S(2)}, u32[]{:S(2)}) collective-permute-start(bf16[384,128]{1,0:T(8,128)(2,1)S(1)} %get-tuple-element.57), channel_id=1, source_target_pairs={{0,12},{4,8},{8,4},{12,0},{16,28},{20,24},{24,20},{28,16},{1,13},{... | collective-permute-start | bytes 294920 | tf_op jit(solution)/shard_map/ppermute | solution.py:425
  36.7 5.7 %collective-permute-start.17 = (bf16[384,128]{1,0:T(8,128)(2,1)S(1)}, bf16[384,128]{1,0:T(8,128)(2,1)S(1)}, u32[]{:S(2)}, u32[]{:S(2)}) collective-permute-start(bf16[384,128]{1,0:T(8,128)(2,1)S(1)} %get-tuple-element.58), channel_id=1, source_target_pairs={{0,20},{4,16},{8,28},{12,24},{16,4},{20,0},{24,12},{28,8},{1,21},{... | collective-permute-start | bytes 294920 | tf_op jit(solution)/shard_map/ppermute | solution.py:425
  38.6 6.3 %collective-permute-start.18 = (bf16[384,128]{1,0:T(8,128)(2,1)S(1)}, bf16[384,128]{1,0:T(8,128)(2,1)S(1)}, u32[]{:S(2)}, u32[]{:S(2)}) collective-permute-start(bf16[384,128]{1,0:T(8,128)(2,1)S(1)} %get-tuple-element.59), channel_id=1, source_target_pairs={{0,28},{4,24},{8,20},{12,16},{16,12},{20,8},{24,4},{28,0},{1,29},{... | collective-permute-start | bytes 294920 | tf_op jit(solution)/shard_map/ppermute | solution.py:425
  39.4 5.4 %collective-permute-start.19 = (bf16[384,128]{1,0:T(8,128)(2,1)S(1)}, bf16[384,128]{1,0:T(8,128)(2,1)S(1)}, u32[]{:S(2)}, u32[]{:S(2)}) collective-permute-start(bf16[384,128]{1,0:T(8,128)(2,1)S(1)} %get-tuple-element.60), channel_id=1, source_target_pairs={{0,4},{4,0},{8,12},{12,8},{16,20},{20,16},{24,28},{28,24},{1,5},{5... | collective-permute-start | bytes 294920 | tf_op jit(solution)/shard_map/ppermute | solution.py:425
  45.8 6.9 %collective-permute-start.20 = (s16[272,128]{1,0:T(8,128)(2,1)S(1)}, s16[272,128]{1,0:T(8,128)(2,1)S(1)}, u32[]{:S(2)}, u32[]{:S(2)}) collective-permute-start(s16[272,128]{1,0:T(8,128)(2,1)S(1)} %get-tuple-element.62), channel_id=1, source_target_pairs={{0,3},{1,2},{2,1},{3,0},{4,7},{5,6},{6,5},{7,4},{8,11},{9,10},{10,... | collective-permute-start | bytes 208904 | tf_op jit(solution)/shard_map/ppermute | solution.py:428
  49.1 5.4 %collective-permute-start.21 = (s16[272,128]{1,0:T(8,128)(2,1)S(1)}, s16[272,128]{1,0:T(8,128)(2,1)S(1)}, u32[]{:S(2)}, u32[]{:S(2)}) collective-permute-start(s16[272,128]{1,0:T(8,128)(2,1)S(1)} %get-tuple-element.63), channel_id=1, source_target_pairs={{0,1},{1,0},{2,3},{3,2},{4,5},{5,4},{6,7},{7,6},{8,9},{9,8},{10,11... | collective-permute-start | bytes 208904 | tf_op jit(solution)/shard_map/ppermute | solution.py:428
  49.1 6.0 %collective-permute-start.22 = (s16[272,128]{1,0:T(8,128)(2,1)S(1)}, s16[272,128]{1,0:T(8,128)(2,1)S(1)}, u32[]{:S(2)}, u32[]{:S(2)}) collective-permute-start(s16[272,128]{1,0:T(8,128)(2,1)S(1)} %get-tuple-element.64), channel_id=1, source_target_pairs={{0,2},{1,3},{2,0},{3,1},{4,6},{5,7},{6,4},{7,5},{8,10},{9,11},{10,... | collective-permute-start | bytes 208904 | tf_op jit(solution)/shard_map/ppermute | solution.py:428
  55.6 6.3 %collective-permute-start.25 = (s16[272,128]{1,0:T(8,128)(2,1)S(1)}, s16[272,128]{1,0:T(8,128)(2,1)S(1)}, u32[]{:S(2)}, u32[]{:S(2)}) collective-permute-start(s16[272,128]{1,0:T(8,128)(2,1)S(1)} %solve_1.1.refs_0_), channel_id=1, source_target_pairs={{0,3},{1,2},{2,1},{3,0},{4,7},{5,6},{6,5},{7,4},{8,11},{9,10},{10,... | collective-permute-start | bytes 208904 | tf_op jit(solution)/shard_map/ppermute | solution.py:428
  58.7 4.5 %collective-permute-start.24 = (s16[272,128]{1,0:T(8,128)(2,1)S(1)}, s16[272,128]{1,0:T(8,128)(2,1)S(1)}, u32[]{:S(2)}, u32[]{:S(2)}) collective-permute-start(s16[272,128]{1,0:T(8,128)(2,1)S(1)} %solve_1.1.refs_0_), channel_id=1, source_target_pairs={{0,1},{1,0},{2,3},{3,2},{4,5},{5,4},{6,7},{7,6},{8,9},{9,8},{10,11... | collective-permute-start | bytes 208904 | tf_op jit(solution)/shard_map/ppermute | solution.py:428
  58.7 5.3 %collective-permute-start.23 = (s16[272,128]{1,0:T(8,128)(2,1)S(1)}, s16[272,128]{1,0:T(8,128)(2,1)S(1)}, u32[]{:S(2)}, u32[]{:S(2)}) collective-permute-start(s16[272,128]{1,0:T(8,128)(2,1)S(1)} %solve_1.1.refs_0_), channel_id=1, source_target_pairs={{0,2},{1,3},{2,0},{3,1},{4,6},{5,7},{6,4},{7,5},{8,10},{9,11},{10,... | collective-permute-start | bytes 208904 | tf_op jit(solution)/shard_map/ppermute | solution.py:428
  (3 other events, 22.9 us)

commit v5 on v4

--- a/solution.py
+++ b/solution.py
@@ -68,56 +68,39 @@
     )
 
 
-def start_kernel(groups, prior_dev, colidx, live, prior, msg_ref, first_ref, alive_ref, *scratch):
-    colidx_ref, live_ref, rows, sems = scratch
+def start_kernel(colidx, prior, msg_ref, colidx_ref, rows, sems):
     slots, _, rows_dev = colidx_ref.shape
     copies = [
-        pltpu.make_async_copy(prior, msg_ref.at[pl.ds(0, prior.shape[0])], sems.at[0]),
-        pltpu.make_async_copy(colidx, colidx_ref, sems.at[1]),
-        pltpu.make_async_copy(live, live_ref, sems.at[2]),
+        pltpu.make_async_copy(colidx, colidx_ref, sems.at[0]),
+        pltpu.make_async_copy(prior, msg_ref.at[pl.ds(0, prior.shape[0])], sems.at[1]),
     ]
     for copy in copies:
         copy.start()
     rows[...] = jnp.zeros(rows.shape, I32)
+    copies[0].wait()
+    for j in range(slots):
+        rows[j : j + 1] = lax.shift_right_logical(colidx_ref[j, 1:2], 4)
+        rows[8 + j : 9 + j] = colidx_ref[j, 1:2] & 15
+    msg_ref[prior.shape[0] :] = spread(rows[...], rows_dev).astype(BF16)
     copies[1].wait()
-    copies[2].wait()
-    for j in range(slots):
-        rows[j : j + 1] = colidx_ref[j, 0:1]
-        rows[8 + j : 9 + j] = lax.shift_right_logical(colidx_ref[j, 1:2], 4)
-        rows[16 + j : 17 + j] = colidx_ref[j, 1:2] & 15
-        rows[24 + j : 25 + j] = lax.shift_right_logical(colidx_ref[j, 0:1], 4)
-        rows[32 + j : 33 + j] = colidx_ref[j, 0:1] & 15
-    rows[40:42] = live_ref[...]
-    wide = spread(rows[...], rows_dev)
-    msg_ref[prior.shape[0] :] = wide[8:24].astype(BF16)
-    me, here = lax.axis_index("rows"), lax.axis_index("cols")
-    ids = here * slots + lanes_like((8, LANES), 0)
-    refs = (wide[24:32] * 16.0 + wide[32:40]).astype(I32)
-    live = wide[40:48].astype(I32)
-    found = table_at(refs, me, prior_dev, groups // 2)
-    first_ref[...] = jnp.where(ids < live[0:1], found, groups * prior_dev)
-    alive_ref[...] = (ids < live[1:2]).astype(I32)
-    copies[0].wait()
-
-
-def start(groups, colidx, live, prior):
-    rows_dev, slots = colidx.shape[1:]
+
+
+def start(colidx, prior):
+    slots, _, rows_dev = colidx.shape
     prior_dev, probes, order = prior.shape
-    table = jax.ShapeDtypeStruct((8, LANES), I32)
-    return pl.pallas_call(
-        functools.partial(start_kernel, groups, prior_dev),
-        out_shape=[jax.ShapeDtypeStruct((prior_dev * probes + TAIL, order), BF16), table, table],
-        in_specs=[HBM] * 3,
-        out_specs=[VMEM] * 3,
+    return pl.pallas_call(
+        start_kernel,
+        out_shape=jax.ShapeDtypeStruct((prior_dev * probes + TAIL, order), BF16),
+        in_specs=[HBM] * 2,
+        out_specs=VMEM,
         scratch_shapes=[
             pltpu.VMEM((slots, 2, rows_dev), I32),
-            pltpu.VMEM((2, rows_dev), I32),
-            pltpu.VMEM((48, rows_dev), I32),
-            pltpu.SemaphoreType.DMA((3,)),
+            pltpu.VMEM((TAIL, rows_dev), I32),
+            pltpu.SemaphoreType.DMA((2,)),
         ],
         compiler_params=PARAMS,
         name="start",
-    )(*(in_hbm(x) for x in (jnp.transpose(colidx, (2, 0, 1)), live, prior.reshape(-1, order))))
+    )(in_hbm(colidx), in_hbm(prior.reshape(-1, order)))
 
 
 def ranks(mask, within, slots):
@@ -187,7 +170,9 @@
         prior_count + group * cap + rank.astype(I32),
         table_at(own, me, prior_dev, half),
     )
-    second_ref[...] = jnp.where(alive_ref[...] > 0, at, prior_count + groups * cap)
+    even = ((lax.axis_index("cols") * slots + lanes_like((8, LANES), 0)) & 1) == 0
+    dead = jnp.where(even, prior_count + groups * cap, prior_count)
+    second_ref[...] = jnp.where(alive_ref[...] > 0, at, dead)
     copies = [
         pltpu.make_async_copy(x, out, sems.at[i])
         for i, (x, out) in enumerate(zip((want_ref, second_ref), outs))
@@ -211,35 +196,50 @@
     )(owner_map, alive, *pieces)
 
 
-def load_kernel(cols, first_at, blocks, right_side, inverse, *refs):
-    outs, at_ref, raw, raw_inverse, sems = refs[:4], refs[4], refs[5], refs[6], refs[7]
+def load_kernel(groups, cols, prior_dev, colidx, live, blocks, right_side, inverse, *refs):
+    outs, alive_ref, at_ref = refs[:4], refs[4], refs[5]
+    colidx_ref, live_ref, rows, first_ref, raw, raw_inverse, sems = refs[6:]
     fronts, rows_dev, slots = blocks.shape[:3]
     part = rows_dev // cols
-    first = lax.axis_index("cols") * part
-    names = pltpu.make_async_copy(first_at, at_ref, sems.at[fronts * cols + 2])
-    names.start()
-    copies = []
+    mine = pl.ds(lax.axis_index("cols") * part, part)
+    count = fronts * cols
+    copies = [
+        pltpu.make_async_copy(colidx, colidx_ref, sems.at[count]),
+        pltpu.make_async_copy(live, live_ref, sems.at[count + 1]),
+    ]
     for f in range(fronts):
         for s in range(cols):
-            rows = pl.ds(s * part, part)
+            part_rows = pl.ds(s * part, part)
             copies.append(
                 pltpu.make_async_copy(
-                    blocks.at[f, rows], raw.at[f, rows], sems.at[f * cols + s]
+                    blocks.at[f, part_rows], raw.at[f, part_rows], sems.at[f * cols + s]
                 )
             )
     copies += [
-        pltpu.make_async_copy(
-            inverse.at[:, pl.ds(first, part)], raw_inverse, sems.at[fronts * cols]
-        ),
-        pltpu.make_async_copy(
-            right_side.at[:, pl.ds(first, part)], outs[2], sems.at[fronts * cols + 1]
-        ),
+        pltpu.make_async_copy(inverse.at[:, mine], raw_inverse, sems.at[count + 2]),
+        pltpu.make_async_copy(right_side.at[:, mine], outs[2], sems.at[count + 3]),
     ]
     for copy in copies:
         copy.start()
+    rows[...] = jnp.zeros(rows.shape, I32)
+    copies[0].wait()
+    copies[1].wait()
+    for j in range(slots):
+        rows[j : j + 1] = lax.shift_right_logical(colidx_ref[j, 0:1], 4)
+        rows[8 + j : 9 + j] = colidx_ref[j, 0:1] & 15
+    rows[16:18] = live_ref[...]
+    wide = spread(rows[...], rows_dev)
+    ids = lax.axis_index("cols") * slots + lanes_like((8, LANES), 0)
+    refs0 = (wide[:8] * 16.0 + wide[8:16]).astype(I32)
+    lives = wide[16:24].astype(I32)
+    found = table_at(refs0, lax.axis_index("rows"), prior_dev, groups // 2)
+    first_ref[...] = jnp.where(ids < lives[0:1], found, groups * prior_dev)
+    alive_ref[...] = (ids < lives[1:2]).astype(I32)
+    names = pltpu.make_async_copy(first_ref, at_ref, sems.at[count + 4])
+    names.start()
     for f in range(fronts):
         for s in range(cols):
-            copies[f * cols + s].wait()
+            copies[2 + f * cols + s].wait()
             for i in range(s * part, (s + 1) * part):
                 for j in range(slots):
                     outs[f][i, j] = raw[f, i, j].T
@@ -251,75 +251,128 @@
     names.wait()
 
 
-def load(cols, first_at, blocks, right_side, inverse):
-    part = blocks.shape[1] // cols
+def load(groups, cols, prior_dev, colidx, live, blocks, right_side, inverse):
+    _, rows_dev, slots = blocks.shape[:3]
+    part = rows_dev // cols
     shapes = [blocks.shape[1:]] * 2
     shapes += [a.shape[:1] + (part,) + a.shape[2:] for a in (right_side, inverse)]
     kinds = [BF16, BF16, F32, F32]
     return pl.pallas_call(
-        functools.partial(load_kernel, cols),
+        functools.partial(load_kernel, groups, cols, prior_dev),
         out_shape=[pltpu.VMEM(a, b) for a, b in zip(shapes, kinds)]
-        + [pltpu.SMEM(first_at.shape, I32)],
-        in_specs=[VMEM] + [HBM] * 3,
-        out_specs=[VMEM] * 4 + [SMEM],
+        + [jax.ShapeDtypeStruct((8, LANES), I32), pltpu.SMEM((8, LANES), I32)],
+        in_specs=[HBM] * 5,
+        out_specs=[VMEM] * 5 + [SMEM],
         scratch_shapes=[
+            pltpu.VMEM((slots, 2, rows_dev), I32),
+            pltpu.VMEM((2, rows_dev), I32),
+            pltpu.VMEM((24, rows_dev), I32),
+            pltpu.VMEM((8, LANES), I32),
             pltpu.VMEM(blocks.shape, BF16),
             pltpu.VMEM(shapes[3], F32),
-            pltpu.SemaphoreType.DMA((2 * cols + 3,)),
+            pltpu.SemaphoreType.DMA((2 * cols + 5,)),
         ],
         compiler_params=PARAMS,
         cost_estimate=pl.CostEstimate(
             flops=0, transcendentals=0, bytes_accessed=2 * blocks.size * blocks.dtype.itemsize
         ),
         name="load",
-    )(first_at, *(in_hbm(x) for x in (blocks, right_side, inverse)))
-
-
-def partial_kernel(cols, n_early, probes, places, idx_ref, blk, *refs):
-    ins, own_ref, msgs, known = refs[:-cols - 1], refs[-cols - 1], refs[-cols:-1], refs[-1]
-    rows_dev, slots, order, _ = blk.shape
+    )(*(in_hbm(x) for x in (colidx, live, blocks, right_side, inverse)))
+
+
+def fill(known, refs, places, tail):
+    probes = known.shape[1]
+    for ref, at in zip(refs, places):
+        for k in range((ref.shape[0] - tail) // probes):
+            known[at + k] = ref[k * probes : (k + 1) * probes]
+    known[known.shape[0] - 1] = jnp.zeros(known.shape[1:], known.dtype)
+
+
+def slots_of(parity, slots, here):
+    if slots % 2 == 0:
+        return slots // 2, lambda q: (2 * q + parity, None)
+    shift = (here * slots + parity) & 1
+    return (slots + 1) // 2, lambda q: (
+        jnp.minimum(2 * q + shift, slots - 1),
+        2 * q + shift < slots,
+    )
+
+
+def row_product(known, idx_ref, blk, row, picks, base):
+    xs, ws = [], []
+    for j, there in picks:
+        at = idx_ref[j, row] - base
+        if there is not None:
+            at = jnp.where(there, at, known.shape[0] - 1)
+        xs.append(known[at])
+        ws.append(blk[row, j])
+    return jnp.dot(
+        jnp.concatenate(xs, axis=1), jnp.concatenate(ws, axis=0), preferred_element_type=F32
+    )
+
+
+def partial_kernel(cols, tail, places, base, parity, idx_ref, blk, *refs):
+    refs, own_ref, msgs, known = refs[: -cols - 1], refs[-cols - 1], refs[-cols:-1], refs[-1]
+    ins, start_from = refs[: len(places)], refs[len(places) :]
+    rows_dev, slots = blk.shape[:2]
     part = rows_dev // cols
     here = lax.axis_index("cols")
-    for i, (ref, at) in enumerate(zip(ins, places)):
-        for k in range((ref.shape[0] - (TAIL if i < n_early else 0)) // probes):
-            known[at + k] = ref[k * probes : (k + 1) * probes]
-    known[known.shape[0] - 1] = jnp.zeros(known.shape[1:], known.dtype)
+    fill(known, ins, places, tail)
+    if parity is None:
+        picks = [(j, None) for j in range(slots)]
+    else:
+        count, pick = slots_of(parity, slots, here)
+        picks = [pick(q) for q in range(count)]
     for s in list(range(1, cols)) + [0]:
         first = (here ^ s) * part
-        sums = []
-        for k in range(part):
-            xs = [known[idx_ref[j, first + k]] for j in range(slots)]
-            ws = [blk[first + k, j] for j in range(slots)]
-            sums.append(
-                lax.dot_general(
-                    jnp.concatenate(xs, axis=1),
-                    jnp.concatenate(ws, axis=0),
-                    (((1,), (0,)), ((), ())),
-                    preferred_element_type=F32,
-                )
-            )
+        sums = [row_product(known, idx_ref, blk, first + k, picks, base) for k in range(part)]
+        for ref in start_from:
+            sums = [x + ref[first + k] for k, x in enumerate(sums)]
         if s == 0:
             for k in range(part):
                 own_ref[k] = sums[k]
         else:
-            encode_blocks(sums, msgs[s - 1], probes)
-
-
-def partial_products(name, cols, probes, idx, blocks, early, recent, places):
+            encode_blocks(sums, msgs[s - 1], own_ref.shape[1])
+
+
+def partial_products(name, cols, probes, idx, blocks, ins, tail, places, base=0, parity=None, start_from=()):
     rows_dev, slots, order, _ = blocks.shape
     part = rows_dev // cols
-    rows = sum(a.shape[0] - TAIL for a in early) + sum(a.shape[0] for a in recent)
+    rows = sum(a.shape[0] - tail for a in ins) // probes
     msg = jax.ShapeDtypeStruct((part * probes + TAIL, order), I16)
     out = pl.pallas_call(
-        functools.partial(partial_kernel, cols, len(early), probes, places),
+        functools.partial(partial_kernel, cols, tail, places, base, parity),
         out_shape=[jax.ShapeDtypeStruct((part, probes, order), F32)] + [msg] * (cols - 1),
-        in_specs=[SMEM] + [VMEM] * (len(early) + len(recent) + 1),
+        in_specs=[SMEM] + [VMEM] * (len(ins) + len(start_from) + 1),
         out_specs=[VMEM] * cols,
-        scratch_shapes=[pltpu.VMEM((rows // probes + 1, probes, order), BF16)],
+        scratch_shapes=[pltpu.VMEM((rows + 1, probes, order), BF16)],
         compiler_params=PARAMS,
         name=name,
-    )(in_smem(idx), blocks, *early, *recent)
+    )(in_smem(idx), blocks, *ins, *start_from)
     return out[0], out[1:]
+
+
+def early_kernel(places, idx_ref, blk, *refs):
+    ins, out_ref, known = refs[:-2], refs[-2], refs[-1]
+    rows_dev, slots = blk.shape[:2]
+    fill(known, ins, places, TAIL)
+    count, pick = slots_of(1, slots, lax.axis_index("cols"))
+    for i in range(rows_dev):
+        out_ref[i] = row_product(known, idx_ref, blk, i, [pick(q) for q in range(count)], 0)
+
+
+def early_products(probes, idx, blocks, ins, places):
+    rows_dev, slots, order, _ = blocks.shape
+    rows = sum(a.shape[0] - TAIL for a in ins) // probes
+    return pl.pallas_call(
+        functools.partial(early_kernel, places),
+        out_shape=jax.ShapeDtypeStruct((rows_dev, probes, order), F32),
+        in_specs=[SMEM] + [VMEM] * (len(ins) + 1),
+        out_specs=VMEM,
+        scratch_shapes=[pltpu.VMEM((rows + 1, probes, order), BF16)],
+        compiler_params=PARAMS,
+        name="early_products",
+    )(in_smem(idx), blocks, *ins)
 
 
 def solve_kernel(front, cols, own_ref, *refs):
@@ -396,9 +449,9 @@
         copy.wait()
 
 
-def unpack(front, sources, msgs, shape, base=None):
-    _, rows_dev, probes, order = shape
-    cols = len(sources)
+def unpack(front, sources, msgs, shape, rows_part, base=None):
+    _, _, probes, order = shape
+    cols, part = len(sources), rows_part
     rest = [] if base is None else [base]
     return pl.pallas_call(
         functools.partial(unpack_kernel, front, sources),
@@ -407,7 +460,7 @@
         out_specs=HBM,
         input_output_aliases={} if base is None else {cols: 0},
         scratch_shapes=[
-            pltpu.VMEM((cols, rows_dev // cols, probes, order), F32),
+            pltpu.VMEM((cols, part, probes, order), F32),
             pltpu.SemaphoreType.DMA((cols,)),
         ],
         compiler_params=PARAMS,
@@ -433,15 +486,15 @@
     def scatter(xs):
         return [over_cols(xs[m - 1], m) for m in col_order]
 
-    def gather(x):
-        masks = [0] + col_order[::-1]
-        return masks, [over_cols(x, m) if m else x for m in masks]
-
-    own, first_at, alive = start(groups, colidx, live, prior)
+    def gather(x, masks):
+        return [over_cols(x, m) if m else x for m in masks]
+
+    colidx = jnp.transpose(colidx, (2, 0, 1))
+    own = start(colidx, prior)
     peers = [m for m in row_order if m % 2 == 0][::-1]
     chips = [over_rows(own, m) for m in peers]
-    blocks0, blocks1, rhs, inverse, first_at = load(
-        cols, first_at, blocks, right_side, diag_inverse
+    blocks0, blocks1, rhs, inverse, alive, first_at = load(
+        groups, cols, prior_dev, colidx, live, blocks, right_side, diag_inverse
     )
     chips, blocks0 = lax.optimization_barrier((chips, blocks0))
     chips = [own] + [chips[peers.index(2 * k)] for k in range(1, half)]
@@ -450,23 +503,38 @@
     want, second_at = route(groups, cap, slots, prior_dev, owner_map, alive, pieces)
 
     own0, msgs0 = partial_products(
-        "partial_0", cols, probes, first_at, blocks0, pieces, [], early_at
+        "partial_0", cols, probes, first_at, blocks0, pieces, TAIL, early_at
     )
     coded0 = solve_part(0, cols, own0, scatter(msgs0), rhs, inverse)
-    sources, all0 = gather(coded0)
+    sources = [0] + col_order[::-1]
+    all0 = gather(coded0, sources)
 
     place = {m: (m & 1) * half + (m >> 1) for m in range(groups)}
     sends = pack(sources, groups, cap, want, all0, right_side.shape[1:])
     recent = [sends[0]] + [over_rows(sends[place[m]], m) for m in row_order]
-    recent_at = [groups * prior_dev + place[m] * cap for m in [0] + row_order]
-    solved = unpack(0, sources, all0, right_side.shape)
+    recent_at = [place[m] * cap for m in [0] + row_order]
+    early = early_products(probes, second_at, blocks1, pieces, early_at)
+    part = rows_dev // cols
+    solved = unpack(0, sources, all0, right_side.shape, part)
 
     own1, msgs1 = partial_products(
-        "partial_1", cols, probes, second_at, blocks1, pieces, recent, early_at + recent_at
+        "partial_1",
+        cols,
+        probes,
+        second_at,
+        blocks1,
+        recent,
+        0,
+        recent_at,
+        groups * prior_dev,
+        0,
+        [early],
     )
     coded1 = solve_part(1, cols, own1, scatter(msgs1), rhs, inverse)
-    sources, all1 = gather(coded1)
-    return unpack(1, sources, all1, right_side.shape, solved)
+    sources = [0] + col_order[-2::-1] + col_order[-1:]
+    all1 = gather(coded1, sources)
+    solved = unpack(1, sources[:-1], all1[:-1], right_side.shape, part, solved)
+    return unpack(1, sources[-1:], all1[-1:], right_side.shape, part, solved)
 
 
 def solution(mesh):

time: 65 us -> 64.7 us (level)
  waiting for transfers between devices: 24.1 us -> 22.7 us
  Pallas kernels: 10.6 us -> 11.5 us
    ppermute x12, waiting for transfers between devices: 15.3 us -> 14.6 us  [over_cols(): return lax.ppermute(x, 'cols', [(i, i ^ mask) for i in range(cols)])]
    pallas_call x2 -> x3, Pallas kernels: 1.68 us -> 2.31 us  [unpack(): pl.pallas_call(functools.partial(unpack_kernel, front, sources), out_shap...]
    pallas_call x4 -> x5, Pallas kernels: 6.17 us -> 6.41 us  [the longest x1 3.56 us: load(): pl.pallas_call(functools.partial(load_kernel, groups, cols, prior_dev), o...]
  transfers between devices with their start and end apart: 26 -> 26, of which waited for: 21 -> 20; matrix products, arithmetic and copies ran while one was open for 0% -> 0% of each run, Pallas kernels for 9% -> 11%
where the time goes in v5:
time: 64.7 us; the launch traced here: 64.4 us
  starting transfers between devices  30.1 us (47%)
  waiting for transfers between devices  22.7 us (35%)
  Pallas kernels  11.5 us (18%)
    ppermute x12, starting transfers between devices, over_cols(): return lax.ppermute(x, 'cols', [(i, i ^ mask) for i in range(cols)])  17.8 us
    ppermute x12, waiting for transfers between devices, over_cols(): return lax.ppermute(x, 'cols', [(i, i ^ mask) for i in range(cols)])  14.6 us
    ppermute x14, starting transfers between devices, over_rows(): return lax.ppermute(x, 'rows', [(i, i ^ mask) for i in range(groups)])  12.3 us
    ppermute x14, waiting for transfers between devices, over_rows(): return lax.ppermute(x, 'rows', [(i, i ^ mask) for i in range(groups)])  8.15 us
    pallas_call x1, Pallas kernels, load(): pl.pallas_call(functools.partial(load_kernel, groups, cols, prior_dev), o...  3.56 us
    pallas_call x3, Pallas kernels, unpack(): pl.pallas_call(functools.partial(unpack_kernel, front, sources), out_shap...  2.31 us
    pallas_call x1, Pallas kernels, route(): pl.pallas_call(functools.partial(route_kernel, groups, cap, slots, prior_...  1.62 us
    pallas_call x2, Pallas kernels, partial_products(): pl.pallas_call(functools.partial(partial_kernel, cols, tail, places, base...  1.42 us
  transfers between devices with their start and end apart: 26, of which 20 were waited for; matrix products, arithmetic and copies ran while one was open for 0% of the time, Pallas kernels for 11%

profile of v5, /device:TPU:0, one launch (start us, length us, event | category | flops | bytes accessed | tf_op | source)
XLA Modules:
  0.0 64.4 jit_solution(7740156283801727877)
XLA Ops:
  0.9 3.0 %collective-permute-start.2 = (bf16[528,128]{1,0:T(8,128)(2,1)S(1)}, bf16[528,128]{1,0:T(8,128)(2,1)S(1)}, u32[]{:S(2)}, u32[]{:S(2)}) collective-permute-start(bf16[528,128]{1,0:T(8,128)(2,1)S(1)} %start.1.refs_0_), channel_id=1, source_target_pairs={{0,8},{4,12},{8,0},{12,4},{16,24},{20,28},{24,16},{28,20},{1,9},{5... | collective-permute-start | bytes 405512 | tf_op jit(solution)/shard_map/ppermute | solution.py:478
  4.0 1.5 %collective-permute-start.1 = (bf16[528,128]{1,0:T(8,128)(2,1)S(1)}, bf16[528,128]{1,0:T(8,128)(2,1)S(1)}, u32[]{:S(2)}, u32[]{:S(2)}) collective-permute-start(bf16[528,128]{1,0:T(8,128)(2,1)S(1)} %start.1.refs_0_), channel_id=1, source_target_pairs={{0,16},{4,20},{8,24},{12,28},{16,0},{20,4},{24,8},{28,12},{1,17},{... | collective-permute-start | bytes 405512 | tf_op jit(solution)/shard_map/ppermute | solution.py:478
  5.5 3.6 %load.1 = (bf16[16,6,128,128]{3,2,1,0:T(8,128)(2,1)S(1)}, bf16[16,6,128,128]{3,2,1,0:T(8,128)(2,1)S(1)}, f32[2,4,64,128]{3,2,1,0:T(8,128)S(1)}, f32[2,4,128,128]...) custom-call(s32[6,2,16]{2,1,0:T(2,128)} %bitcast.4, s32[2,16]{1,0:T(2,128)} %live.1, ...), custom_call_target="tpu_custom_call" | custom-call | bytes 12582912 | tf_op jit(solution)/shard_map/load/pallas_call | solution.py:260
  9.1 2.8 %collective-permute-done.1.refs_2_ = bf16[528,128]{1,0:T(8,128)(2,1)S(1)} collective-permute-done((bf16[528,128]{1,0:T(8,128)(2,1)S(1)}, bf16[528,128]{1,0:T(8,128)(2,1)S(1)}, u32[]{:S(2)}, u32[]{:S(2)}) %collective-permute-start.1) | collective-permute-done | bytes 135200 | tf_op jit(solution)/shard_map/ppermute | solution.py:478
  14.6 3.7 %collective-permute-start.7 = (s16[272,128]{1,0:T(8,128)(2,1)S(1)}, s16[272,128]{1,0:T(8,128)(2,1)S(1)}, u32[]{:S(2)}, u32[]{:S(2)}) collective-permute-start(s16[272,128]{1,0:T(8,128)(2,1)S(1)} %get-tuple-element.44), channel_id=1, source_target_pairs={{0,3},{1,2},{2,1},{3,0},{4,7},{5,6},{6,5},{7,4},{8,11},{9,10},{10,... | collective-permute-start | bytes 208904 | tf_op jit(solution)/shard_map/ppermute | solution.py:481
  19.0 2.4 %collective-permute-done.7.refs_0_ = s16[272,128]{1,0:T(8,128)(2,1)S(1)} collective-permute-done((s16[272,128]{1,0:T(8,128)(2,1)S(1)}, s16[272,128]{1,0:T(8,128)(2,1)S(1)}, u32[]{:S(2)}, u32[]{:S(2)}) %collective-permute-start.7) | collective-permute-done | bytes 69664 | tf_op jit(solution)/shard_map/ppermute | solution.py:481
  21.5 2.1 %collective-permute-done.8.refs_1_ = s16[272,128]{1,0:T(8,128)(2,1)S(1)} collective-permute-done((s16[272,128]{1,0:T(8,128)(2,1)S(1)}, s16[272,128]{1,0:T(8,128)(2,1)S(1)}, u32[]{:S(2)}, u32[]{:S(2)}) %collective-permute-start.8) | collective-permute-done | bytes 69664 | tf_op jit(solution)/shard_map/ppermute | solution.py:481
  24.8 2.4 %collective-permute-start.12 = (s16[272,128]{1,0:T(8,128)(2,1)S(1)}, s16[272,128]{1,0:T(8,128)(2,1)S(1)}, u32[]{:S(2)}, u32[]{:S(2)}) collective-permute-start(s16[272,128]{1,0:T(8,128)(2,1)S(1)} %solve_0.1.refs_0_), channel_id=1, source_target_pairs={{0,3},{1,2},{2,1},{3,0},{4,7},{5,6},{6,5},{7,4},{8,11},{9,10},{10,... | collective-permute-start | bytes 208904 | tf_op jit(solution)/shard_map/ppermute | solution.py:481
  27.6 1.6 %collective-permute-start.10 = (s16[272,128]{1,0:T(8,128)(2,1)S(1)}, s16[272,128]{1,0:T(8,128)(2,1)S(1)}, u32[]{:S(2)}, u32[]{:S(2)}) collective-permute-start(s16[272,128]{1,0:T(8,128)(2,1)S(1)} %solve_0.1.refs_0_), channel_id=1, source_target_pairs={{0,2},{1,3},{2,0},{3,1},{4,6},{5,7},{6,4},{7,5},{8,10},{9,11},{10,... | collective-permute-start | bytes 208904 | tf_op jit(solution)/shard_map/ppermute | solution.py:481
  29.2 1.6 %route.1 = (s32[8,128]{1,0:T(8,128)S(4)}, s32[8,128]{1,0:T(8,128)S(4)}) custom-call(s32[2,128]{1,0:T(2,128)S(1)} %copy-done, s32[8,128]{1,0:T(8,128)S(1)} %get-tuple-element.33.alive_ref, bf16[528,128]{1,0:T(8,128)(2,1)S(1)} %start.1.refs_0_, bf16[528,128]{1,0:T(8,128)(2,1)S(1)} %collective-permute-done.2.refs_1_, ...), custom_call_target="tpu_custom_call" | custom-call | tf_op jit(solution)/shard_map/route/pallas_call | solution.py:188
  31.1 1.2 %collective-permute-done.11.refs_2_ = s16[272,128]{1,0:T(8,128)(2,1)S(1)} collective-permute-done((s16[272,128]{1,0:T(8,128)(2,1)S(1)}, s16[272,128]{1,0:T(8,128)(2,1)S(1)}, u32[]{:S(2)}, u32[]{:S(2)}) %collective-permute-start.11) | collective-permute-done | bytes 69664 | tf_op jit(solution)/shard_map/ppermute | solution.py:481
  33.2 1.3 %collective-permute-start.13 = (bf16[384,128]{1,0:T(8,128)(2,1)S(1)}, bf16[384,128]{1,0:T(8,128)(2,1)S(1)}, u32[]{:S(2)}, u32[]{:S(2)}) collective-permute-start(bf16[384,128]{1,0:T(8,128)(2,1)S(1)} %get-tuple-element.50), channel_id=1, source_target_pairs={{0,8},{4,12},{8,0},{12,4},{16,24},{20,28},{24,16},{28,20},{1,9},{5... | collective-permute-start | bytes 294920 | tf_op jit(solution)/shard_map/ppermute | solution.py:478
  35.3 1.4 %collective-permute-start.15 = (bf16[384,128]{1,0:T(8,128)(2,1)S(1)}, bf16[384,128]{1,0:T(8,128)(2,1)S(1)}, u32[]{:S(2)}, u32[]{:S(2)}) collective-permute-start(bf16[384,128]{1,0:T(8,128)(2,1)S(1)} %get-tuple-element.52), channel_id=1, source_target_pairs={{0,24},{4,28},{8,16},{12,20},{16,8},{20,12},{24,0},{28,4},{1,25},{... | collective-permute-start | bytes 294920 | tf_op jit(solution)/shard_map/ppermute | solution.py:478
  36.7 1.8 %collective-permute-start.17 = (bf16[384,128]{1,0:T(8,128)(2,1)S(1)}, bf16[384,128]{1,0:T(8,128)(2,1)S(1)}, u32[]{:S(2)}, u32[]{:S(2)}) collective-permute-start(bf16[384,128]{1,0:T(8,128)(2,1)S(1)} %get-tuple-element.54), channel_id=1, source_target_pairs={{0,20},{4,16},{8,28},{12,24},{16,4},{20,0},{24,12},{28,8},{1,21},{... | collective-permute-start | bytes 294920 | tf_op jit(solution)/shard_map/ppermute | solution.py:478
  39.4 1.0 %collective-permute-start.19 = (bf16[384,128]{1,0:T(8,128)(2,1)S(1)}, bf16[384,128]{1,0:T(8,128)(2,1)S(1)}, u32[]{:S(2)}, u32[]{:S(2)}) collective-permute-start(bf16[384,128]{1,0:T(8,128)(2,1)S(1)} %get-tuple-element.56), channel_id=1, source_target_pairs={{0,4},{4,0},{8,12},{12,8},{16,20},{20,16},{24,28},{28,24},{1,5},{5... | collective-permute-start | bytes 294920 | tf_op jit(solution)/shard_map/ppermute | solution.py:478
  42.4 2.4 %collective-permute-done.18.refs_6_ = bf16[384,128]{1,0:T(8,128)(2,1)S(1)} collective-permute-done((bf16[384,128]{1,0:T(8,128)(2,1)S(1)}, bf16[384,128]{1,0:T(8,128)(2,1)S(1)}, u32[]{:S(2)}, u32[]{:S(2)}) %collective-permute-start.18) | collective-permute-done | bytes 98336 | tf_op jit(solution)/shard_map/ppermute | solution.py:478
  45.5 3.3 %collective-permute-start.20 = (s16[272,128]{1,0:T(8,128)(2,1)S(1)}, s16[272,128]{1,0:T(8,128)(2,1)S(1)}, u32[]{:S(2)}, u32[]{:S(2)}) collective-permute-start(s16[272,128]{1,0:T(8,128)(2,1)S(1)} %get-tuple-element.58), channel_id=1, source_target_pairs={{0,3},{1,2},{2,1},{3,0},{4,7},{5,6},{6,5},{7,4},{8,11},{9,10},{10,... | collective-permute-start | bytes 208904 | tf_op jit(solution)/shard_map/ppermute | solution.py:481
  48.8 1.1 %collective-permute-start.22 = (s16[272,128]{1,0:T(8,128)(2,1)S(1)}, s16[272,128]{1,0:T(8,128)(2,1)S(1)}, u32[]{:S(2)}, u32[]{:S(2)}) collective-permute-start(s16[272,128]{1,0:T(8,128)(2,1)S(1)} %get-tuple-element.60), channel_id=1, source_target_pairs={{0,2},{1,3},{2,0},{3,1},{4,6},{5,7},{6,4},{7,5},{8,10},{9,11},{10,... | collective-permute-start | bytes 208904 | tf_op jit(solution)/shard_map/ppermute | solution.py:481
  49.9 2.5 %collective-permute-done.20.refs_0_ = s16[272,128]{1,0:T(8,128)(2,1)S(1)} collective-permute-done((s16[272,128]{1,0:T(8,128)(2,1)S(1)}, s16[272,128]{1,0:T(8,128)(2,1)S(1)}, u32[]{:S(2)}, u32[]{:S(2)}) %collective-permute-start.20) | collective-permute-done | bytes 69664 | tf_op jit(solution)/shard_map/ppermute | solution.py:481
  52.4 1.8 %collective-permute-done.21.refs_1_ = s16[272,128]{1,0:T(8,128)(2,1)S(1)} collective-permute-done((s16[272,128]{1,0:T(8,128)(2,1)S(1)}, s16[272,128]{1,0:T(8,128)(2,1)S(1)}, u32[]{:S(2)}, u32[]{:S(2)}) %collective-permute-start.21) | collective-permute-done | bytes 69664 | tf_op jit(solution)/shard_map/ppermute | solution.py:481
  55.3 3.1 %collective-permute-start.25 = (s16[272,128]{1,0:T(8,128)(2,1)S(1)}, s16[272,128]{1,0:T(8,128)(2,1)S(1)}, u32[]{:S(2)}, u32[]{:S(2)}) collective-permute-start(s16[272,128]{1,0:T(8,128)(2,1)S(1)} %solve_1.1.refs_0_), channel_id=1, source_target_pairs={{0,3},{1,2},{2,1},{3,0},{4,7},{5,6},{6,5},{7,4},{8,11},{9,10},{10,... | collective-permute-start | bytes 208904 | tf_op jit(solution)/shard_map/ppermute | solution.py:481
  58.4 1.3 %collective-permute-start.23 = (s16[272,128]{1,0:T(8,128)(2,1)S(1)}, s16[272,128]{1,0:T(8,128)(2,1)S(1)}, u32[]{:S(2)}, u32[]{:S(2)}) collective-permute-start(s16[272,128]{1,0:T(8,128)(2,1)S(1)} %solve_1.1.refs_0_), channel_id=1, source_target_pairs={{0,2},{1,3},{2,0},{3,1},{4,6},{5,7},{6,4},{7,5},{8,10},{9,11},{10,... | collective-permute-start | bytes 208904 | tf_op jit(solution)/shard_map/ppermute | solution.py:481
  60.6 1.0 %collective-permute-done.25.refs_2_ = s16[272,128]{1,0:T(8,128)(2,1)S(1)} collective-permute-done((s16[272,128]{1,0:T(8,128)(2,1)S(1)}, s16[272,128]{1,0:T(8,128)(2,1)S(1)}, u32[]{:S(2)}, u32[]{:S(2)}) %collective-permute-start.25) | collective-permute-done | bytes 69664 | tf_op jit(solution)/shard_map/ppermute | solution.py:481
  61.6 1.3 %collective-permute-done.24.refs_1_ = s16[272,128]{1,0:T(8,128)(2,1)S(1)} collective-permute-done((s16[272,128]{1,0:T(8,128)(2,1)S(1)}, s16[272,128]{1,0:T(8,128)(2,1)S(1)}, u32[]{:S(2)}, u32[]{:S(2)}) %collective-permute-start.24) | collective-permute-done | bytes 69664 | tf_op jit(solution)/shard_map/ppermute | solution.py:481
  (42 shorter events, 15.0 us)
Async XLA Ops:
  0.9 8.1 %collective-permute-start.2 = (bf16[528,128]{1,0:T(8,128)(2,1)S(1)}, bf16[528,128]{1,0:T(8,128)(2,1)S(1)}, u32[]{:S(2)}, u32[]{:S(2)}) collective-permute-start(bf16[528,128]{1,0:T(8,128)(2,1)S(1)} %start.1.refs_0_), channel_id=1, source_target_pairs={{0,8},{4,12},{8,0},{12,4},{16,24},{20,28},{24,16},{28,20},{1,9},{5... | collective-permute-start | bytes 405512 | tf_op jit(solution)/shard_map/ppermute | solution.py:478
  4.0 7.9 %collective-permute-start.1 = (bf16[528,128]{1,0:T(8,128)(2,1)S(1)}, bf16[528,128]{1,0:T(8,128)(2,1)S(1)}, u32[]{:S(2)}, u32[]{:S(2)}) collective-permute-start(bf16[528,128]{1,0:T(8,128)(2,1)S(1)} %start.1.refs_0_), channel_id=1, source_target_pairs={{0,16},{4,20},{8,24},{12,28},{16,0},{20,4},{24,8},{28,12},{1,17},{... | collective-permute-start | bytes 405512 | tf_op jit(solution)/shard_map/ppermute | solution.py:478
  5.5 6.4 %collective-permute-start = (bf16[528,128]{1,0:T(8,128)(2,1)S(1)}, bf16[528,128]{1,0:T(8,128)(2,1)S(1)}, u32[]{:S(2)}, u32[]{:S(2)}) collective-permute-start(bf16[528,128]{1,0:T(8,128)(2,1)S(1)} %start.1.refs_0_), channel_id=1, source_target_pairs={{0,24},{4,28},{8,16},{12,20},{16,8},{20,12},{24,0},{28,4},{1,25},{... | collective-permute-start | bytes 405512 | tf_op jit(solution)/shard_map/ppermute | solution.py:478
  5.5 6.9 %collective-permute-start.3 = (bf16[528,128]{1,0:T(8,128)(2,1)S(1)}, bf16[528,128]{1,0:T(8,128)(2,1)S(1)}, u32[]{:S(2)}, u32[]{:S(2)}) collective-permute-start(bf16[528,128]{1,0:T(8,128)(2,1)S(1)} %start.1.refs_0_), channel_id=1, source_target_pairs={{0,4},{4,0},{8,12},{12,8},{16,20},{20,16},{24,28},{28,24},{1,5},{5... | collective-permute-start | bytes 405512 | tf_op jit(solution)/shard_map/ppermute | solution.py:478
  11.9 1.5 %collective-permute-start.5 = (bf16[528,128]{1,0:T(8,128)(2,1)S(1)}, bf16[528,128]{1,0:T(8,128)(2,1)S(1)}, u32[]{:S(2)}, u32[]{:S(2)}) collective-permute-start(bf16[528,128]{1,0:T(8,128)(2,1)S(1)} %collective-permute-done.1.refs_2_), channel_id=1, source_target_pairs={{0,4},{4,0},{8,12},{12,8},{16,20},{20,16},{24,28},{28,24},{1,5},{5... | collective-permute-start | bytes 405512 | tf_op jit(solution)/shard_map/ppermute | solution.py:478
  14.6 6.9 %collective-permute-start.7 = (s16[272,128]{1,0:T(8,128)(2,1)S(1)}, s16[272,128]{1,0:T(8,128)(2,1)S(1)}, u32[]{:S(2)}, u32[]{:S(2)}) collective-permute-start(s16[272,128]{1,0:T(8,128)(2,1)S(1)} %get-tuple-element.44), channel_id=1, source_target_pairs={{0,3},{1,2},{2,1},{3,0},{4,7},{5,6},{6,5},{7,4},{8,11},{9,10},{10,... | collective-permute-start | bytes 208904 | tf_op jit(solution)/shard_map/ppermute | solution.py:481
  18.3 5.3 %collective-permute-start.8 = (s16[272,128]{1,0:T(8,128)(2,1)S(1)}, s16[272,128]{1,0:T(8,128)(2,1)S(1)}, u32[]{:S(2)}, u32[]{:S(2)}) collective-permute-start(s16[272,128]{1,0:T(8,128)(2,1)S(1)} %get-tuple-element.45), channel_id=1, source_target_pairs={{0,1},{1,0},{2,3},{3,2},{4,5},{5,4},{6,7},{7,6},{8,9},{9,8},{10,11... | collective-permute-start | bytes 208904 | tf_op jit(solution)/shard_map/ppermute | solution.py:481
  18.3 6.0 %collective-permute-start.9 = (s16[272,128]{1,0:T(8,128)(2,1)S(1)}, s16[272,128]{1,0:T(8,128)(2,1)S(1)}, u32[]{:S(2)}, u32[]{:S(2)}) collective-permute-start(s16[272,128]{1,0:T(8,128)(2,1)S(1)} %get-tuple-element.46), channel_id=1, source_target_pairs={{0,2},{1,3},{2,0},{3,1},{4,6},{5,7},{6,4},{7,5},{8,10},{9,11},{10,... | collective-permute-start | bytes 208904 | tf_op jit(solution)/shard_map/ppermute | solution.py:481
  24.8 6.3 %collective-permute-start.12 = (s16[272,128]{1,0:T(8,128)(2,1)S(1)}, s16[272,128]{1,0:T(8,128)(2,1)S(1)}, u32[]{:S(2)}, u32[]{:S(2)}) collective-permute-start(s16[272,128]{1,0:T(8,128)(2,1)S(1)} %solve_0.1.refs_0_), channel_id=1, source_target_pairs={{0,3},{1,2},{2,1},{3,0},{4,7},{5,6},{6,5},{7,4},{8,11},{9,10},{10,... | collective-permute-start | bytes 208904 | tf_op jit(solution)/shard_map/ppermute | solution.py:481
  27.2 5.1 %collective-permute-start.11 = (s16[272,128]{1,0:T(8,128)(2,1)S(1)}, s16[272,128]{1,0:T(8,128)(2,1)S(1)}, u32[]{:S(2)}, u32[]{:S(2)}) collective-permute-start(s16[272,128]{1,0:T(8,128)(2,1)S(1)} %solve_0.1.refs_0_), channel_id=1, source_target_pairs={{0,1},{1,0},{2,3},{3,2},{4,5},{5,4},{6,7},{7,6},{8,9},{9,8},{10,11... | collective-permute-start | bytes 208904 | tf_op jit(solution)/shard_map/ppermute | solution.py:481
  27.6 5.5 %collective-permute-start.10 = (s16[272,128]{1,0:T(8,128)(2,1)S(1)}, s16[272,128]{1,0:T(8,128)(2,1)S(1)}, u32[]{:S(2)}, u32[]{:S(2)}) collective-permute-start(s16[272,128]{1,0:T(8,128)(2,1)S(1)} %solve_0.1.refs_0_), channel_id=1, source_target_pairs={{0,2},{1,3},{2,0},{3,1},{4,6},{5,7},{6,4},{7,5},{8,10},{9,11},{10,... | collective-permute-start | bytes 208904 | tf_op jit(solution)/shard_map/ppermute | solution.py:481
  33.2 5.4 %collective-permute-start.13 = (bf16[384,128]{1,0:T(8,128)(2,1)S(1)}, bf16[384,128]{1,0:T(8,128)(2,1)S(1)}, u32[]{:S(2)}, u32[]{:S(2)}) collective-permute-start(bf16[384,128]{1,0:T(8,128)(2,1)S(1)} %get-tuple-element.50), channel_id=1, source_target_pairs={{0,8},{4,12},{8,0},{12,4},{16,24},{20,28},{24,16},{28,20},{1,9},{5... | collective-permute-start | bytes 294920 | tf_op jit(solution)/shard_map/ppermute | solution.py:478
  34.5 5.0 %collective-permute-start.14 = (bf16[384,128]{1,0:T(8,128)(2,1)S(1)}, bf16[384,128]{1,0:T(8,128)(2,1)S(1)}, u32[]{:S(2)}, u32[]{:S(2)}) collective-permute-start(bf16[384,128]{1,0:T(8,128)(2,1)S(1)} %get-tuple-element.51), channel_id=1, source_target_pairs={{0,16},{4,20},{8,24},{12,28},{16,0},{20,4},{24,8},{28,12},{1,17},{... | collective-permute-start | bytes 294920 | tf_op jit(solution)/shard_map/ppermute | solution.py:478
  35.3 5.7 %collective-permute-start.15 = (bf16[384,128]{1,0:T(8,128)(2,1)S(1)}, bf16[384,128]{1,0:T(8,128)(2,1)S(1)}, u32[]{:S(2)}, u32[]{:S(2)}) collective-permute-start(bf16[384,128]{1,0:T(8,128)(2,1)S(1)} %get-tuple-element.52), channel_id=1, source_target_pairs={{0,24},{4,28},{8,16},{12,20},{16,8},{20,12},{24,0},{28,4},{1,25},{... | collective-permute-start | bytes 294920 | tf_op jit(solution)/shard_map/ppermute | solution.py:478
  36.7 5.1 %collective-permute-start.16 = (bf16[384,128]{1,0:T(8,128)(2,1)S(1)}, bf16[384,128]{1,0:T(8,128)(2,1)S(1)}, u32[]{:S(2)}, u32[]{:S(2)}) collective-permute-start(bf16[384,128]{1,0:T(8,128)(2,1)S(1)} %get-tuple-element.53), channel_id=1, source_target_pairs={{0,12},{4,8},{8,4},{12,0},{16,28},{20,24},{24,20},{28,16},{1,13},{... | collective-permute-start | bytes 294920 | tf_op jit(solution)/shard_map/ppermute | solution.py:478
  36.7 5.7 %collective-permute-start.17 = (bf16[384,128]{1,0:T(8,128)(2,1)S(1)}, bf16[384,128]{1,0:T(8,128)(2,1)S(1)}, u32[]{:S(2)}, u32[]{:S(2)}) collective-permute-start(bf16[384,128]{1,0:T(8,128)(2,1)S(1)} %get-tuple-element.54), channel_id=1, source_target_pairs={{0,20},{4,16},{8,28},{12,24},{16,4},{20,0},{24,12},{28,8},{1,21},{... | collective-permute-start | bytes 294920 | tf_op jit(solution)/shard_map/ppermute | solution.py:478
  38.6 6.3 %collective-permute-start.18 = (bf16[384,128]{1,0:T(8,128)(2,1)S(1)}, bf16[384,128]{1,0:T(8,128)(2,1)S(1)}, u32[]{:S(2)}, u32[]{:S(2)}) collective-permute-start(bf16[384,128]{1,0:T(8,128)(2,1)S(1)} %get-tuple-element.55), channel_id=1, source_target_pairs={{0,28},{4,24},{8,20},{12,16},{16,12},{20,8},{24,4},{28,0},{1,29},{... | collective-permute-start | bytes 294920 | tf_op jit(solution)/shard_map/ppermute | solution.py:478
  39.4 5.4 %collective-permute-start.19 = (bf16[384,128]{1,0:T(8,128)(2,1)S(1)}, bf16[384,128]{1,0:T(8,128)(2,1)S(1)}, u32[]{:S(2)}, u32[]{:S(2)}) collective-permute-start(bf16[384,128]{1,0:T(8,128)(2,1)S(1)} %get-tuple-element.56), channel_id=1, source_target_pairs={{0,4},{4,0},{8,12},{12,8},{16,20},{20,16},{24,28},{28,24},{1,5},{5... | collective-permute-start | bytes 294920 | tf_op jit(solution)/shard_map/ppermute | solution.py:478
  45.5 6.9 %collective-permute-start.20 = (s16[272,128]{1,0:T(8,128)(2,1)S(1)}, s16[272,128]{1,0:T(8,128)(2,1)S(1)}, u32[]{:S(2)}, u32[]{:S(2)}) collective-permute-start(s16[272,128]{1,0:T(8,128)(2,1)S(1)} %get-tuple-element.58), channel_id=1, source_target_pairs={{0,3},{1,2},{2,1},{3,0},{4,7},{5,6},{6,5},{7,4},{8,11},{9,10},{10,... | collective-permute-start | bytes 208904 | tf_op jit(solution)/shard_map/ppermute | solution.py:481
  48.8 5.4 %collective-permute-start.21 = (s16[272,128]{1,0:T(8,128)(2,1)S(1)}, s16[272,128]{1,0:T(8,128)(2,1)S(1)}, u32[]{:S(2)}, u32[]{:S(2)}) collective-permute-start(s16[272,128]{1,0:T(8,128)(2,1)S(1)} %get-tuple-element.59), channel_id=1, source_target_pairs={{0,1},{1,0},{2,3},{3,2},{4,5},{5,4},{6,7},{7,6},{8,9},{9,8},{10,11... | collective-permute-start | bytes 208904 | tf_op jit(solution)/shard_map/ppermute | solution.py:481
  48.8 6.0 %collective-permute-start.22 = (s16[272,128]{1,0:T(8,128)(2,1)S(1)}, s16[272,128]{1,0:T(8,128)(2,1)S(1)}, u32[]{:S(2)}, u32[]{:S(2)}) collective-permute-start(s16[272,128]{1,0:T(8,128)(2,1)S(1)} %get-tuple-element.60), channel_id=1, source_target_pairs={{0,2},{1,3},{2,0},{3,1},{4,6},{5,7},{6,4},{7,5},{8,10},{9,11},{10,... | collective-permute-start | bytes 208904 | tf_op jit(solution)/shard_map/ppermute | solution.py:481
  55.3 6.3 %collective-permute-start.25 = (s16[272,128]{1,0:T(8,128)(2,1)S(1)}, s16[272,128]{1,0:T(8,128)(2,1)S(1)}, u32[]{:S(2)}, u32[]{:S(2)}) collective-permute-start(s16[272,128]{1,0:T(8,128)(2,1)S(1)} %solve_1.1.refs_0_), channel_id=1, source_target_pairs={{0,3},{1,2},{2,1},{3,0},{4,7},{5,6},{6,5},{7,4},{8,11},{9,10},{10,... | collective-permute-start | bytes 208904 | tf_op jit(solution)/shard_map/ppermute | solution.py:481
  58.4 4.5 %collective-permute-start.24 = (s16[272,128]{1,0:T(8,128)(2,1)S(1)}, s16[272,128]{1,0:T(8,128)(2,1)S(1)}, u32[]{:S(2)}, u32[]{:S(2)}) collective-permute-start(s16[272,128]{1,0:T(8,128)(2,1)S(1)} %solve_1.1.refs_0_), channel_id=1, source_target_pairs={{0,1},{1,0},{2,3},{3,2},{4,5},{5,4},{6,7},{7,6},{8,9},{9,8},{10,11... | collective-permute-start | bytes 208904 | tf_op jit(solution)/shard_map/ppermute | solution.py:481
  58.4 5.3 %collective-permute-start.23 = (s16[272,128]{1,0:T(8,128)(2,1)S(1)}, s16[272,128]{1,0:T(8,128)(2,1)S(1)}, u32[]{:S(2)}, u32[]{:S(2)}) collective-permute-start(s16[272,128]{1,0:T(8,128)(2,1)S(1)} %solve_1.1.refs_0_), channel_id=1, source_target_pairs={{0,2},{1,3},{2,0},{3,1},{4,6},{5,7},{6,4},{7,5},{8,10},{9,11},{10,... | collective-permute-start | bytes 208904 | tf_op jit(solution)/shard_map/ppermute | solution.py:481
  (3 other events, 22.9 us)

commit v6 on v5

--- a/solution.py
+++ b/solution.py
@@ -14,20 +14,21 @@
 PARAMS = pltpu.CompilerParams(vmem_limit_bytes=16 * 2**20)
 STEPS = 128.0
 TAIL = 16
+SCALES = 16
 LANES = 128
+PIECES = 4
 
 
 def encode_blocks(values, msg_ref, probes):
-    rows = lax.broadcasted_iota(I32, (TAIL, msg_ref.shape[1]), 0)
-    tail = jnp.zeros((TAIL, msg_ref.shape[1]), F32)
+    peaks = [jnp.max(jnp.abs(value), axis=0, keepdims=True) for value in values]
+    peaks += [jnp.zeros((SCALES - len(peaks), msg_ref.shape[1]), F32)] * (len(peaks) < SCALES)
+    peaks = jnp.maximum(jnp.max(jnp.concatenate(peaks), axis=1, keepdims=True), 2.0**-100)
+    level = jnp.broadcast_to(jnp.ceil(jnp.log2(peaks) * STEPS), (SCALES, msg_ref.shape[1]))
+    factor = jnp.exp2(15.0 - level * (1.0 / STEPS))
     for k, value in enumerate(values):
-        peak = jnp.maximum(jnp.max(jnp.abs(value), keepdims=True), 2.0**-100)
-        level = jnp.ceil(jnp.log2(peak) * STEPS)
-        scaled = jnp.round(value * jnp.exp2(15.0 - level * (1.0 / STEPS)))
-        scaled = jnp.clip(scaled, -32767.0, 32767.0)
+        scaled = jnp.clip(jnp.round(value * factor[k : k + 1]), -32767.0, 32767.0)
         msg_ref[k * probes : (k + 1) * probes] = scaled.astype(I32).astype(I16)
-        tail = jnp.where(rows == k, level, tail)
-    msg_ref[len(values) * probes :] = tail.astype(I32).astype(I16)
+    msg_ref[len(values) * probes :] = level.astype(I32).astype(I16)
 
 
 def decode_blocks(msg_ref, count, probes):
@@ -70,10 +71,10 @@
 
 def start_kernel(colidx, prior, msg_ref, colidx_ref, rows, sems):
     slots, _, rows_dev = colidx_ref.shape
-    copies = [
-        pltpu.make_async_copy(colidx, colidx_ref, sems.at[0]),
-        pltpu.make_async_copy(prior, msg_ref.at[pl.ds(0, prior.shape[0])], sems.at[1]),
-    ]
+    copies = [pltpu.make_async_copy(colidx, colidx_ref, sems.at[0])]
+    for i in range(PIECES):
+        some = pl.ds(i * (prior.shape[0] // PIECES), prior.shape[0] // PIECES)
+        copies.append(pltpu.make_async_copy(prior.at[some], msg_ref.at[some], sems.at[1 + i]))
     for copy in copies:
         copy.start()
     rows[...] = jnp.zeros(rows.shape, I32)
@@ -82,7 +83,8 @@
         rows[j : j + 1] = lax.shift_right_logical(colidx_ref[j, 1:2], 4)
         rows[8 + j : 9 + j] = colidx_ref[j, 1:2] & 15
     msg_ref[prior.shape[0] :] = spread(rows[...], rows_dev).astype(BF16)
-    copies[1].wait()
+    for copy in copies[1:]:
+        copy.wait()
 
 
 def start(colidx, prior):
@@ -96,7 +98,7 @@
         scratch_shapes=[
             pltpu.VMEM((slots, 2, rows_dev), I32),
             pltpu.VMEM((TAIL, rows_dev), I32),
-            pltpu.SemaphoreType.DMA((2,)),
+            pltpu.SemaphoreType.DMA((1 + PIECES,)),
         ],
         compiler_params=PARAMS,
         name="start",
@@ -339,7 +341,7 @@
     rows_dev, slots, order, _ = blocks.shape
     part = rows_dev // cols
     rows = sum(a.shape[0] - tail for a in ins) // probes
-    msg = jax.ShapeDtypeStruct((part * probes + TAIL, order), I16)
+    msg = jax.ShapeDtypeStruct((part * probes + SCALES, order), I16)
     out = pl.pallas_call(
         functools.partial(partial_kernel, cols, tail, places, base, parity),
         out_shape=[jax.ShapeDtypeStruct((part, probes, order), F32)] + [msg] * (cols - 1),
@@ -386,7 +388,7 @@
             rhs_ref[front, k] - total[k],
             inv_ref[front, k],
             (((1,), (0,)), ((), ())),
-            precision=lax.Precision.HIGHEST,
+            precision=lax.Precision.HIGH,
             preferred_element_type=F32,
         )
         for k in range(part)
@@ -398,7 +400,7 @@
     part, probes, order = own.shape
     return pl.pallas_call(
         functools.partial(solve_kernel, front, cols),
-        out_shape=jax.ShapeDtypeStruct((part * probes + TAIL, order), I16),
+        out_shape=jax.ShapeDtypeStruct((part * probes + SCALES, order), I16),
         in_specs=[VMEM] * (cols + 2),
         out_specs=VMEM,
         compiler_params=PARAMS,

time: 64.7 us -> 64.2 us (level)
  no operation moved by 1% of the time
where the time goes in v6:
time: 64.2 us; the launch traced here: 64 us
  starting transfers between devices  30.1 us (47%)
  waiting for transfers between devices  22.7 us (35%)
  Pallas kernels  11.1 us (17%)
    ppermute x12, starting transfers between devices, over_cols(): return lax.ppermute(x, 'cols', [(i, i ^ mask) for i in range(cols)])  17.8 us
    ppermute x12, waiting for transfers between devices, over_cols(): return lax.ppermute(x, 'cols', [(i, i ^ mask) for i in range(cols)])  14.5 us
    ppermute x14, starting transfers between devices, over_rows(): return lax.ppermute(x, 'rows', [(i, i ^ mask) for i in range(groups)])  12.2 us
    ppermute x14, waiting for transfers between devices, over_rows(): return lax.ppermute(x, 'rows', [(i, i ^ mask) for i in range(groups)])  8.17 us
    pallas_call x1, Pallas kernels, load(): pl.pallas_call(functools.partial(load_kernel, groups, cols, prior_dev), o...  3.56 us
    pallas_call x3, Pallas kernels, unpack(): pl.pallas_call(functools.partial(unpack_kernel, front, sources), out_shap...  2.31 us
    pallas_call x1, Pallas kernels, route(): pl.pallas_call(functools.partial(route_kernel, groups, cap, slots, prior_...  1.62 us
    pallas_call x2, Pallas kernels, partial_products(): pl.pallas_call(functools.partial(partial_kernel, cols, tail, places, base...  1.35 us
  transfers between devices with their start and end apart: 26, of which 20 were waited for; matrix products, arithmetic and copies ran while one was open for 0% of the time, Pallas kernels for 11%

profile of v6, /device:TPU:0, one launch (start us, length us, event | category | flops | bytes accessed | tf_op | source)
XLA Modules:
  0.0 64.0 jit_solution(6907627413379970246)
XLA Ops:
  0.9 3.0 %collective-permute-start.2 = (bf16[528,128]{1,0:T(8,128)(2,1)S(1)}, bf16[528,128]{1,0:T(8,128)(2,1)S(1)}, u32[]{:S(2)}, u32[]{:S(2)}) collective-permute-start(bf16[528,128]{1,0:T(8,128)(2,1)S(1)} %start.1.refs_0_), channel_id=1, source_target_pairs={{0,8},{4,12},{8,0},{12,4},{16,24},{20,28},{24,16},{28,20},{1,9},{5... | collective-permute-start | bytes 405512 | tf_op jit(solution)/shard_map/ppermute | solution.py:480
  3.9 1.5 %collective-permute-start.1 = (bf16[528,128]{1,0:T(8,128)(2,1)S(1)}, bf16[528,128]{1,0:T(8,128)(2,1)S(1)}, u32[]{:S(2)}, u32[]{:S(2)}) collective-permute-start(bf16[528,128]{1,0:T(8,128)(2,1)S(1)} %start.1.refs_0_), channel_id=1, source_target_pairs={{0,16},{4,20},{8,24},{12,28},{16,0},{20,4},{24,8},{28,12},{1,17},{... | collective-permute-start | bytes 405512 | tf_op jit(solution)/shard_map/ppermute | solution.py:480
  5.4 3.6 %load.1 = (bf16[16,6,128,128]{3,2,1,0:T(8,128)(2,1)S(1)}, bf16[16,6,128,128]{3,2,1,0:T(8,128)(2,1)S(1)}, f32[2,4,64,128]{3,2,1,0:T(8,128)S(1)}, f32[2,4,128,128]...) custom-call(s32[6,2,16]{2,1,0:T(2,128)} %bitcast.4, s32[2,16]{1,0:T(2,128)} %live.1, ...), custom_call_target="tpu_custom_call" | custom-call | bytes 12582912 | tf_op jit(solution)/shard_map/load/pallas_call | solution.py:262
  9.0 2.8 %collective-permute-done.1.refs_2_ = bf16[528,128]{1,0:T(8,128)(2,1)S(1)} collective-permute-done((bf16[528,128]{1,0:T(8,128)(2,1)S(1)}, bf16[528,128]{1,0:T(8,128)(2,1)S(1)}, u32[]{:S(2)}, u32[]{:S(2)}) %collective-permute-start.1) | collective-permute-done | bytes 135200 | tf_op jit(solution)/shard_map/ppermute | solution.py:480
  14.5 3.7 %collective-permute-start.7 = (s16[272,128]{1,0:T(8,128)(2,1)S(1)}, s16[272,128]{1,0:T(8,128)(2,1)S(1)}, u32[]{:S(2)}, u32[]{:S(2)}) collective-permute-start(s16[272,128]{1,0:T(8,128)(2,1)S(1)} %get-tuple-element.44), channel_id=1, source_target_pairs={{0,3},{1,2},{2,1},{3,0},{4,7},{5,6},{6,5},{7,4},{8,11},{9,10},{10,... | collective-permute-start | bytes 208904 | tf_op jit(solution)/shard_map/ppermute | solution.py:483
  19.0 2.4 %collective-permute-done.7.refs_0_ = s16[272,128]{1,0:T(8,128)(2,1)S(1)} collective-permute-done((s16[272,128]{1,0:T(8,128)(2,1)S(1)}, s16[272,128]{1,0:T(8,128)(2,1)S(1)}, u32[]{:S(2)}, u32[]{:S(2)}) %collective-permute-start.7) | collective-permute-done | bytes 69664 | tf_op jit(solution)/shard_map/ppermute | solution.py:483
  21.4 2.1 %collective-permute-done.8.refs_1_ = s16[272,128]{1,0:T(8,128)(2,1)S(1)} collective-permute-done((s16[272,128]{1,0:T(8,128)(2,1)S(1)}, s16[272,128]{1,0:T(8,128)(2,1)S(1)}, u32[]{:S(2)}, u32[]{:S(2)}) %collective-permute-start.8) | collective-permute-done | bytes 69664 | tf_op jit(solution)/shard_map/ppermute | solution.py:483
  24.5 2.4 %collective-permute-start.12 = (s16[272,128]{1,0:T(8,128)(2,1)S(1)}, s16[272,128]{1,0:T(8,128)(2,1)S(1)}, u32[]{:S(2)}, u32[]{:S(2)}) collective-permute-start(s16[272,128]{1,0:T(8,128)(2,1)S(1)} %solve_0.1.refs_0_), channel_id=1, source_target_pairs={{0,3},{1,2},{2,1},{3,0},{4,7},{5,6},{6,5},{7,4},{8,11},{9,10},{10,... | collective-permute-start | bytes 208904 | tf_op jit(solution)/shard_map/ppermute | solution.py:483
  27.3 1.6 %collective-permute-start.10 = (s16[272,128]{1,0:T(8,128)(2,1)S(1)}, s16[272,128]{1,0:T(8,128)(2,1)S(1)}, u32[]{:S(2)}, u32[]{:S(2)}) collective-permute-start(s16[272,128]{1,0:T(8,128)(2,1)S(1)} %solve_0.1.refs_0_), channel_id=1, source_target_pairs={{0,2},{1,3},{2,0},{3,1},{4,6},{5,7},{6,4},{7,5},{8,10},{9,11},{10,... | collective-permute-start | bytes 208904 | tf_op jit(solution)/shard_map/ppermute | solution.py:483
  29.0 1.6 %route.1 = (s32[8,128]{1,0:T(8,128)S(4)}, s32[8,128]{1,0:T(8,128)S(4)}) custom-call(s32[2,128]{1,0:T(2,128)S(1)} %copy-done, s32[8,128]{1,0:T(8,128)S(1)} %get-tuple-element.33.alive_ref, bf16[528,128]{1,0:T(8,128)(2,1)S(1)} %start.1.refs_0_, bf16[528,128]{1,0:T(8,128)(2,1)S(1)} %collective-permute-done.2.refs_1_, ...), custom_call_target="tpu_custom_call" | custom-call | tf_op jit(solution)/shard_map/route/pallas_call | solution.py:190
  30.8 1.2 %collective-permute-done.11.refs_2_ = s16[272,128]{1,0:T(8,128)(2,1)S(1)} collective-permute-done((s16[272,128]{1,0:T(8,128)(2,1)S(1)}, s16[272,128]{1,0:T(8,128)(2,1)S(1)}, u32[]{:S(2)}, u32[]{:S(2)}) %collective-permute-start.11) | collective-permute-done | bytes 69664 | tf_op jit(solution)/shard_map/ppermute | solution.py:483
  32.9 1.3 %collective-permute-start.13 = (bf16[384,128]{1,0:T(8,128)(2,1)S(1)}, bf16[384,128]{1,0:T(8,128)(2,1)S(1)}, u32[]{:S(2)}, u32[]{:S(2)}) collective-permute-start(bf16[384,128]{1,0:T(8,128)(2,1)S(1)} %get-tuple-element.50), channel_id=1, source_target_pairs={{0,8},{4,12},{8,0},{12,4},{16,24},{20,28},{24,16},{28,20},{1,9},{5... | collective-permute-start | bytes 294920 | tf_op jit(solution)/shard_map/ppermute | solution.py:480
  35.0 1.4 %collective-permute-start.15 = (bf16[384,128]{1,0:T(8,128)(2,1)S(1)}, bf16[384,128]{1,0:T(8,128)(2,1)S(1)}, u32[]{:S(2)}, u32[]{:S(2)}) collective-permute-start(bf16[384,128]{1,0:T(8,128)(2,1)S(1)} %get-tuple-element.52), channel_id=1, source_target_pairs={{0,24},{4,28},{8,16},{12,20},{16,8},{20,12},{24,0},{28,4},{1,25},{... | collective-permute-start | bytes 294920 | tf_op jit(solution)/shard_map/ppermute | solution.py:480
  36.5 1.8 %collective-permute-start.17 = (bf16[384,128]{1,0:T(8,128)(2,1)S(1)}, bf16[384,128]{1,0:T(8,128)(2,1)S(1)}, u32[]{:S(2)}, u32[]{:S(2)}) collective-permute-start(bf16[384,128]{1,0:T(8,128)(2,1)S(1)} %get-tuple-element.54), channel_id=1, source_target_pairs={{0,20},{4,16},{8,28},{12,24},{16,4},{20,0},{24,12},{28,8},{1,21},{... | collective-permute-start | bytes 294920 | tf_op jit(solution)/shard_map/ppermute | solution.py:480
  39.2 1.0 %collective-permute-start.19 = (bf16[384,128]{1,0:T(8,128)(2,1)S(1)}, bf16[384,128]{1,0:T(8,128)(2,1)S(1)}, u32[]{:S(2)}, u32[]{:S(2)}) collective-permute-start(bf16[384,128]{1,0:T(8,128)(2,1)S(1)} %get-tuple-element.56), channel_id=1, source_target_pairs={{0,4},{4,0},{8,12},{12,8},{16,20},{20,16},{24,28},{28,24},{1,5},{5... | collective-permute-start | bytes 294920 | tf_op jit(solution)/shard_map/ppermute | solution.py:480
  42.2 2.5 %collective-permute-done.18.refs_6_ = bf16[384,128]{1,0:T(8,128)(2,1)S(1)} collective-permute-done((bf16[384,128]{1,0:T(8,128)(2,1)S(1)}, bf16[384,128]{1,0:T(8,128)(2,1)S(1)}, u32[]{:S(2)}, u32[]{:S(2)}) %collective-permute-start.18) | collective-permute-done | bytes 98336 | tf_op jit(solution)/shard_map/ppermute | solution.py:480
  45.2 3.3 %collective-permute-start.20 = (s16[272,128]{1,0:T(8,128)(2,1)S(1)}, s16[272,128]{1,0:T(8,128)(2,1)S(1)}, u32[]{:S(2)}, u32[]{:S(2)}) collective-permute-start(s16[272,128]{1,0:T(8,128)(2,1)S(1)} %get-tuple-element.58), channel_id=1, source_target_pairs={{0,3},{1,2},{2,1},{3,0},{4,7},{5,6},{6,5},{7,4},{8,11},{9,10},{10,... | collective-permute-start | bytes 208904 | tf_op jit(solution)/shard_map/ppermute | solution.py:483
  48.5 1.1 %collective-permute-start.22 = (s16[272,128]{1,0:T(8,128)(2,1)S(1)}, s16[272,128]{1,0:T(8,128)(2,1)S(1)}, u32[]{:S(2)}, u32[]{:S(2)}) collective-permute-start(s16[272,128]{1,0:T(8,128)(2,1)S(1)} %get-tuple-element.60), channel_id=1, source_target_pairs={{0,2},{1,3},{2,0},{3,1},{4,6},{5,7},{6,4},{7,5},{8,10},{9,11},{10,... | collective-permute-start | bytes 208904 | tf_op jit(solution)/shard_map/ppermute | solution.py:483
  49.6 2.5 %collective-permute-done.20.refs_0_ = s16[272,128]{1,0:T(8,128)(2,1)S(1)} collective-permute-done((s16[272,128]{1,0:T(8,128)(2,1)S(1)}, s16[272,128]{1,0:T(8,128)(2,1)S(1)}, u32[]{:S(2)}, u32[]{:S(2)}) %collective-permute-start.20) | collective-permute-done | bytes 69664 | tf_op jit(solution)/shard_map/ppermute | solution.py:483
  52.1 1.8 %collective-permute-done.21.refs_1_ = s16[272,128]{1,0:T(8,128)(2,1)S(1)} collective-permute-done((s16[272,128]{1,0:T(8,128)(2,1)S(1)}, s16[272,128]{1,0:T(8,128)(2,1)S(1)}, u32[]{:S(2)}, u32[]{:S(2)}) %collective-permute-start.21) | collective-permute-done | bytes 69664 | tf_op jit(solution)/shard_map/ppermute | solution.py:483
  54.9 3.1 %collective-permute-start.25 = (s16[272,128]{1,0:T(8,128)(2,1)S(1)}, s16[272,128]{1,0:T(8,128)(2,1)S(1)}, u32[]{:S(2)}, u32[]{:S(2)}) collective-permute-start(s16[272,128]{1,0:T(8,128)(2,1)S(1)} %solve_1.1.refs_0_), channel_id=1, source_target_pairs={{0,3},{1,2},{2,1},{3,0},{4,7},{5,6},{6,5},{7,4},{8,11},{9,10},{10,... | collective-permute-start | bytes 208904 | tf_op jit(solution)/shard_map/ppermute | solution.py:483
  58.0 1.4 %collective-permute-start.23 = (s16[272,128]{1,0:T(8,128)(2,1)S(1)}, s16[272,128]{1,0:T(8,128)(2,1)S(1)}, u32[]{:S(2)}, u32[]{:S(2)}) collective-permute-start(s16[272,128]{1,0:T(8,128)(2,1)S(1)} %solve_1.1.refs_0_), channel_id=1, source_target_pairs={{0,2},{1,3},{2,0},{3,1},{4,6},{5,7},{6,4},{7,5},{8,10},{9,11},{10,... | collective-permute-start | bytes 208904 | tf_op jit(solution)/shard_map/ppermute | solution.py:483
  60.2 1.0 %collective-permute-done.25.refs_2_ = s16[272,128]{1,0:T(8,128)(2,1)S(1)} collective-permute-done((s16[272,128]{1,0:T(8,128)(2,1)S(1)}, s16[272,128]{1,0:T(8,128)(2,1)S(1)}, u32[]{:S(2)}, u32[]{:S(2)}) %collective-permute-start.25) | collective-permute-done | bytes 69664 | tf_op jit(solution)/shard_map/ppermute | solution.py:483
  61.1 1.3 %collective-permute-done.24.refs_1_ = s16[272,128]{1,0:T(8,128)(2,1)S(1)} collective-permute-done((s16[272,128]{1,0:T(8,128)(2,1)S(1)}, s16[272,128]{1,0:T(8,128)(2,1)S(1)}, u32[]{:S(2)}, u32[]{:S(2)}) %collective-permute-start.24) | collective-permute-done | bytes 69664 | tf_op jit(solution)/shard_map/ppermute | solution.py:483
  (42 shorter events, 14.6 us)
Async XLA Ops:
  0.9 8.1 %collective-permute-start.2 = (bf16[528,128]{1,0:T(8,128)(2,1)S(1)}, bf16[528,128]{1,0:T(8,128)(2,1)S(1)}, u32[]{:S(2)}, u32[]{:S(2)}) collective-permute-start(bf16[528,128]{1,0:T(8,128)(2,1)S(1)} %start.1.refs_0_), channel_id=1, source_target_pairs={{0,8},{4,12},{8,0},{12,4},{16,24},{20,28},{24,16},{28,20},{1,9},{5... | collective-permute-start | bytes 405512 | tf_op jit(solution)/shard_map/ppermute | solution.py:480
  3.9 7.9 %collective-permute-start.1 = (bf16[528,128]{1,0:T(8,128)(2,1)S(1)}, bf16[528,128]{1,0:T(8,128)(2,1)S(1)}, u32[]{:S(2)}, u32[]{:S(2)}) collective-permute-start(bf16[528,128]{1,0:T(8,128)(2,1)S(1)} %start.1.refs_0_), channel_id=1, source_target_pairs={{0,16},{4,20},{8,24},{12,28},{16,0},{20,4},{24,8},{28,12},{1,17},{... | collective-permute-start | bytes 405512 | tf_op jit(solution)/shard_map/ppermute | solution.py:480
  5.4 6.4 %collective-permute-start = (bf16[528,128]{1,0:T(8,128)(2,1)S(1)}, bf16[528,128]{1,0:T(8,128)(2,1)S(1)}, u32[]{:S(2)}, u32[]{:S(2)}) collective-permute-start(bf16[528,128]{1,0:T(8,128)(2,1)S(1)} %start.1.refs_0_), channel_id=1, source_target_pairs={{0,24},{4,28},{8,16},{12,20},{16,8},{20,12},{24,0},{28,4},{1,25},{... | collective-permute-start | bytes 405512 | tf_op jit(solution)/shard_map/ppermute | solution.py:480
  5.4 6.9 %collective-permute-start.3 = (bf16[528,128]{1,0:T(8,128)(2,1)S(1)}, bf16[528,128]{1,0:T(8,128)(2,1)S(1)}, u32[]{:S(2)}, u32[]{:S(2)}) collective-permute-start(bf16[528,128]{1,0:T(8,128)(2,1)S(1)} %start.1.refs_0_), channel_id=1, source_target_pairs={{0,4},{4,0},{8,12},{12,8},{16,20},{20,16},{24,28},{28,24},{1,5},{5... | collective-permute-start | bytes 405512 | tf_op jit(solution)/shard_map/ppermute | solution.py:480
  11.8 1.5 %collective-permute-start.5 = (bf16[528,128]{1,0:T(8,128)(2,1)S(1)}, bf16[528,128]{1,0:T(8,128)(2,1)S(1)}, u32[]{:S(2)}, u32[]{:S(2)}) collective-permute-start(bf16[528,128]{1,0:T(8,128)(2,1)S(1)} %collective-permute-done.1.refs_2_), channel_id=1, source_target_pairs={{0,4},{4,0},{8,12},{12,8},{16,20},{20,16},{24,28},{28,24},{1,5},{5... | collective-permute-start | bytes 405512 | tf_op jit(solution)/shard_map/ppermute | solution.py:480
  14.5 6.9 %collective-permute-start.7 = (s16[272,128]{1,0:T(8,128)(2,1)S(1)}, s16[272,128]{1,0:T(8,128)(2,1)S(1)}, u32[]{:S(2)}, u32[]{:S(2)}) collective-permute-start(s16[272,128]{1,0:T(8,128)(2,1)S(1)} %get-tuple-element.44), channel_id=1, source_target_pairs={{0,3},{1,2},{2,1},{3,0},{4,7},{5,6},{6,5},{7,4},{8,11},{9,10},{10,... | collective-permute-start | bytes 208904 | tf_op jit(solution)/shard_map/ppermute | solution.py:483
  18.2 5.3 %collective-permute-start.8 = (s16[272,128]{1,0:T(8,128)(2,1)S(1)}, s16[272,128]{1,0:T(8,128)(2,1)S(1)}, u32[]{:S(2)}, u32[]{:S(2)}) collective-permute-start(s16[272,128]{1,0:T(8,128)(2,1)S(1)} %get-tuple-element.45), channel_id=1, source_target_pairs={{0,1},{1,0},{2,3},{3,2},{4,5},{5,4},{6,7},{7,6},{8,9},{9,8},{10,11... | collective-permute-start | bytes 208904 | tf_op jit(solution)/shard_map/ppermute | solution.py:483
  18.2 6.0 %collective-permute-start.9 = (s16[272,128]{1,0:T(8,128)(2,1)S(1)}, s16[272,128]{1,0:T(8,128)(2,1)S(1)}, u32[]{:S(2)}, u32[]{:S(2)}) collective-permute-start(s16[272,128]{1,0:T(8,128)(2,1)S(1)} %get-tuple-element.46), channel_id=1, source_target_pairs={{0,2},{1,3},{2,0},{3,1},{4,6},{5,7},{6,4},{7,5},{8,10},{9,11},{10,... | collective-permute-start | bytes 208904 | tf_op jit(solution)/shard_map/ppermute | solution.py:483
  24.5 6.3 %collective-permute-start.12 = (s16[272,128]{1,0:T(8,128)(2,1)S(1)}, s16[272,128]{1,0:T(8,128)(2,1)S(1)}, u32[]{:S(2)}, u32[]{:S(2)}) collective-permute-start(s16[272,128]{1,0:T(8,128)(2,1)S(1)} %solve_0.1.refs_0_), channel_id=1, source_target_pairs={{0,3},{1,2},{2,1},{3,0},{4,7},{5,6},{6,5},{7,4},{8,11},{9,10},{10,... | collective-permute-start | bytes 208904 | tf_op jit(solution)/shard_map/ppermute | solution.py:483
  26.9 5.1 %collective-permute-start.11 = (s16[272,128]{1,0:T(8,128)(2,1)S(1)}, s16[272,128]{1,0:T(8,128)(2,1)S(1)}, u32[]{:S(2)}, u32[]{:S(2)}) collective-permute-start(s16[272,128]{1,0:T(8,128)(2,1)S(1)} %solve_0.1.refs_0_), channel_id=1, source_target_pairs={{0,1},{1,0},{2,3},{3,2},{4,5},{5,4},{6,7},{7,6},{8,9},{9,8},{10,11... | collective-permute-start | bytes 208904 | tf_op jit(solution)/shard_map/ppermute | solution.py:483
  27.3 5.5 %collective-permute-start.10 = (s16[272,128]{1,0:T(8,128)(2,1)S(1)}, s16[272,128]{1,0:T(8,128)(2,1)S(1)}, u32[]{:S(2)}, u32[]{:S(2)}) collective-permute-start(s16[272,128]{1,0:T(8,128)(2,1)S(1)} %solve_0.1.refs_0_), channel_id=1, source_target_pairs={{0,2},{1,3},{2,0},{3,1},{4,6},{5,7},{6,4},{7,5},{8,10},{9,11},{10,... | collective-permute-start | bytes 208904 | tf_op jit(solution)/shard_map/ppermute | solution.py:483
  32.9 5.4 %collective-permute-start.13 = (bf16[384,128]{1,0:T(8,128)(2,1)S(1)}, bf16[384,128]{1,0:T(8,128)(2,1)S(1)}, u32[]{:S(2)}, u32[]{:S(2)}) collective-permute-start(bf16[384,128]{1,0:T(8,128)(2,1)S(1)} %get-tuple-element.50), channel_id=1, source_target_pairs={{0,8},{4,12},{8,0},{12,4},{16,24},{20,28},{24,16},{28,20},{1,9},{5... | collective-permute-start | bytes 294920 | tf_op jit(solution)/shard_map/ppermute | solution.py:480
  34.2 5.0 %collective-permute-start.14 = (bf16[384,128]{1,0:T(8,128)(2,1)S(1)}, bf16[384,128]{1,0:T(8,128)(2,1)S(1)}, u32[]{:S(2)}, u32[]{:S(2)}) collective-permute-start(bf16[384,128]{1,0:T(8,128)(2,1)S(1)} %get-tuple-element.51), channel_id=1, source_target_pairs={{0,16},{4,20},{8,24},{12,28},{16,0},{20,4},{24,8},{28,12},{1,17},{... | collective-permute-start | bytes 294920 | tf_op jit(solution)/shard_map/ppermute | solution.py:480
  35.0 5.7 %collective-permute-start.15 = (bf16[384,128]{1,0:T(8,128)(2,1)S(1)}, bf16[384,128]{1,0:T(8,128)(2,1)S(1)}, u32[]{:S(2)}, u32[]{:S(2)}) collective-permute-start(bf16[384,128]{1,0:T(8,128)(2,1)S(1)} %get-tuple-element.52), channel_id=1, source_target_pairs={{0,24},{4,28},{8,16},{12,20},{16,8},{20,12},{24,0},{28,4},{1,25},{... | collective-permute-start | bytes 294920 | tf_op jit(solution)/shard_map/ppermute | solution.py:480
  36.5 5.1 %collective-permute-start.16 = (bf16[384,128]{1,0:T(8,128)(2,1)S(1)}, bf16[384,128]{1,0:T(8,128)(2,1)S(1)}, u32[]{:S(2)}, u32[]{:S(2)}) collective-permute-start(bf16[384,128]{1,0:T(8,128)(2,1)S(1)} %get-tuple-element.53), channel_id=1, source_target_pairs={{0,12},{4,8},{8,4},{12,0},{16,28},{20,24},{24,20},{28,16},{1,13},{... | collective-permute-start | bytes 294920 | tf_op jit(solution)/shard_map/ppermute | solution.py:480
  36.5 5.7 %collective-permute-start.17 = (bf16[384,128]{1,0:T(8,128)(2,1)S(1)}, bf16[384,128]{1,0:T(8,128)(2,1)S(1)}, u32[]{:S(2)}, u32[]{:S(2)}) collective-permute-start(bf16[384,128]{1,0:T(8,128)(2,1)S(1)} %get-tuple-element.54), channel_id=1, source_target_pairs={{0,20},{4,16},{8,28},{12,24},{16,4},{20,0},{24,12},{28,8},{1,21},{... | collective-permute-start | bytes 294920 | tf_op jit(solution)/shard_map/ppermute | solution.py:480
  38.3 6.3 %collective-permute-start.18 = (bf16[384,128]{1,0:T(8,128)(2,1)S(1)}, bf16[384,128]{1,0:T(8,128)(2,1)S(1)}, u32[]{:S(2)}, u32[]{:S(2)}) collective-permute-start(bf16[384,128]{1,0:T(8,128)(2,1)S(1)} %get-tuple-element.55), channel_id=1, source_target_pairs={{0,28},{4,24},{8,20},{12,16},{16,12},{20,8},{24,4},{28,0},{1,29},{... | collective-permute-start | bytes 294920 | tf_op jit(solution)/shard_map/ppermute | solution.py:480
  39.2 5.4 %collective-permute-start.19 = (bf16[384,128]{1,0:T(8,128)(2,1)S(1)}, bf16[384,128]{1,0:T(8,128)(2,1)S(1)}, u32[]{:S(2)}, u32[]{:S(2)}) collective-permute-start(bf16[384,128]{1,0:T(8,128)(2,1)S(1)} %get-tuple-element.56), channel_id=1, source_target_pairs={{0,4},{4,0},{8,12},{12,8},{16,20},{20,16},{24,28},{28,24},{1,5},{5... | collective-permute-start | bytes 294920 | tf_op jit(solution)/shard_map/ppermute | solution.py:480
  45.2 6.9 %collective-permute-start.20 = (s16[272,128]{1,0:T(8,128)(2,1)S(1)}, s16[272,128]{1,0:T(8,128)(2,1)S(1)}, u32[]{:S(2)}, u32[]{:S(2)}) collective-permute-start(s16[272,128]{1,0:T(8,128)(2,1)S(1)} %get-tuple-element.58), channel_id=1, source_target_pairs={{0,3},{1,2},{2,1},{3,0},{4,7},{5,6},{6,5},{7,4},{8,11},{9,10},{10,... | collective-permute-start | bytes 208904 | tf_op jit(solution)/shard_map/ppermute | solution.py:483
  48.5 5.4 %collective-permute-start.21 = (s16[272,128]{1,0:T(8,128)(2,1)S(1)}, s16[272,128]{1,0:T(8,128)(2,1)S(1)}, u32[]{:S(2)}, u32[]{:S(2)}) collective-permute-start(s16[272,128]{1,0:T(8,128)(2,1)S(1)} %get-tuple-element.59), channel_id=1, source_target_pairs={{0,1},{1,0},{2,3},{3,2},{4,5},{5,4},{6,7},{7,6},{8,9},{9,8},{10,11... | collective-permute-start | bytes 208904 | tf_op jit(solution)/shard_map/ppermute | solution.py:483
  48.5 6.0 %collective-permute-start.22 = (s16[272,128]{1,0:T(8,128)(2,1)S(1)}, s16[272,128]{1,0:T(8,128)(2,1)S(1)}, u32[]{:S(2)}, u32[]{:S(2)}) collective-permute-start(s16[272,128]{1,0:T(8,128)(2,1)S(1)} %get-tuple-element.60), channel_id=1, source_target_pairs={{0,2},{1,3},{2,0},{3,1},{4,6},{5,7},{6,4},{7,5},{8,10},{9,11},{10,... | collective-permute-start | bytes 208904 | tf_op jit(solution)/shard_map/ppermute | solution.py:483
  54.9 6.3 %collective-permute-start.25 = (s16[272,128]{1,0:T(8,128)(2,1)S(1)}, s16[272,128]{1,0:T(8,128)(2,1)S(1)}, u32[]{:S(2)}, u32[]{:S(2)}) collective-permute-start(s16[272,128]{1,0:T(8,128)(2,1)S(1)} %solve_1.1.refs_0_), channel_id=1, source_target_pairs={{0,3},{1,2},{2,1},{3,0},{4,7},{5,6},{6,5},{7,4},{8,11},{9,10},{10,... | collective-permute-start | bytes 208904 | tf_op jit(solution)/shard_map/ppermute | solution.py:483
  58.0 4.5 %collective-permute-start.24 = (s16[272,128]{1,0:T(8,128)(2,1)S(1)}, s16[272,128]{1,0:T(8,128)(2,1)S(1)}, u32[]{:S(2)}, u32[]{:S(2)}) collective-permute-start(s16[272,128]{1,0:T(8,128)(2,1)S(1)} %solve_1.1.refs_0_), channel_id=1, source_target_pairs={{0,1},{1,0},{2,3},{3,2},{4,5},{5,4},{6,7},{7,6},{8,9},{9,8},{10,11... | collective-permute-start | bytes 208904 | tf_op jit(solution)/shard_map/ppermute | solution.py:483
  58.0 5.3 %collective-permute-start.23 = (s16[272,128]{1,0:T(8,128)(2,1)S(1)}, s16[272,128]{1,0:T(8,128)(2,1)S(1)}, u32[]{:S(2)}, u32[]{:S(2)}) collective-permute-start(s16[272,128]{1,0:T(8,128)(2,1)S(1)} %solve_1.1.refs_0_), channel_id=1, source_target_pairs={{0,2},{1,3},{2,0},{3,1},{4,6},{5,7},{6,4},{7,5},{8,10},{9,11},{10,... | collective-permute-start | bytes 208904 | tf_op jit(solution)/shard_map/ppermute | solution.py:483
  (3 other events, 22.7 us)

commit v7 on v6

--- a/solution.py
+++ b/solution.py
@@ -19,16 +19,26 @@
 PIECES = 4
 
 
-def encode_blocks(values, msg_ref, probes):
-    peaks = [jnp.max(jnp.abs(value), axis=0, keepdims=True) for value in values]
-    peaks += [jnp.zeros((SCALES - len(peaks), msg_ref.shape[1]), F32)] * (len(peaks) < SCALES)
+def peak_of(value):
+    return jnp.max(jnp.abs(value), axis=0, keepdims=True)
+
+
+def scales_of(peaks):
+    lanes = peaks[0].shape[1]
+    padding = -len(peaks) % SCALES
+    peaks = peaks + [jnp.zeros((padding, lanes), F32)] * (padding > 0)
     peaks = jnp.maximum(jnp.max(jnp.concatenate(peaks), axis=1, keepdims=True), 2.0**-100)
-    level = jnp.broadcast_to(jnp.ceil(jnp.log2(peaks) * STEPS), (SCALES, msg_ref.shape[1]))
-    factor = jnp.exp2(15.0 - level * (1.0 / STEPS))
+    level = jnp.broadcast_to(jnp.ceil(jnp.log2(peaks) * STEPS), (peaks.shape[0], lanes))
+    return level, jnp.exp2(15.0 - level * (1.0 / STEPS))
+
+
+def encode_blocks(values, level, factor, msg_ref, probes):
     for k, value in enumerate(values):
         scaled = jnp.clip(jnp.round(value * factor[k : k + 1]), -32767.0, 32767.0)
         msg_ref[k * probes : (k + 1) * probes] = scaled.astype(I32).astype(I16)
-    msg_ref[len(values) * probes :] = level.astype(I32).astype(I16)
+    rows = level.shape[0]
+    tail = jnp.concatenate([level, jnp.zeros((SCALES - rows, level.shape[1]), F32)] if rows < SCALES else [level])
+    msg_ref[len(values) * probes :] = tail.astype(I32).astype(I16)
 
 
 def decode_blocks(msg_ref, count, probes):
@@ -314,7 +324,7 @@
 
 
 def partial_kernel(cols, tail, places, base, parity, idx_ref, blk, *refs):
-    refs, own_ref, msgs, known = refs[: -cols - 1], refs[-cols - 1], refs[-cols:-1], refs[-1]
+    refs, own_ref, msgs, (known, held) = refs[: -cols - 2], refs[-cols - 2], refs[-cols - 1 : -2], refs[-2:]
     ins, start_from = refs[: len(places)], refs[len(places) :]
     rows_dev, slots = blk.shape[:2]
     part = rows_dev // cols
@@ -325,16 +335,23 @@
     else:
         count, pick = slots_of(parity, slots, here)
         picks = [pick(q) for q in range(count)]
+    peaks = []
     for s in list(range(1, cols)) + [0]:
         first = (here ^ s) * part
         sums = [row_product(known, idx_ref, blk, first + k, picks, base) for k in range(part)]
         for ref in start_from:
             sums = [x + ref[first + k] for k, x in enumerate(sums)]
-        if s == 0:
-            for k in range(part):
+        for k in range(part):
+            if s == 0:
                 own_ref[k] = sums[k]
-        else:
-            encode_blocks(sums, msgs[s - 1], own_ref.shape[1])
+            else:
+                held[(s - 1) * part + k] = sums[k]
+                peaks.append(peak_of(sums[k]))
+    level, factor = scales_of(peaks)
+    for s in range(1, cols):
+        at = slice((s - 1) * part, s * part)
+        values = [held[k] for k in range(at.start, at.stop)]
+        encode_blocks(values, level[at], factor[at], msgs[s - 1], own_ref.shape[1])
 
 
 def partial_products(name, cols, probes, idx, blocks, ins, tail, places, base=0, parity=None, start_from=()):
@@ -347,7 +364,10 @@
         out_shape=[jax.ShapeDtypeStruct((part, probes, order), F32)] + [msg] * (cols - 1),
         in_specs=[SMEM] + [VMEM] * (len(ins) + len(start_from) + 1),
         out_specs=[VMEM] * cols,
-        scratch_shapes=[pltpu.VMEM((rows + 1, probes, order), BF16)],
+        scratch_shapes=[
+            pltpu.VMEM((rows + 1, probes, order), BF16),
+            pltpu.VMEM((rows_dev - part, probes, order), F32),
+        ],
         compiler_params=PARAMS,
         name=name,
     )(in_smem(idx), blocks, *ins, *start_from)
@@ -393,7 +413,8 @@
         )
         for k in range(part)
     ]
-    encode_blocks(solved, out_ref, probes)
+    level, factor = scales_of([peak_of(value) for value in solved])
+    encode_blocks(solved, level, factor, out_ref, probes)
 
 
 def solve_part(front, cols, own, msgs, rhs, inverse):
@@ -533,10 +554,10 @@
         [early],
     )
     coded1 = solve_part(1, cols, own1, scatter(msgs1), rhs, inverse)
-    sources = [0] + col_order[-2::-1] + col_order[-1:]
+    sources = [0] + col_order[:1] + col_order[:0:-1]
     all1 = gather(coded1, sources)
-    solved = unpack(1, sources[:-1], all1[:-1], right_side.shape, part, solved)
-    return unpack(1, sources[-1:], all1[-1:], right_side.shape, part, solved)
+    solved = unpack(1, sources[:2], all1[:2], right_side.shape, part, solved)
+    return unpack(1, sources[2:], all1[2:], right_side.shape, part, solved)
 
 
 def solution(mesh):

time: 64.2 us -> 64.3 us (level)
  no operation moved by 1% of the time
where the time goes in v7:
time: 64.3 us; the launch traced here: 64 us
  starting transfers between devices  30.1 us (47%)
  waiting for transfers between devices  22.8 us (35%)
  Pallas kernels  11.1 us (17%)
    ppermute x12, starting transfers between devices, over_cols(): return lax.ppermute(x, 'cols', [(i, i ^ mask) for i in range(cols)])  17.8 us
    ppermute x12, waiting for transfers between devices, over_cols(): return lax.ppermute(x, 'cols', [(i, i ^ mask) for i in range(cols)])  14.6 us
    ppermute x14, starting transfers between devices, over_rows(): return lax.ppermute(x, 'rows', [(i, i ^ mask) for i in range(groups)])  12.3 us
    ppermute x14, waiting for transfers between devices, over_rows(): return lax.ppermute(x, 'rows', [(i, i ^ mask) for i in range(groups)])  8.17 us
    pallas_call x1, Pallas kernels, load(): pl.pallas_call(functools.partial(load_kernel, groups, cols, prior_dev), o...  3.56 us
    pallas_call x3, Pallas kernels, unpack(): pl.pallas_call(functools.partial(unpack_kernel, front, sources), out_shap...  2.31 us
    pallas_call x1, Pallas kernels, route(): pl.pallas_call(functools.partial(route_kernel, groups, cap, slots, prior_...  1.62 us
    pallas_call x2, Pallas kernels, partial_products(): pl.pallas_call(functools.partial(partial_kernel, cols, tail, places, base...  1.35 us
  transfers between devices with their start and end apart: 26, of which 20 were waited for; matrix products, arithmetic and copies ran while one was open for 0% of the time, Pallas kernels for 11%

profile of v7, /device:TPU:0, one launch (start us, length us, event | category | flops | bytes accessed | tf_op | source)
XLA Modules:
  0.0 64.0 jit_solution(5429709326626695168)
XLA Ops:
  0.0 0.9 %start.1.refs_0_ = bf16[528,128]{1,0:T(8,128)(2,1)S(1)} custom-call(s32[6,2,16]{2,1,0:T(2,128)} %bitcast.3, bf16[512,128]{1,0:T(8,128)(2,1)} %bitcast.2), custom_call_target="tpu_custom_call" | custom-call | tf_op jit(solution)/shard_map/start/pallas_call | solution.py:103
  0.9 3.0 %collective-permute-start.2 = (bf16[528,128]{1,0:T(8,128)(2,1)S(1)}, bf16[528,128]{1,0:T(8,128)(2,1)S(1)}, u32[]{:S(2)}, u32[]{:S(2)}) collective-permute-start(bf16[528,128]{1,0:T(8,128)(2,1)S(1)} %start.1.refs_0_), channel_id=1, source_target_pairs={{0,8},{4,12},{8,0},{12,4},{16,24},{20,28},{24,16},{28,20},{1,9},{5... | collective-permute-start | bytes 405512 | tf_op jit(solution)/shard_map/ppermute | solution.py:501
  3.9 1.5 %collective-permute-start.1 = (bf16[528,128]{1,0:T(8,128)(2,1)S(1)}, bf16[528,128]{1,0:T(8,128)(2,1)S(1)}, u32[]{:S(2)}, u32[]{:S(2)}) collective-permute-start(bf16[528,128]{1,0:T(8,128)(2,1)S(1)} %start.1.refs_0_), channel_id=1, source_target_pairs={{0,16},{4,20},{8,24},{12,28},{16,0},{20,4},{24,8},{28,12},{1,17},{... | collective-permute-start | bytes 405512 | tf_op jit(solution)/shard_map/ppermute | solution.py:501
  5.4 3.6 %load.1 = (bf16[16,6,128,128]{3,2,1,0:T(8,128)(2,1)S(1)}, bf16[16,6,128,128]{3,2,1,0:T(8,128)(2,1)S(1)}, f32[2,4,64,128]{3,2,1,0:T(8,128)S(1)}, f32[2,4,128,128]...) custom-call(s32[6,2,16]{2,1,0:T(2,128)} %bitcast.4, s32[2,16]{1,0:T(2,128)} %live.1, ...), custom_call_target="tpu_custom_call" | custom-call | bytes 12582912 | tf_op jit(solution)/shard_map/load/pallas_call | solution.py:272
  9.0 2.8 %collective-permute-done.1.refs_2_ = bf16[528,128]{1,0:T(8,128)(2,1)S(1)} collective-permute-done((bf16[528,128]{1,0:T(8,128)(2,1)S(1)}, bf16[528,128]{1,0:T(8,128)(2,1)S(1)}, u32[]{:S(2)}, u32[]{:S(2)}) %collective-permute-start.1) | collective-permute-done | bytes 135200 | tf_op jit(solution)/shard_map/ppermute | solution.py:501
  14.5 3.7 %collective-permute-start.7 = (s16[272,128]{1,0:T(8,128)(2,1)S(1)}, s16[272,128]{1,0:T(8,128)(2,1)S(1)}, u32[]{:S(2)}, u32[]{:S(2)}) collective-permute-start(s16[272,128]{1,0:T(8,128)(2,1)S(1)} %get-tuple-element.44), channel_id=1, source_target_pairs={{0,3},{1,2},{2,1},{3,0},{4,7},{5,6},{6,5},{7,4},{8,11},{9,10},{10,... | collective-permute-start | bytes 208904 | tf_op jit(solution)/shard_map/ppermute | solution.py:504
  18.9 2.4 %collective-permute-done.7.refs_0_ = s16[272,128]{1,0:T(8,128)(2,1)S(1)} collective-permute-done((s16[272,128]{1,0:T(8,128)(2,1)S(1)}, s16[272,128]{1,0:T(8,128)(2,1)S(1)}, u32[]{:S(2)}, u32[]{:S(2)}) %collective-permute-start.7) | collective-permute-done | bytes 69664 | tf_op jit(solution)/shard_map/ppermute | solution.py:504
  21.4 2.1 %collective-permute-done.8.refs_1_ = s16[272,128]{1,0:T(8,128)(2,1)S(1)} collective-permute-done((s16[272,128]{1,0:T(8,128)(2,1)S(1)}, s16[272,128]{1,0:T(8,128)(2,1)S(1)}, u32[]{:S(2)}, u32[]{:S(2)}) %collective-permute-start.8) | collective-permute-done | bytes 69664 | tf_op jit(solution)/shard_map/ppermute | solution.py:504
  24.5 2.4 %collective-permute-start.12 = (s16[272,128]{1,0:T(8,128)(2,1)S(1)}, s16[272,128]{1,0:T(8,128)(2,1)S(1)}, u32[]{:S(2)}, u32[]{:S(2)}) collective-permute-start(s16[272,128]{1,0:T(8,128)(2,1)S(1)} %solve_0.1.refs_0_), channel_id=1, source_target_pairs={{0,3},{1,2},{2,1},{3,0},{4,7},{5,6},{6,5},{7,4},{8,11},{9,10},{10,... | collective-permute-start | bytes 208904 | tf_op jit(solution)/shard_map/ppermute | solution.py:504
  27.3 1.6 %collective-permute-start.10 = (s16[272,128]{1,0:T(8,128)(2,1)S(1)}, s16[272,128]{1,0:T(8,128)(2,1)S(1)}, u32[]{:S(2)}, u32[]{:S(2)}) collective-permute-start(s16[272,128]{1,0:T(8,128)(2,1)S(1)} %solve_0.1.refs_0_), channel_id=1, source_target_pairs={{0,2},{1,3},{2,0},{3,1},{4,6},{5,7},{6,4},{7,5},{8,10},{9,11},{10,... | collective-permute-start | bytes 208904 | tf_op jit(solution)/shard_map/ppermute | solution.py:504
  29.0 1.6 %route.1 = (s32[8,128]{1,0:T(8,128)S(4)}, s32[8,128]{1,0:T(8,128)S(4)}) custom-call(s32[2,128]{1,0:T(2,128)S(1)} %copy-done, s32[8,128]{1,0:T(8,128)S(1)} %get-tuple-element.33.alive_ref, bf16[528,128]{1,0:T(8,128)(2,1)S(1)} %start.1.refs_0_, bf16[528,128]{1,0:T(8,128)(2,1)S(1)} %collective-permute-done.2.refs_1_, ...), custom_call_target="tpu_custom_call" | custom-call | tf_op jit(solution)/shard_map/route/pallas_call | solution.py:200
  30.8 1.2 %collective-permute-done.11.refs_2_ = s16[272,128]{1,0:T(8,128)(2,1)S(1)} collective-permute-done((s16[272,128]{1,0:T(8,128)(2,1)S(1)}, s16[272,128]{1,0:T(8,128)(2,1)S(1)}, u32[]{:S(2)}, u32[]{:S(2)}) %collective-permute-start.11) | collective-permute-done | bytes 69664 | tf_op jit(solution)/shard_map/ppermute | solution.py:504
  32.9 1.3 %collective-permute-start.13 = (bf16[384,128]{1,0:T(8,128)(2,1)S(1)}, bf16[384,128]{1,0:T(8,128)(2,1)S(1)}, u32[]{:S(2)}, u32[]{:S(2)}) collective-permute-start(bf16[384,128]{1,0:T(8,128)(2,1)S(1)} %get-tuple-element.50), channel_id=1, source_target_pairs={{0,8},{4,12},{8,0},{12,4},{16,24},{20,28},{24,16},{28,20},{1,9},{5... | collective-permute-start | bytes 294920 | tf_op jit(solution)/shard_map/ppermute | solution.py:501
  35.0 1.4 %collective-permute-start.15 = (bf16[384,128]{1,0:T(8,128)(2,1)S(1)}, bf16[384,128]{1,0:T(8,128)(2,1)S(1)}, u32[]{:S(2)}, u32[]{:S(2)}) collective-permute-start(bf16[384,128]{1,0:T(8,128)(2,1)S(1)} %get-tuple-element.52), channel_id=1, source_target_pairs={{0,24},{4,28},{8,16},{12,20},{16,8},{20,12},{24,0},{28,4},{1,25},{... | collective-permute-start | bytes 294920 | tf_op jit(solution)/shard_map/ppermute | solution.py:501
  36.5 1.8 %collective-permute-start.17 = (bf16[384,128]{1,0:T(8,128)(2,1)S(1)}, bf16[384,128]{1,0:T(8,128)(2,1)S(1)}, u32[]{:S(2)}, u32[]{:S(2)}) collective-permute-start(bf16[384,128]{1,0:T(8,128)(2,1)S(1)} %get-tuple-element.54), channel_id=1, source_target_pairs={{0,20},{4,16},{8,28},{12,24},{16,4},{20,0},{24,12},{28,8},{1,21},{... | collective-permute-start | bytes 294920 | tf_op jit(solution)/shard_map/ppermute | solution.py:501
  39.2 1.0 %collective-permute-start.19 = (bf16[384,128]{1,0:T(8,128)(2,1)S(1)}, bf16[384,128]{1,0:T(8,128)(2,1)S(1)}, u32[]{:S(2)}, u32[]{:S(2)}) collective-permute-start(bf16[384,128]{1,0:T(8,128)(2,1)S(1)} %get-tuple-element.56), channel_id=1, source_target_pairs={{0,4},{4,0},{8,12},{12,8},{16,20},{20,16},{24,28},{28,24},{1,5},{5... | collective-permute-start | bytes 294920 | tf_op jit(solution)/shard_map/ppermute | solution.py:501
  42.1 2.5 %collective-permute-done.18.refs_6_ = bf16[384,128]{1,0:T(8,128)(2,1)S(1)} collective-permute-done((bf16[384,128]{1,0:T(8,128)(2,1)S(1)}, bf16[384,128]{1,0:T(8,128)(2,1)S(1)}, u32[]{:S(2)}, u32[]{:S(2)}) %collective-permute-start.18) | collective-permute-done | bytes 98336 | tf_op jit(solution)/shard_map/ppermute | solution.py:501
  45.2 3.3 %collective-permute-start.20 = (s16[272,128]{1,0:T(8,128)(2,1)S(1)}, s16[272,128]{1,0:T(8,128)(2,1)S(1)}, u32[]{:S(2)}, u32[]{:S(2)}) collective-permute-start(s16[272,128]{1,0:T(8,128)(2,1)S(1)} %get-tuple-element.58), channel_id=1, source_target_pairs={{0,3},{1,2},{2,1},{3,0},{4,7},{5,6},{6,5},{7,4},{8,11},{9,10},{10,... | collective-permute-start | bytes 208904 | tf_op jit(solution)/shard_map/ppermute | solution.py:504
  48.5 1.1 %collective-permute-start.22 = (s16[272,128]{1,0:T(8,128)(2,1)S(1)}, s16[272,128]{1,0:T(8,128)(2,1)S(1)}, u32[]{:S(2)}, u32[]{:S(2)}) collective-permute-start(s16[272,128]{1,0:T(8,128)(2,1)S(1)} %get-tuple-element.60), channel_id=1, source_target_pairs={{0,2},{1,3},{2,0},{3,1},{4,6},{5,7},{6,4},{7,5},{8,10},{9,11},{10,... | collective-permute-start | bytes 208904 | tf_op jit(solution)/shard_map/ppermute | solution.py:504
  49.6 2.4 %collective-permute-done.20.refs_0_ = s16[272,128]{1,0:T(8,128)(2,1)S(1)} collective-permute-done((s16[272,128]{1,0:T(8,128)(2,1)S(1)}, s16[272,128]{1,0:T(8,128)(2,1)S(1)}, u32[]{:S(2)}, u32[]{:S(2)}) %collective-permute-start.20) | collective-permute-done | bytes 69664 | tf_op jit(solution)/shard_map/ppermute | solution.py:504
  52.0 1.9 %collective-permute-done.21.refs_1_ = s16[272,128]{1,0:T(8,128)(2,1)S(1)} collective-permute-done((s16[272,128]{1,0:T(8,128)(2,1)S(1)}, s16[272,128]{1,0:T(8,128)(2,1)S(1)}, u32[]{:S(2)}, u32[]{:S(2)}) %collective-permute-start.21) | collective-permute-done | bytes 69664 | tf_op jit(solution)/shard_map/ppermute | solution.py:504
  54.9 3.1 %collective-permute-start.25 = (s16[272,128]{1,0:T(8,128)(2,1)S(1)}, s16[272,128]{1,0:T(8,128)(2,1)S(1)}, u32[]{:S(2)}, u32[]{:S(2)}) collective-permute-start(s16[272,128]{1,0:T(8,128)(2,1)S(1)} %solve_1.1.refs_0_), channel_id=1, source_target_pairs={{0,3},{1,2},{2,1},{3,0},{4,7},{5,6},{6,5},{7,4},{8,11},{9,10},{10,... | collective-permute-start | bytes 208904 | tf_op jit(solution)/shard_map/ppermute | solution.py:504
  58.0 1.3 %collective-permute-start.23 = (s16[272,128]{1,0:T(8,128)(2,1)S(1)}, s16[272,128]{1,0:T(8,128)(2,1)S(1)}, u32[]{:S(2)}, u32[]{:S(2)}) collective-permute-start(s16[272,128]{1,0:T(8,128)(2,1)S(1)} %solve_1.1.refs_0_), channel_id=1, source_target_pairs={{0,2},{1,3},{2,0},{3,1},{4,6},{5,7},{6,4},{7,5},{8,10},{9,11},{10,... | collective-permute-start | bytes 208904 | tf_op jit(solution)/shard_map/ppermute | solution.py:504
  60.2 1.0 %collective-permute-done.25.refs_1_ = s16[272,128]{1,0:T(8,128)(2,1)S(1)} collective-permute-done((s16[272,128]{1,0:T(8,128)(2,1)S(1)}, s16[272,128]{1,0:T(8,128)(2,1)S(1)}, u32[]{:S(2)}, u32[]{:S(2)}) %collective-permute-start.25) | collective-permute-done | bytes 69664 | tf_op jit(solution)/shard_map/ppermute | solution.py:504
  (42 shorter events, 15.0 us)
Async XLA Ops:
  0.9 8.1 %collective-permute-start.2 = (bf16[528,128]{1,0:T(8,128)(2,1)S(1)}, bf16[528,128]{1,0:T(8,128)(2,1)S(1)}, u32[]{:S(2)}, u32[]{:S(2)}) collective-permute-start(bf16[528,128]{1,0:T(8,128)(2,1)S(1)} %start.1.refs_0_), channel_id=1, source_target_pairs={{0,8},{4,12},{8,0},{12,4},{16,24},{20,28},{24,16},{28,20},{1,9},{5... | collective-permute-start | bytes 405512 | tf_op jit(solution)/shard_map/ppermute | solution.py:501
  3.9 7.9 %collective-permute-start.1 = (bf16[528,128]{1,0:T(8,128)(2,1)S(1)}, bf16[528,128]{1,0:T(8,128)(2,1)S(1)}, u32[]{:S(2)}, u32[]{:S(2)}) collective-permute-start(bf16[528,128]{1,0:T(8,128)(2,1)S(1)} %start.1.refs_0_), channel_id=1, source_target_pairs={{0,16},{4,20},{8,24},{12,28},{16,0},{20,4},{24,8},{28,12},{1,17},{... | collective-permute-start | bytes 405512 | tf_op jit(solution)/shard_map/ppermute | solution.py:501
  5.4 6.4 %collective-permute-start = (bf16[528,128]{1,0:T(8,128)(2,1)S(1)}, bf16[528,128]{1,0:T(8,128)(2,1)S(1)}, u32[]{:S(2)}, u32[]{:S(2)}) collective-permute-start(bf16[528,128]{1,0:T(8,128)(2,1)S(1)} %start.1.refs_0_), channel_id=1, source_target_pairs={{0,24},{4,28},{8,16},{12,20},{16,8},{20,12},{24,0},{28,4},{1,25},{... | collective-permute-start | bytes 405512 | tf_op jit(solution)/shard_map/ppermute | solution.py:501
  5.4 6.9 %collective-permute-start.3 = (bf16[528,128]{1,0:T(8,128)(2,1)S(1)}, bf16[528,128]{1,0:T(8,128)(2,1)S(1)}, u32[]{:S(2)}, u32[]{:S(2)}) collective-permute-start(bf16[528,128]{1,0:T(8,128)(2,1)S(1)} %start.1.refs_0_), channel_id=1, source_target_pairs={{0,4},{4,0},{8,12},{12,8},{16,20},{20,16},{24,28},{28,24},{1,5},{5... | collective-permute-start | bytes 405512 | tf_op jit(solution)/shard_map/ppermute | solution.py:501
  11.8 1.5 %collective-permute-start.5 = (bf16[528,128]{1,0:T(8,128)(2,1)S(1)}, bf16[528,128]{1,0:T(8,128)(2,1)S(1)}, u32[]{:S(2)}, u32[]{:S(2)}) collective-permute-start(bf16[528,128]{1,0:T(8,128)(2,1)S(1)} %collective-permute-done.1.refs_2_), channel_id=1, source_target_pairs={{0,4},{4,0},{8,12},{12,8},{16,20},{20,16},{24,28},{28,24},{1,5},{5... | collective-permute-start | bytes 405512 | tf_op jit(solution)/shard_map/ppermute | solution.py:501
  14.5 6.9 %collective-permute-start.7 = (s16[272,128]{1,0:T(8,128)(2,1)S(1)}, s16[272,128]{1,0:T(8,128)(2,1)S(1)}, u32[]{:S(2)}, u32[]{:S(2)}) collective-permute-start(s16[272,128]{1,0:T(8,128)(2,1)S(1)} %get-tuple-element.44), channel_id=1, source_target_pairs={{0,3},{1,2},{2,1},{3,0},{4,7},{5,6},{6,5},{7,4},{8,11},{9,10},{10,... | collective-permute-start | bytes 208904 | tf_op jit(solution)/shard_map/ppermute | solution.py:504
  18.2 5.3 %collective-permute-start.8 = (s16[272,128]{1,0:T(8,128)(2,1)S(1)}, s16[272,128]{1,0:T(8,128)(2,1)S(1)}, u32[]{:S(2)}, u32[]{:S(2)}) collective-permute-start(s16[272,128]{1,0:T(8,128)(2,1)S(1)} %get-tuple-element.45), channel_id=1, source_target_pairs={{0,1},{1,0},{2,3},{3,2},{4,5},{5,4},{6,7},{7,6},{8,9},{9,8},{10,11... | collective-permute-start | bytes 208904 | tf_op jit(solution)/shard_map/ppermute | solution.py:504
  18.2 6.0 %collective-permute-start.9 = (s16[272,128]{1,0:T(8,128)(2,1)S(1)}, s16[272,128]{1,0:T(8,128)(2,1)S(1)}, u32[]{:S(2)}, u32[]{:S(2)}) collective-permute-start(s16[272,128]{1,0:T(8,128)(2,1)S(1)} %get-tuple-element.46), channel_id=1, source_target_pairs={{0,2},{1,3},{2,0},{3,1},{4,6},{5,7},{6,4},{7,5},{8,10},{9,11},{10,... | collective-permute-start | bytes 208904 | tf_op jit(solution)/shard_map/ppermute | solution.py:504
  24.5 6.3 %collective-permute-start.12 = (s16[272,128]{1,0:T(8,128)(2,1)S(1)}, s16[272,128]{1,0:T(8,128)(2,1)S(1)}, u32[]{:S(2)}, u32[]{:S(2)}) collective-permute-start(s16[272,128]{1,0:T(8,128)(2,1)S(1)} %solve_0.1.refs_0_), channel_id=1, source_target_pairs={{0,3},{1,2},{2,1},{3,0},{4,7},{5,6},{6,5},{7,4},{8,11},{9,10},{10,... | collective-permute-start | bytes 208904 | tf_op jit(solution)/shard_map/ppermute | solution.py:504
  26.9 5.0 %collective-permute-start.11 = (s16[272,128]{1,0:T(8,128)(2,1)S(1)}, s16[272,128]{1,0:T(8,128)(2,1)S(1)}, u32[]{:S(2)}, u32[]{:S(2)}) collective-permute-start(s16[272,128]{1,0:T(8,128)(2,1)S(1)} %solve_0.1.refs_0_), channel_id=1, source_target_pairs={{0,1},{1,0},{2,3},{3,2},{4,5},{5,4},{6,7},{7,6},{8,9},{9,8},{10,11... | collective-permute-start | bytes 208904 | tf_op jit(solution)/shard_map/ppermute | solution.py:504
  27.3 5.5 %collective-permute-start.10 = (s16[272,128]{1,0:T(8,128)(2,1)S(1)}, s16[272,128]{1,0:T(8,128)(2,1)S(1)}, u32[]{:S(2)}, u32[]{:S(2)}) collective-permute-start(s16[272,128]{1,0:T(8,128)(2,1)S(1)} %solve_0.1.refs_0_), channel_id=1, source_target_pairs={{0,2},{1,3},{2,0},{3,1},{4,6},{5,7},{6,4},{7,5},{8,10},{9,11},{10,... | collective-permute-start | bytes 208904 | tf_op jit(solution)/shard_map/ppermute | solution.py:504
  32.9 5.4 %collective-permute-start.13 = (bf16[384,128]{1,0:T(8,128)(2,1)S(1)}, bf16[384,128]{1,0:T(8,128)(2,1)S(1)}, u32[]{:S(2)}, u32[]{:S(2)}) collective-permute-start(bf16[384,128]{1,0:T(8,128)(2,1)S(1)} %get-tuple-element.50), channel_id=1, source_target_pairs={{0,8},{4,12},{8,0},{12,4},{16,24},{20,28},{24,16},{28,20},{1,9},{5... | collective-permute-start | bytes 294920 | tf_op jit(solution)/shard_map/ppermute | solution.py:501
  34.2 5.0 %collective-permute-start.14 = (bf16[384,128]{1,0:T(8,128)(2,1)S(1)}, bf16[384,128]{1,0:T(8,128)(2,1)S(1)}, u32[]{:S(2)}, u32[]{:S(2)}) collective-permute-start(bf16[384,128]{1,0:T(8,128)(2,1)S(1)} %get-tuple-element.51), channel_id=1, source_target_pairs={{0,16},{4,20},{8,24},{12,28},{16,0},{20,4},{24,8},{28,12},{1,17},{... | collective-permute-start | bytes 294920 | tf_op jit(solution)/shard_map/ppermute | solution.py:501
  35.0 5.7 %collective-permute-start.15 = (bf16[384,128]{1,0:T(8,128)(2,1)S(1)}, bf16[384,128]{1,0:T(8,128)(2,1)S(1)}, u32[]{:S(2)}, u32[]{:S(2)}) collective-permute-start(bf16[384,128]{1,0:T(8,128)(2,1)S(1)} %get-tuple-element.52), channel_id=1, source_target_pairs={{0,24},{4,28},{8,16},{12,20},{16,8},{20,12},{24,0},{28,4},{1,25},{... | collective-permute-start | bytes 294920 | tf_op jit(solution)/shard_map/ppermute | solution.py:501
  36.5 5.1 %collective-permute-start.16 = (bf16[384,128]{1,0:T(8,128)(2,1)S(1)}, bf16[384,128]{1,0:T(8,128)(2,1)S(1)}, u32[]{:S(2)}, u32[]{:S(2)}) collective-permute-start(bf16[384,128]{1,0:T(8,128)(2,1)S(1)} %get-tuple-element.53), channel_id=1, source_target_pairs={{0,12},{4,8},{8,4},{12,0},{16,28},{20,24},{24,20},{28,16},{1,13},{... | collective-permute-start | bytes 294920 | tf_op jit(solution)/shard_map/ppermute | solution.py:501
  36.5 5.7 %collective-permute-start.17 = (bf16[384,128]{1,0:T(8,128)(2,1)S(1)}, bf16[384,128]{1,0:T(8,128)(2,1)S(1)}, u32[]{:S(2)}, u32[]{:S(2)}) collective-permute-start(bf16[384,128]{1,0:T(8,128)(2,1)S(1)} %get-tuple-element.54), channel_id=1, source_target_pairs={{0,20},{4,16},{8,28},{12,24},{16,4},{20,0},{24,12},{28,8},{1,21},{... | collective-permute-start | bytes 294920 | tf_op jit(solution)/shard_map/ppermute | solution.py:501
  38.3 6.3 %collective-permute-start.18 = (bf16[384,128]{1,0:T(8,128)(2,1)S(1)}, bf16[384,128]{1,0:T(8,128)(2,1)S(1)}, u32[]{:S(2)}, u32[]{:S(2)}) collective-permute-start(bf16[384,128]{1,0:T(8,128)(2,1)S(1)} %get-tuple-element.55), channel_id=1, source_target_pairs={{0,28},{4,24},{8,20},{12,16},{16,12},{20,8},{24,4},{28,0},{1,29},{... | collective-permute-start | bytes 294920 | tf_op jit(solution)/shard_map/ppermute | solution.py:501
  39.2 5.4 %collective-permute-start.19 = (bf16[384,128]{1,0:T(8,128)(2,1)S(1)}, bf16[384,128]{1,0:T(8,128)(2,1)S(1)}, u32[]{:S(2)}, u32[]{:S(2)}) collective-permute-start(bf16[384,128]{1,0:T(8,128)(2,1)S(1)} %get-tuple-element.56), channel_id=1, source_target_pairs={{0,4},{4,0},{8,12},{12,8},{16,20},{20,16},{24,28},{28,24},{1,5},{5... | collective-permute-start | bytes 294920 | tf_op jit(solution)/shard_map/ppermute | solution.py:501
  45.2 6.8 %collective-permute-start.20 = (s16[272,128]{1,0:T(8,128)(2,1)S(1)}, s16[272,128]{1,0:T(8,128)(2,1)S(1)}, u32[]{:S(2)}, u32[]{:S(2)}) collective-permute-start(s16[272,128]{1,0:T(8,128)(2,1)S(1)} %get-tuple-element.58), channel_id=1, source_target_pairs={{0,3},{1,2},{2,1},{3,0},{4,7},{5,6},{6,5},{7,4},{8,11},{9,10},{10,... | collective-permute-start | bytes 208904 | tf_op jit(solution)/shard_map/ppermute | solution.py:504
  48.5 5.4 %collective-permute-start.21 = (s16[272,128]{1,0:T(8,128)(2,1)S(1)}, s16[272,128]{1,0:T(8,128)(2,1)S(1)}, u32[]{:S(2)}, u32[]{:S(2)}) collective-permute-start(s16[272,128]{1,0:T(8,128)(2,1)S(1)} %get-tuple-element.59), channel_id=1, source_target_pairs={{0,1},{1,0},{2,3},{3,2},{4,5},{5,4},{6,7},{7,6},{8,9},{9,8},{10,11... | collective-permute-start | bytes 208904 | tf_op jit(solution)/shard_map/ppermute | solution.py:504
  48.5 6.0 %collective-permute-start.22 = (s16[272,128]{1,0:T(8,128)(2,1)S(1)}, s16[272,128]{1,0:T(8,128)(2,1)S(1)}, u32[]{:S(2)}, u32[]{:S(2)}) collective-permute-start(s16[272,128]{1,0:T(8,128)(2,1)S(1)} %get-tuple-element.60), channel_id=1, source_target_pairs={{0,2},{1,3},{2,0},{3,1},{4,6},{5,7},{6,4},{7,5},{8,10},{9,11},{10,... | collective-permute-start | bytes 208904 | tf_op jit(solution)/shard_map/ppermute | solution.py:504
  54.9 6.3 %collective-permute-start.25 = (s16[272,128]{1,0:T(8,128)(2,1)S(1)}, s16[272,128]{1,0:T(8,128)(2,1)S(1)}, u32[]{:S(2)}, u32[]{:S(2)}) collective-permute-start(s16[272,128]{1,0:T(8,128)(2,1)S(1)} %solve_1.1.refs_0_), channel_id=1, source_target_pairs={{0,3},{1,2},{2,1},{3,0},{4,7},{5,6},{6,5},{7,4},{8,11},{9,10},{10,... | collective-permute-start | bytes 208904 | tf_op jit(solution)/shard_map/ppermute | solution.py:504
  58.0 4.4 %collective-permute-start.24 = (s16[272,128]{1,0:T(8,128)(2,1)S(1)}, s16[272,128]{1,0:T(8,128)(2,1)S(1)}, u32[]{:S(2)}, u32[]{:S(2)}) collective-permute-start(s16[272,128]{1,0:T(8,128)(2,1)S(1)} %solve_1.1.refs_0_), channel_id=1, source_target_pairs={{0,1},{1,0},{2,3},{3,2},{4,5},{5,4},{6,7},{7,6},{8,9},{9,8},{10,11... | collective-permute-start | bytes 208904 | tf_op jit(solution)/shard_map/ppermute | solution.py:504
  58.0 5.3 %collective-permute-start.23 = (s16[272,128]{1,0:T(8,128)(2,1)S(1)}, s16[272,128]{1,0:T(8,128)(2,1)S(1)}, u32[]{:S(2)}, u32[]{:S(2)}) collective-permute-start(s16[272,128]{1,0:T(8,128)(2,1)S(1)} %solve_1.1.refs_0_), channel_id=1, source_target_pairs={{0,2},{1,3},{2,0},{3,1},{4,6},{5,7},{6,4},{7,5},{8,10},{9,11},{10,... | collective-permute-start | bytes 208904 | tf_op jit(solution)/shard_map/ppermute | solution.py:504
  (3 other events, 22.7 us)

commit v8 on v6

--- a/solution.py
+++ b/solution.py
@@ -493,14 +493,15 @@
 
     colidx = jnp.transpose(colidx, (2, 0, 1))
     own = start(colidx, prior)
-    peers = [m for m in row_order if m % 2 == 0][::-1]
+    peers = [m + (m.bit_count() > 1) for m in row_order if m % 2 == 0][::-1]
     chips = [over_rows(own, m) for m in peers]
     blocks0, blocks1, rhs, inverse, alive, first_at = load(
         groups, cols, prior_dev, colidx, live, blocks, right_side, diag_inverse
     )
     chips, blocks0 = lax.optimization_barrier((chips, blocks0))
-    chips = [own] + [chips[peers.index(2 * k)] for k in range(1, half)]
-    pieces = chips + [over_rows(x, 1) for x in chips]
+    held = {0: own} | dict(zip(peers, chips))
+    held |= {m ^ 1: over_rows(held[m], 1) for m in [0] + peers[::-1]}
+    pieces = [held[2 * k] for k in range(half)] + [held[2 * k + 1] for k in range(half)]
     early_at = [g * prior_dev for g in range(groups)]
     want, second_at = route(groups, cap, slots, prior_dev, owner_map, alive, pieces)
 

time: 64.2 us -> 64.2 us (level)
  transfers between devices with their start and end apart: 26 -> 26, of which waited for: 20 -> 19; matrix products, arithmetic and copies ran while one was open for 0% -> 0% of each run, Pallas kernels for 11% -> 11%
where the time goes in v8:
time: 64.2 us; the launch traced here: 64 us
  starting transfers between devices  30.2 us (47%)
  waiting for transfers between devices  22.5 us (35%)
  Pallas kernels  11.1 us (17%)
    ppermute x12, starting transfers between devices, over_cols(): return lax.ppermute(x, 'cols', [(i, i ^ mask) for i in range(cols)])  17.8 us
    ppermute x12, waiting for transfers between devices, over_cols(): return lax.ppermute(x, 'cols', [(i, i ^ mask) for i in range(cols)])  14.5 us
    ppermute x14, starting transfers between devices, over_rows(): return lax.ppermute(x, 'rows', [(i, i ^ mask) for i in range(groups)])  12.4 us
    ppermute x14, waiting for transfers between devices, over_rows(): return lax.ppermute(x, 'rows', [(i, i ^ mask) for i in range(groups)])  8 us
    pallas_call x1, Pallas kernels, load(): pl.pallas_call(functools.partial(load_kernel, groups, cols, prior_dev), o...  3.56 us
    pallas_call x3, Pallas kernels, unpack(): pl.pallas_call(functools.partial(unpack_kernel, front, sources), out_shap...  2.31 us
    pallas_call x1, Pallas kernels, route(): pl.pallas_call(functools.partial(route_kernel, groups, cap, slots, prior_...  1.62 us
    pallas_call x2, Pallas kernels, partial_products(): pl.pallas_call(functools.partial(partial_kernel, cols, tail, places, base...  1.35 us
  transfers between devices with their start and end apart: 26, of which 19 were waited for; matrix products, arithmetic and copies ran while one was open for 0% of the time, Pallas kernels for 11%

profile of v8, /device:TPU:0, one launch (start us, length us, event | category | flops | bytes accessed | tf_op | source)
XLA Modules:
  0.0 64.0 jit_solution(1790226545741821482)
XLA Ops:
  0.9 3.0 %collective-permute-start.2 = (bf16[528,128]{1,0:T(8,128)(2,1)S(1)}, bf16[528,128]{1,0:T(8,128)(2,1)S(1)}, u32[]{:S(2)}, u32[]{:S(2)}) collective-permute-start(bf16[528,128]{1,0:T(8,128)(2,1)S(1)} %start.1.refs_0_), channel_id=1, source_target_pairs={{0,8},{4,12},{8,0},{12,4},{16,24},{20,28},{24,16},{28,20},{1,9},{5... | collective-permute-start | bytes 405512 | tf_op jit(solution)/shard_map/ppermute | solution.py:480
  3.9 1.5 %collective-permute-start.1 = (bf16[528,128]{1,0:T(8,128)(2,1)S(1)}, bf16[528,128]{1,0:T(8,128)(2,1)S(1)}, u32[]{:S(2)}, u32[]{:S(2)}) collective-permute-start(bf16[528,128]{1,0:T(8,128)(2,1)S(1)} %start.1.refs_0_), channel_id=1, source_target_pairs={{0,16},{4,20},{8,24},{12,28},{16,0},{20,4},{24,8},{28,12},{1,17},{... | collective-permute-start | bytes 405512 | tf_op jit(solution)/shard_map/ppermute | solution.py:480
  5.5 3.6 %load.1 = (bf16[16,6,128,128]{3,2,1,0:T(8,128)(2,1)S(1)}, bf16[16,6,128,128]{3,2,1,0:T(8,128)(2,1)S(1)}, f32[2,4,64,128]{3,2,1,0:T(8,128)S(1)}, f32[2,4,128,128]...) custom-call(s32[6,2,16]{2,1,0:T(2,128)} %bitcast.4, s32[2,16]{1,0:T(2,128)} %live.1, ...), custom_call_target="tpu_custom_call" | custom-call | bytes 12582912 | tf_op jit(solution)/shard_map/load/pallas_call | solution.py:262
  9.1 2.7 %collective-permute-done.1.refs_2_ = bf16[528,128]{1,0:T(8,128)(2,1)S(1)} collective-permute-done((bf16[528,128]{1,0:T(8,128)(2,1)S(1)}, bf16[528,128]{1,0:T(8,128)(2,1)S(1)}, u32[]{:S(2)}, u32[]{:S(2)}) %collective-permute-start.1) | collective-permute-done | bytes 135200 | tf_op jit(solution)/shard_map/ppermute | solution.py:480
  14.5 3.7 %collective-permute-start.7 = (s16[272,128]{1,0:T(8,128)(2,1)S(1)}, s16[272,128]{1,0:T(8,128)(2,1)S(1)}, u32[]{:S(2)}, u32[]{:S(2)}) collective-permute-start(s16[272,128]{1,0:T(8,128)(2,1)S(1)} %get-tuple-element.44), channel_id=1, source_target_pairs={{0,3},{1,2},{2,1},{3,0},{4,7},{5,6},{6,5},{7,4},{8,11},{9,10},{10,... | collective-permute-start | bytes 208904 | tf_op jit(solution)/shard_map/ppermute | solution.py:483
  19.0 2.4 %collective-permute-done.7.refs_0_ = s16[272,128]{1,0:T(8,128)(2,1)S(1)} collective-permute-done((s16[272,128]{1,0:T(8,128)(2,1)S(1)}, s16[272,128]{1,0:T(8,128)(2,1)S(1)}, u32[]{:S(2)}, u32[]{:S(2)}) %collective-permute-start.7) | collective-permute-done | bytes 69664 | tf_op jit(solution)/shard_map/ppermute | solution.py:483
  21.4 2.1 %collective-permute-done.8.refs_1_ = s16[272,128]{1,0:T(8,128)(2,1)S(1)} collective-permute-done((s16[272,128]{1,0:T(8,128)(2,1)S(1)}, s16[272,128]{1,0:T(8,128)(2,1)S(1)}, u32[]{:S(2)}, u32[]{:S(2)}) %collective-permute-start.8) | collective-permute-done | bytes 69664 | tf_op jit(solution)/shard_map/ppermute | solution.py:483
  24.5 2.4 %collective-permute-start.12 = (s16[272,128]{1,0:T(8,128)(2,1)S(1)}, s16[272,128]{1,0:T(8,128)(2,1)S(1)}, u32[]{:S(2)}, u32[]{:S(2)}) collective-permute-start(s16[272,128]{1,0:T(8,128)(2,1)S(1)} %solve_0.1.refs_0_), channel_id=1, source_target_pairs={{0,3},{1,2},{2,1},{3,0},{4,7},{5,6},{6,5},{7,4},{8,11},{9,10},{10,... | collective-permute-start | bytes 208904 | tf_op jit(solution)/shard_map/ppermute | solution.py:483
  27.3 1.6 %collective-permute-start.10 = (s16[272,128]{1,0:T(8,128)(2,1)S(1)}, s16[272,128]{1,0:T(8,128)(2,1)S(1)}, u32[]{:S(2)}, u32[]{:S(2)}) collective-permute-start(s16[272,128]{1,0:T(8,128)(2,1)S(1)} %solve_0.1.refs_0_), channel_id=1, source_target_pairs={{0,2},{1,3},{2,0},{3,1},{4,6},{5,7},{6,4},{7,5},{8,10},{9,11},{10,... | collective-permute-start | bytes 208904 | tf_op jit(solution)/shard_map/ppermute | solution.py:483
  29.0 1.6 %route.1 = (s32[8,128]{1,0:T(8,128)S(4)}, s32[8,128]{1,0:T(8,128)S(4)}) custom-call(s32[2,128]{1,0:T(2,128)S(1)} %copy-done, s32[8,128]{1,0:T(8,128)S(1)} %get-tuple-element.33.alive_ref, bf16[528,128]{1,0:T(8,128)(2,1)S(1)} %start.1.refs_0_, bf16[528,128]{1,0:T(8,128)(2,1)S(1)} %collective-permute-done.2.refs_1_, ...), custom_call_target="tpu_custom_call" | custom-call | tf_op jit(solution)/shard_map/route/pallas_call | solution.py:190
  30.8 1.2 %collective-permute-done.11.refs_2_ = s16[272,128]{1,0:T(8,128)(2,1)S(1)} collective-permute-done((s16[272,128]{1,0:T(8,128)(2,1)S(1)}, s16[272,128]{1,0:T(8,128)(2,1)S(1)}, u32[]{:S(2)}, u32[]{:S(2)}) %collective-permute-start.11) | collective-permute-done | bytes 69664 | tf_op jit(solution)/shard_map/ppermute | solution.py:483
  32.9 1.0 %collective-permute-start.13 = (bf16[384,128]{1,0:T(8,128)(2,1)S(1)}, bf16[384,128]{1,0:T(8,128)(2,1)S(1)}, u32[]{:S(2)}, u32[]{:S(2)}) collective-permute-start(bf16[384,128]{1,0:T(8,128)(2,1)S(1)} %get-tuple-element.50), channel_id=1, source_target_pairs={{0,8},{4,12},{8,0},{12,4},{16,24},{20,28},{24,16},{28,20},{1,9},{5... | collective-permute-start | bytes 294920 | tf_op jit(solution)/shard_map/ppermute | solution.py:480
  33.9 1.1 %collective-permute-start.14 = (bf16[384,128]{1,0:T(8,128)(2,1)S(1)}, bf16[384,128]{1,0:T(8,128)(2,1)S(1)}, u32[]{:S(2)}, u32[]{:S(2)}) collective-permute-start(bf16[384,128]{1,0:T(8,128)(2,1)S(1)} %get-tuple-element.51), channel_id=1, source_target_pairs={{0,16},{4,20},{8,24},{12,28},{16,0},{20,4},{24,8},{28,12},{1,17},{... | collective-permute-start | bytes 294920 | tf_op jit(solution)/shard_map/ppermute | solution.py:480
  35.1 1.4 %collective-permute-start.15 = (bf16[384,128]{1,0:T(8,128)(2,1)S(1)}, bf16[384,128]{1,0:T(8,128)(2,1)S(1)}, u32[]{:S(2)}, u32[]{:S(2)}) collective-permute-start(bf16[384,128]{1,0:T(8,128)(2,1)S(1)} %get-tuple-element.52), channel_id=1, source_target_pairs={{0,24},{4,28},{8,16},{12,20},{16,8},{20,12},{24,0},{28,4},{1,25},{... | collective-permute-start | bytes 294920 | tf_op jit(solution)/shard_map/ppermute | solution.py:480
  36.5 1.8 %collective-permute-start.17 = (bf16[384,128]{1,0:T(8,128)(2,1)S(1)}, bf16[384,128]{1,0:T(8,128)(2,1)S(1)}, u32[]{:S(2)}, u32[]{:S(2)}) collective-permute-start(bf16[384,128]{1,0:T(8,128)(2,1)S(1)} %get-tuple-element.54), channel_id=1, source_target_pairs={{0,20},{4,16},{8,28},{12,24},{16,4},{20,0},{24,12},{28,8},{1,21},{... | collective-permute-start | bytes 294920 | tf_op jit(solution)/shard_map/ppermute | solution.py:480
  41.5 1.0 %collective-permute-done.17.refs_5_ = bf16[384,128]{1,0:T(8,128)(2,1)S(1)} collective-permute-done((bf16[384,128]{1,0:T(8,128)(2,1)S(1)}, bf16[384,128]{1,0:T(8,128)(2,1)S(1)}, u32[]{:S(2)}, u32[]{:S(2)}) %collective-permute-start.17) | collective-permute-done | bytes 98336 | tf_op jit(solution)/shard_map/ppermute | solution.py:480
  42.5 2.1 %collective-permute-done.18.refs_6_ = bf16[384,128]{1,0:T(8,128)(2,1)S(1)} collective-permute-done((bf16[384,128]{1,0:T(8,128)(2,1)S(1)}, bf16[384,128]{1,0:T(8,128)(2,1)S(1)}, u32[]{:S(2)}, u32[]{:S(2)}) %collective-permute-start.18) | collective-permute-done | bytes 98336 | tf_op jit(solution)/shard_map/ppermute | solution.py:480
  45.2 3.3 %collective-permute-start.20 = (s16[272,128]{1,0:T(8,128)(2,1)S(1)}, s16[272,128]{1,0:T(8,128)(2,1)S(1)}, u32[]{:S(2)}, u32[]{:S(2)}) collective-permute-start(s16[272,128]{1,0:T(8,128)(2,1)S(1)} %get-tuple-element.58), channel_id=1, source_target_pairs={{0,3},{1,2},{2,1},{3,0},{4,7},{5,6},{6,5},{7,4},{8,11},{9,10},{10,... | collective-permute-start | bytes 208904 | tf_op jit(solution)/shard_map/ppermute | solution.py:483
  48.5 1.1 %collective-permute-start.22 = (s16[272,128]{1,0:T(8,128)(2,1)S(1)}, s16[272,128]{1,0:T(8,128)(2,1)S(1)}, u32[]{:S(2)}, u32[]{:S(2)}) collective-permute-start(s16[272,128]{1,0:T(8,128)(2,1)S(1)} %get-tuple-element.60), channel_id=1, source_target_pairs={{0,2},{1,3},{2,0},{3,1},{4,6},{5,7},{6,4},{7,5},{8,10},{9,11},{10,... | collective-permute-start | bytes 208904 | tf_op jit(solution)/shard_map/ppermute | solution.py:483
  49.6 2.5 %collective-permute-done.20.refs_0_ = s16[272,128]{1,0:T(8,128)(2,1)S(1)} collective-permute-done((s16[272,128]{1,0:T(8,128)(2,1)S(1)}, s16[272,128]{1,0:T(8,128)(2,1)S(1)}, u32[]{:S(2)}, u32[]{:S(2)}) %collective-permute-start.20) | collective-permute-done | bytes 69664 | tf_op jit(solution)/shard_map/ppermute | solution.py:483
  52.1 1.8 %collective-permute-done.21.refs_1_ = s16[272,128]{1,0:T(8,128)(2,1)S(1)} collective-permute-done((s16[272,128]{1,0:T(8,128)(2,1)S(1)}, s16[272,128]{1,0:T(8,128)(2,1)S(1)}, u32[]{:S(2)}, u32[]{:S(2)}) %collective-permute-start.21) | collective-permute-done | bytes 69664 | tf_op jit(solution)/shard_map/ppermute | solution.py:483
  54.9 3.1 %collective-permute-start.25 = (s16[272,128]{1,0:T(8,128)(2,1)S(1)}, s16[272,128]{1,0:T(8,128)(2,1)S(1)}, u32[]{:S(2)}, u32[]{:S(2)}) collective-permute-start(s16[272,128]{1,0:T(8,128)(2,1)S(1)} %solve_1.1.refs_0_), channel_id=1, source_target_pairs={{0,3},{1,2},{2,1},{3,0},{4,7},{5,6},{6,5},{7,4},{8,11},{9,10},{10,... | collective-permute-start | bytes 208904 | tf_op jit(solution)/shard_map/ppermute | solution.py:483
  58.0 1.3 %collective-permute-start.23 = (s16[272,128]{1,0:T(8,128)(2,1)S(1)}, s16[272,128]{1,0:T(8,128)(2,1)S(1)}, u32[]{:S(2)}, u32[]{:S(2)}) collective-permute-start(s16[272,128]{1,0:T(8,128)(2,1)S(1)} %solve_1.1.refs_0_), channel_id=1, source_target_pairs={{0,2},{1,3},{2,0},{3,1},{4,6},{5,7},{6,4},{7,5},{8,10},{9,11},{10,... | collective-permute-start | bytes 208904 | tf_op jit(solution)/shard_map/ppermute | solution.py:483
  61.2 1.3 %collective-permute-done.24.refs_1_ = s16[272,128]{1,0:T(8,128)(2,1)S(1)} collective-permute-done((s16[272,128]{1,0:T(8,128)(2,1)S(1)}, s16[272,128]{1,0:T(8,128)(2,1)S(1)}, u32[]{:S(2)}, u32[]{:S(2)}) %collective-permute-start.24) | collective-permute-done | bytes 69664 | tf_op jit(solution)/shard_map/ppermute | solution.py:483
  (42 shorter events, 15.2 us)
Async XLA Ops:
  0.9 8.2 %collective-permute-start.2 = (bf16[528,128]{1,0:T(8,128)(2,1)S(1)}, bf16[528,128]{1,0:T(8,128)(2,1)S(1)}, u32[]{:S(2)}, u32[]{:S(2)}) collective-permute-start(bf16[528,128]{1,0:T(8,128)(2,1)S(1)} %start.1.refs_0_), channel_id=1, source_target_pairs={{0,8},{4,12},{8,0},{12,4},{16,24},{20,28},{24,16},{28,20},{1,9},{5... | collective-permute-start | bytes 405512 | tf_op jit(solution)/shard_map/ppermute | solution.py:480
  3.9 7.9 %collective-permute-start.1 = (bf16[528,128]{1,0:T(8,128)(2,1)S(1)}, bf16[528,128]{1,0:T(8,128)(2,1)S(1)}, u32[]{:S(2)}, u32[]{:S(2)}) collective-permute-start(bf16[528,128]{1,0:T(8,128)(2,1)S(1)} %start.1.refs_0_), channel_id=1, source_target_pairs={{0,16},{4,20},{8,24},{12,28},{16,0},{20,4},{24,8},{28,12},{1,17},{... | collective-permute-start | bytes 405512 | tf_op jit(solution)/shard_map/ppermute | solution.py:480
  5.4 6.4 %collective-permute-start = (bf16[528,128]{1,0:T(8,128)(2,1)S(1)}, bf16[528,128]{1,0:T(8,128)(2,1)S(1)}, u32[]{:S(2)}, u32[]{:S(2)}) collective-permute-start(bf16[528,128]{1,0:T(8,128)(2,1)S(1)} %start.1.refs_0_), channel_id=1, source_target_pairs={{0,28},{4,24},{8,20},{12,16},{16,12},{20,8},{24,4},{28,0},{1,29},{... | collective-permute-start | bytes 405512 | tf_op jit(solution)/shard_map/ppermute | solution.py:480
  5.4 6.9 %collective-permute-start.4 = (bf16[528,128]{1,0:T(8,128)(2,1)S(1)}, bf16[528,128]{1,0:T(8,128)(2,1)S(1)}, u32[]{:S(2)}, u32[]{:S(2)}) collective-permute-start(bf16[528,128]{1,0:T(8,128)(2,1)S(1)} %start.1.refs_0_), channel_id=1, source_target_pairs={{0,4},{4,0},{8,12},{12,8},{16,20},{20,16},{24,28},{28,24},{1,5},{5... | collective-permute-start | bytes 405512 | tf_op jit(solution)/shard_map/ppermute | solution.py:480
  11.8 1.5 %collective-permute-start.6 = (bf16[528,128]{1,0:T(8,128)(2,1)S(1)}, bf16[528,128]{1,0:T(8,128)(2,1)S(1)}, u32[]{:S(2)}, u32[]{:S(2)}) collective-permute-start(bf16[528,128]{1,0:T(8,128)(2,1)S(1)} %collective-permute-done.1.refs_2_), channel_id=1, source_target_pairs={{0,4},{4,0},{8,12},{12,8},{16,20},{20,16},{24,28},{28,24},{1,5},{5... | collective-permute-start | bytes 405512 | tf_op jit(solution)/shard_map/ppermute | solution.py:480
  14.5 6.9 %collective-permute-start.7 = (s16[272,128]{1,0:T(8,128)(2,1)S(1)}, s16[272,128]{1,0:T(8,128)(2,1)S(1)}, u32[]{:S(2)}, u32[]{:S(2)}) collective-permute-start(s16[272,128]{1,0:T(8,128)(2,1)S(1)} %get-tuple-element.44), channel_id=1, source_target_pairs={{0,3},{1,2},{2,1},{3,0},{4,7},{5,6},{6,5},{7,4},{8,11},{9,10},{10,... | collective-permute-start | bytes 208904 | tf_op jit(solution)/shard_map/ppermute | solution.py:483
  18.2 5.3 %collective-permute-start.8 = (s16[272,128]{1,0:T(8,128)(2,1)S(1)}, s16[272,128]{1,0:T(8,128)(2,1)S(1)}, u32[]{:S(2)}, u32[]{:S(2)}) collective-permute-start(s16[272,128]{1,0:T(8,128)(2,1)S(1)} %get-tuple-element.45), channel_id=1, source_target_pairs={{0,1},{1,0},{2,3},{3,2},{4,5},{5,4},{6,7},{7,6},{8,9},{9,8},{10,11... | collective-permute-start | bytes 208904 | tf_op jit(solution)/shard_map/ppermute | solution.py:483
  18.2 6.0 %collective-permute-start.9 = (s16[272,128]{1,0:T(8,128)(2,1)S(1)}, s16[272,128]{1,0:T(8,128)(2,1)S(1)}, u32[]{:S(2)}, u32[]{:S(2)}) collective-permute-start(s16[272,128]{1,0:T(8,128)(2,1)S(1)} %get-tuple-element.46), channel_id=1, source_target_pairs={{0,2},{1,3},{2,0},{3,1},{4,6},{5,7},{6,4},{7,5},{8,10},{9,11},{10,... | collective-permute-start | bytes 208904 | tf_op jit(solution)/shard_map/ppermute | solution.py:483
  24.5 6.3 %collective-permute-start.12 = (s16[272,128]{1,0:T(8,128)(2,1)S(1)}, s16[272,128]{1,0:T(8,128)(2,1)S(1)}, u32[]{:S(2)}, u32[]{:S(2)}) collective-permute-start(s16[272,128]{1,0:T(8,128)(2,1)S(1)} %solve_0.1.refs_0_), channel_id=1, source_target_pairs={{0,3},{1,2},{2,1},{3,0},{4,7},{5,6},{6,5},{7,4},{8,11},{9,10},{10,... | collective-permute-start | bytes 208904 | tf_op jit(solution)/shard_map/ppermute | solution.py:483
  26.9 5.1 %collective-permute-start.11 = (s16[272,128]{1,0:T(8,128)(2,1)S(1)}, s16[272,128]{1,0:T(8,128)(2,1)S(1)}, u32[]{:S(2)}, u32[]{:S(2)}) collective-permute-start(s16[272,128]{1,0:T(8,128)(2,1)S(1)} %solve_0.1.refs_0_), channel_id=1, source_target_pairs={{0,1},{1,0},{2,3},{3,2},{4,5},{5,4},{6,7},{7,6},{8,9},{9,8},{10,11... | collective-permute-start | bytes 208904 | tf_op jit(solution)/shard_map/ppermute | solution.py:483
  27.3 5.5 %collective-permute-start.10 = (s16[272,128]{1,0:T(8,128)(2,1)S(1)}, s16[272,128]{1,0:T(8,128)(2,1)S(1)}, u32[]{:S(2)}, u32[]{:S(2)}) collective-permute-start(s16[272,128]{1,0:T(8,128)(2,1)S(1)} %solve_0.1.refs_0_), channel_id=1, source_target_pairs={{0,2},{1,3},{2,0},{3,1},{4,6},{5,7},{6,4},{7,5},{8,10},{9,11},{10,... | collective-permute-start | bytes 208904 | tf_op jit(solution)/shard_map/ppermute | solution.py:483
  32.9 5.3 %collective-permute-start.13 = (bf16[384,128]{1,0:T(8,128)(2,1)S(1)}, bf16[384,128]{1,0:T(8,128)(2,1)S(1)}, u32[]{:S(2)}, u32[]{:S(2)}) collective-permute-start(bf16[384,128]{1,0:T(8,128)(2,1)S(1)} %get-tuple-element.50), channel_id=1, source_target_pairs={{0,8},{4,12},{8,0},{12,4},{16,24},{20,28},{24,16},{28,20},{1,9},{5... | collective-permute-start | bytes 294920 | tf_op jit(solution)/shard_map/ppermute | solution.py:480
  33.9 5.2 %collective-permute-start.14 = (bf16[384,128]{1,0:T(8,128)(2,1)S(1)}, bf16[384,128]{1,0:T(8,128)(2,1)S(1)}, u32[]{:S(2)}, u32[]{:S(2)}) collective-permute-start(bf16[384,128]{1,0:T(8,128)(2,1)S(1)} %get-tuple-element.51), channel_id=1, source_target_pairs={{0,16},{4,20},{8,24},{12,28},{16,0},{20,4},{24,8},{28,12},{1,17},{... | collective-permute-start | bytes 294920 | tf_op jit(solution)/shard_map/ppermute | solution.py:480
  35.1 5.7 %collective-permute-start.15 = (bf16[384,128]{1,0:T(8,128)(2,1)S(1)}, bf16[384,128]{1,0:T(8,128)(2,1)S(1)}, u32[]{:S(2)}, u32[]{:S(2)}) collective-permute-start(bf16[384,128]{1,0:T(8,128)(2,1)S(1)} %get-tuple-element.52), channel_id=1, source_target_pairs={{0,24},{4,28},{8,16},{12,20},{16,8},{20,12},{24,0},{28,4},{1,25},{... | collective-permute-start | bytes 294920 | tf_op jit(solution)/shard_map/ppermute | solution.py:480
  36.5 5.0 %collective-permute-start.16 = (bf16[384,128]{1,0:T(8,128)(2,1)S(1)}, bf16[384,128]{1,0:T(8,128)(2,1)S(1)}, u32[]{:S(2)}, u32[]{:S(2)}) collective-permute-start(bf16[384,128]{1,0:T(8,128)(2,1)S(1)} %get-tuple-element.53), channel_id=1, source_target_pairs={{0,12},{4,8},{8,4},{12,0},{16,28},{20,24},{24,20},{28,16},{1,13},{... | collective-permute-start | bytes 294920 | tf_op jit(solution)/shard_map/ppermute | solution.py:480
  36.5 6.0 %collective-permute-start.17 = (bf16[384,128]{1,0:T(8,128)(2,1)S(1)}, bf16[384,128]{1,0:T(8,128)(2,1)S(1)}, u32[]{:S(2)}, u32[]{:S(2)}) collective-permute-start(bf16[384,128]{1,0:T(8,128)(2,1)S(1)} %get-tuple-element.54), channel_id=1, source_target_pairs={{0,20},{4,16},{8,28},{12,24},{16,4},{20,0},{24,12},{28,8},{1,21},{... | collective-permute-start | bytes 294920 | tf_op jit(solution)/shard_map/ppermute | solution.py:480
  38.3 6.4 %collective-permute-start.18 = (bf16[384,128]{1,0:T(8,128)(2,1)S(1)}, bf16[384,128]{1,0:T(8,128)(2,1)S(1)}, u32[]{:S(2)}, u32[]{:S(2)}) collective-permute-start(bf16[384,128]{1,0:T(8,128)(2,1)S(1)} %get-tuple-element.55), channel_id=1, source_target_pairs={{0,28},{4,24},{8,20},{12,16},{16,12},{20,8},{24,4},{28,0},{1,29},{... | collective-permute-start | bytes 294920 | tf_op jit(solution)/shard_map/ppermute | solution.py:480
  39.2 5.4 %collective-permute-start.19 = (bf16[384,128]{1,0:T(8,128)(2,1)S(1)}, bf16[384,128]{1,0:T(8,128)(2,1)S(1)}, u32[]{:S(2)}, u32[]{:S(2)}) collective-permute-start(bf16[384,128]{1,0:T(8,128)(2,1)S(1)} %get-tuple-element.56), channel_id=1, source_target_pairs={{0,4},{4,0},{8,12},{12,8},{16,20},{20,16},{24,28},{28,24},{1,5},{5... | collective-permute-start | bytes 294920 | tf_op jit(solution)/shard_map/ppermute | solution.py:480
  45.2 6.9 %collective-permute-start.20 = (s16[272,128]{1,0:T(8,128)(2,1)S(1)}, s16[272,128]{1,0:T(8,128)(2,1)S(1)}, u32[]{:S(2)}, u32[]{:S(2)}) collective-permute-start(s16[272,128]{1,0:T(8,128)(2,1)S(1)} %get-tuple-element.58), channel_id=1, source_target_pairs={{0,3},{1,2},{2,1},{3,0},{4,7},{5,6},{6,5},{7,4},{8,11},{9,10},{10,... | collective-permute-start | bytes 208904 | tf_op jit(solution)/shard_map/ppermute | solution.py:483
  48.5 5.4 %collective-permute-start.21 = (s16[272,128]{1,0:T(8,128)(2,1)S(1)}, s16[272,128]{1,0:T(8,128)(2,1)S(1)}, u32[]{:S(2)}, u32[]{:S(2)}) collective-permute-start(s16[272,128]{1,0:T(8,128)(2,1)S(1)} %get-tuple-element.59), channel_id=1, source_target_pairs={{0,1},{1,0},{2,3},{3,2},{4,5},{5,4},{6,7},{7,6},{8,9},{9,8},{10,11... | collective-permute-start | bytes 208904 | tf_op jit(solution)/shard_map/ppermute | solution.py:483
  48.5 6.0 %collective-permute-start.22 = (s16[272,128]{1,0:T(8,128)(2,1)S(1)}, s16[272,128]{1,0:T(8,128)(2,1)S(1)}, u32[]{:S(2)}, u32[]{:S(2)}) collective-permute-start(s16[272,128]{1,0:T(8,128)(2,1)S(1)} %get-tuple-element.60), channel_id=1, source_target_pairs={{0,2},{1,3},{2,0},{3,1},{4,6},{5,7},{6,4},{7,5},{8,10},{9,11},{10,... | collective-permute-start | bytes 208904 | tf_op jit(solution)/shard_map/ppermute | solution.py:483
  54.9 6.3 %collective-permute-start.25 = (s16[272,128]{1,0:T(8,128)(2,1)S(1)}, s16[272,128]{1,0:T(8,128)(2,1)S(1)}, u32[]{:S(2)}, u32[]{:S(2)}) collective-permute-start(s16[272,128]{1,0:T(8,128)(2,1)S(1)} %solve_1.1.refs_0_), channel_id=1, source_target_pairs={{0,3},{1,2},{2,1},{3,0},{4,7},{5,6},{6,5},{7,4},{8,11},{9,10},{10,... | collective-permute-start | bytes 208904 | tf_op jit(solution)/shard_map/ppermute | solution.py:483
  58.0 4.5 %collective-permute-start.24 = (s16[272,128]{1,0:T(8,128)(2,1)S(1)}, s16[272,128]{1,0:T(8,128)(2,1)S(1)}, u32[]{:S(2)}, u32[]{:S(2)}) collective-permute-start(s16[272,128]{1,0:T(8,128)(2,1)S(1)} %solve_1.1.refs_0_), channel_id=1, source_target_pairs={{0,1},{1,0},{2,3},{3,2},{4,5},{5,4},{6,7},{7,6},{8,9},{9,8},{10,11... | collective-permute-start | bytes 208904 | tf_op jit(solution)/shard_map/ppermute | solution.py:483
  58.0 5.3 %collective-permute-start.23 = (s16[272,128]{1,0:T(8,128)(2,1)S(1)}, s16[272,128]{1,0:T(8,128)(2,1)S(1)}, u32[]{:S(2)}, u32[]{:S(2)}) collective-permute-start(s16[272,128]{1,0:T(8,128)(2,1)S(1)} %solve_1.1.refs_0_), channel_id=1, source_target_pairs={{0,2},{1,3},{2,0},{3,1},{4,6},{5,7},{6,4},{7,5},{8,10},{9,11},{10,... | collective-permute-start | bytes 208904 | tf_op jit(solution)/shard_map/ppermute | solution.py:483
  (3 other events, 22.6 us)
